TPU v7x, 128 devices: a whole 4x4x4 slice. The times are simulated.
128 devices in a mesh: dp: 16 (over y, z), graph: 8 (over x, core).
Axes of the slice: x: 4, y: 4, z: 4, core: 2. Of those that a mesh axis runs over, the one named last changes fastest.
Arguments:
- nodes: bfloat16 [16, 512, 1024], P('dp', 'graph'), may hold values from -6 to 6
- node_grad: bfloat16 [16, 512, 1024], P('dp', 'graph'), may hold values from -6 to 6
- edges: bfloat16 [16, 8192, 512], P('dp', 'graph'), may hold values from -6 to 6
- source: int32 [16, 8192], P('dp', 'graph'), may hold values from 0 to 511
- target: int32 [16, 8192], P('dp', 'graph'), may hold values from 0 to 511
- trip_in: int32 [16, 16384], P('dp', 'graph'), may hold values from 0 to 8191
- trip_out: int32 [16, 16384], P('dp', 'graph'), may hold values from 0 to 1023
- basis: bfloat16 [16, 16384, 64], P('dp', 'graph'), may hold values from -6 to 6
- trip_count: int32 [16, 8], P('dp', 'graph'), may hold values from 1 to 2048, 9216 in all within a row
- w_ne: bfloat16 [2048, 512], replicated, may hold values from -0.125 to 0.125
- w_down: bfloat16 [512, 64], replicated, may hold values from -0.25 to 0.25
- w_up: bfloat16 [64, 512], replicated, may hold values from -0.75 to 0.75
- w_en: bfloat16 [512, 1024], replicated, may hold values from -0.25 to 0.25
Outputs:
- new_nodes: bfloat16 [16, 512, 1024], P('dp', 'graph')
- edge_grad: bfloat16 [16, 8192, 512], P('dp', 'graph')
- grad_ne: float32 [2048, 512], replicated
- grad_down: float32 [512, 64], replicated
- grad_up: float32 [64, 512], replicated
- grad_en: float32 [512, 1024], replicated
Inputs may be any that keep to these rules, and one draw needn't show every extreme that they name: `trip_count`: in each batch some device has exactly 2048 live triplet slots; live slots come first on a device.
All inputs are finite; a program needn't handle non-finite values.
Results may differ from a plain program's by a relative error of at most 0.019.
Values may be sent and summed in bfloat16 or wider, within the bound.
No kernel may reach another device: no remote copies, remote signals or barrier semaphores. Data moves between devices by JAX's collectives and lax.ppermute only.
A program may use at most 128 MiB of HBM per device.

v0:
```python
import jax
import jax.numpy as jnp
from jax import lax
from jax.experimental import pallas as pl
from jax.experimental.pallas import tpu as pltpu
from jax.sharding import PartitionSpec as P

BF = jnp.bfloat16
F32 = jnp.float32
NT = (((1,), (1,)), ((), ()))


def dot(a, b):
    return jnp.dot(a, b, preferred_element_type=F32)


def dot_nt(a, b):
    return lax.dot_general(a, b, NT, preferred_element_type=F32)


def call(body, outs, args, scalars=0, scratch=(), vmem=40, far_in=0, far_out=0):
    def places(count, first, last):
        return [
            pl.BlockSpec(
                memory_space=pltpu.SMEM
                if i < first
                else (pltpu.HBM if i >= count - last else pltpu.VMEM)
            )
            for i in range(count)
        ]

    return pl.pallas_call(
        body,
        out_shape=[
            pltpu.HBM(o.shape, o.dtype) if i >= len(outs) - far_out else o
            for i, o in enumerate(outs)
        ],
        in_specs=places(len(args), scalars, far_in),
        out_specs=places(len(outs), 0, far_out),
        scratch_shapes=list(scratch),
        compiler_params=pltpu.CompilerParams(vmem_limit_bytes=vmem << 20),
        cost_estimate=pl.CostEstimate(flops=1, bytes_accessed=1, transcendentals=0),
    )(
        *(
            pltpu.with_memory_space_constraint(a, pltpu.HBM) if i >= len(args) - far_in else a
            for i, a in enumerate(args)
        )
    )


def sds(shape, dtype=BF):
    return jax.ShapeDtypeStruct(shape, dtype)


def at(i, size):
    return pl.ds(pl.multiple_of(i * size, size), size)


def hot(mask):
    return jnp.where(mask, 1.0, 0.0).astype(BF)


def left(w):
    return jnp.concatenate([w, jnp.zeros_like(w)], axis=0)


def right(w):
    return jnp.concatenate([jnp.zeros_like(w), w], axis=0)


def column(row):
    return jnp.broadcast_to(row.astype(F32), (128, row.shape[1])).T.astype(jnp.int32)


def hot_rows(col, width):
    lane = lax.broadcasted_iota(jnp.int32, col.shape, 1)
    return jnp.concatenate([hot(col == lane + j) for j in range(0, width, 128)], axis=1)


def prep_body(
    cnt, src_r, tgt_r, in_r, out_r, basis_t, st, il, ilt, ol, olt, basis, in_hi, out_hi
):
    row = lax.broadcasted_iota(jnp.int32, (128, 1024), 0)
    for i in range(4):
        ch = slice(128 * i, 128 * i + 128)
        st[ch, :] = hot(src_r[...] == row + 128 * i)
        st[512 + 128 * i : 640 + 128 * i, :] = hot(tgt_r[...] == row + 128 * i)
    pos = lax.broadcasted_iota(jnp.int32, (1, 2048), 1)
    live = pos < cnt[0, 0]
    in_lo = jnp.where(live, in_r[...] & 511, -1)
    out_lo = out_r[...] & 511
    for i in range(8):
        ch = slice(256 * i, 256 * i + 256)
        il[ch, :] = hot_rows(column(in_lo[:, ch]), 512)
        ol[ch, :] = hot_rows(column(out_lo[:, ch]), 512)
        in_hi[ch, :] = column(in_r[:, ch] >> 9)
        out_hi[ch, :] = column(out_r[:, ch] >> 9)
    row = lax.broadcasted_iota(jnp.int32, (64, 2048), 0)
    for i in range(8):
        ch = slice(64 * i, 64 * i + 64)
        ilt[ch, :] = hot(in_lo == row + 64 * i)
        olt[ch, :] = hot(out_lo == row + 64 * i)
    basis[...] = jnp.concatenate([basis_t[...], basis_t[...]], axis=0).T


def fetch(far, near, sem):
    copy = pltpu.make_async_copy(far, near, sem)
    copy.start()
    return copy


def gathered(xc, refs, out, sems):
    x, c = xc[0], xc[1]
    copies = []
    for k in range(4):
        g = 2 * lax.rem(x + 4 - k, 4)
        copies.append(fetch(refs[k], out.at[at(g + c, 64), :], sems.at[2 * k]))
        copies.append(fetch(refs[4 + k], out.at[at(g + 1 - c, 64), :], sems.at[2 * k + 1]))
    return copies


def k1_body(xc, *refs):
    ends_far, edges_far, w_far = refs[0:2], refs[2], refs[3]
    down, inner_far, dsilu_far, nodes, ab, w_ne, edges, ends, wd_t, inner, dsilu, sems = refs[13:]
    loads = [fetch(ends_far[i], ends.at[i], sems.at[i]) for i in range(2)]
    loads.append(fetch(refs[4], wd_t, sems.at[2]))
    halves_of_w = [
        fetch(w_far.at[rows, :], w_ne.at[rows, :], sems.at[3 + h])
        for h, rows in enumerate((slice(0, 1024), slice(1024, 2048)))
    ]
    for copy in gathered(xc, refs[5:13], nodes, sems.at[pl.ds(8, 8)]):
        copy.wait()
    load_edges = fetch(edges_far, edges, sems.at[5])
    for h in range(2):
        halves_of_w[h].wait()
        for i in range(2):
            rows = slice(512 * h + 256 * i, 512 * h + 256 * i + 256)
            ab[rows, :] = dot(
                nodes[256 * i : 256 * i + 256, :], w_ne[1024 * h : 1024 * h + 1024, :]
            ).astype(BF)
    for copy in loads:
        copy.wait()
    wd = (left(wd_t[...]), right(wd_t[...]))
    load_edges.wait()
    copies = []
    for i in range(2):
        total = None
        for h in range(2):
            ch = slice(512 * h + 256 * i, 512 * h + 256 * i + 256)
            s = jnp.concatenate(
                [hot_rows(column(ends[j, :, ch]), 512) for j in range(2)], axis=1
            )
            pre = dot(s, ab[...])
            sig = jax.nn.sigmoid(pre)
            held = (edges[ch, :].astype(F32) + pre * sig).astype(BF)
            inner[ch, :] = held
            dsilu[ch, :] = (sig * (1.0 + pre * (1.0 - sig))).astype(BF)
            for near, far in ((inner, inner_far), (dsilu, dsilu_far)):
                copies.append(fetch(near.at[ch, :], far.at[ch, :], sems.at[16 + len(copies)]))
            part = dot_nt(held, wd[h])
            total = part if total is None else total + part
        down[256 * i : 256 * i + 256, :] = total.astype(BF)
    for copy in copies:
        copy.wait()


def kq_body(xc, tgt_r, *refs):
    w_far, d_outer, all_grad, w_en, q, sems = refs[8:]
    load = fetch(w_far, w_en, sems.at[8])
    for copy in gathered(xc, refs[:8], all_grad, sems):
        copy.wait()
    load.wait()
    for i in range(2):
        ch = slice(256 * i, 256 * i + 256)
        q[ch, :] = dot_nt(all_grad[ch, :], w_en[...]).astype(BF)
    for i in range(4):
        ch = slice(256 * i, 256 * i + 256)
        d_outer[ch, :] = dot(hot_rows(column(tgt_r[:, ch]), 512), q[...]).astype(BF)


def kw_body(xc, *refs):
    nodes_t, all_grad, nodes, sems = refs[16:]
    copies = gathered(xc, refs[:8], nodes, sems)
    late = gathered(xc, refs[8:16], all_grad, sems.at[pl.ds(8, 8)])
    for copy in copies:
        copy.wait()
    nodes_t[...] = nodes[...].T
    for copy in late:
        copy.wait()


def halves(value, odd, upper):
    kept = jnp.where(upper == odd, value, 0.0)
    return kept + pltpu.roll(kept, 64, 1)


def k2_body(
    xc, d0, d1, d2, d3, e0, e1, e2, e3, il, ilt, ol, olt, in_hi, out_hi, basis, inner, d_outer, w_up,
    keep, send, outer, summed, dzed, table, gath, spread,
):
    x, c = xc[0], xc[1]
    for k, (mine, other) in enumerate(((d0, e0), (d1, e1), (d2, e2), (d3, e3))):
        g = 2 * lax.rem(x + 4 - k, 4)
        table[:, at(g + c, 128)] = mine[...]
        table[:, at(g + 1 - c, 128)] = other[...]
    upper = lax.broadcasted_iota(jnp.int32, (256, 128), 1) >= 64
    for i in range(8):
        ch = slice(256 * i, 256 * i + 256)
        got = dot(il[ch, :], table[...])
        hi = in_hi[ch, :]
        acc = jnp.zeros((256, 128), F32)
        for g in range(8):
            acc = jnp.where((hi >> 1) == g, got[:, 128 * g : 128 * g + 128], acc)
        term = halves(acc, (hi & 1) == 1, upper) * basis[ch, :].astype(F32)
        gath[ch, :] = jnp.where(upper == (out_hi[ch, :] == 1), term, 0.0).astype(BF)
    held = dot(olt[...], gath[...]).astype(BF)
    summed[...] = held
    d_sum = jnp.zeros((512, 128), F32)
    for h, w in enumerate((left(w_up[...]), right(w_up[...]))):
        ch = slice(512 * h, 512 * h + 512)
        zed = dot(held, w)
        sig = jax.nn.sigmoid(zed)
        outer[ch, :] = (inner[ch, :].astype(F32) + zed * sig).astype(BF)
        dz = (d_outer[ch, :].astype(F32) * (sig * (1.0 + zed * (1.0 - sig)))).astype(BF)
        dzed[ch, :] = dz
        d_sum += dot_nt(dz, w)
    d_sum = d_sum.astype(BF)
    for i in range(8):
        ch = slice(256 * i, 256 * i + 256)
        got = dot(ol[ch, :], d_sum)
        term = halves(got, out_hi[ch, :] == 1, upper) * basis[ch, :].astype(F32)
        hi = in_hi[ch, :]
        term = jnp.where(upper == ((hi & 1) == 1), term, 0.0)
        for g in range(8):
            spread[ch, 128 * g : 128 * g + 128] = jnp.where((hi >> 1) == g, term, 0.0).astype(BF)
    for i in range(4):
        ch = slice(128 * i, 128 * i + 128)
        part = dot(ilt[...], spread[:, 256 * i : 256 * i + 256])
        low, high = part[:, 0:128], part[:, 128:256]
        keep[:, ch] = jnp.where(c == 0, low, high)
        send[:, ch] = jnp.where(c == 0, high, low).astype(BF)


def ko_body(xc, outer, st, summed, dzed, ot, gup, keep, send):
    c = xc[1]
    for i in range(2):
        ch = slice(256 * i, 256 * i + 256)
        part = dot(st[512 + 256 * i : 768 + 256 * i, :], outer[...])
        ot[:, ch] = part.T.astype(BF)
        for j in range(2):
            low, high = part[128 * j : 128 * j + 64, :], part[128 * j + 64 : 128 * j + 128, :]
            rows = slice(128 * i + 64 * j, 128 * i + 64 * j + 64)
            keep[rows, :] = jnp.where(c == 0, low, high)
            send[rows, :] = jnp.where(c == 0, high, low).astype(BF)
    summed_t = summed[...].T
    gup[...] = dot(summed_t[0:64, :], dzed[0:512, :]) + dot(summed_t[64:128, :], dzed[512:1024, :])


def kr_body(xc, keep, recv, own, s1, s2, s3):
    x = xc[0]
    for k, ref in enumerate((own, s1, s2, s3)):
        rows = at(lax.rem(x + k, 4), 64)
        ref[...] = (keep[rows, :] + recv[rows, :].astype(F32)).astype(BF)


def kn_body(own, r1, r2, r3, nodes, w_en, out):
    rows = total4(own[...], r1[...], r2[...], r3[...]).astype(BF)
    out[...] = (nodes[...].astype(F32) + dot(rows, w_en[...])).astype(BF)


def ka_body(xc, keep, recv, own, s1, s2, s3):
    x = xc[0]
    for k, ref in enumerate((own, s1, s2, s3)):
        ch = at(lax.rem(x + k, 4), 128)
        ref[...] = (keep[:, ch] + recv[:, ch].astype(F32)).astype(BF)


def total4(a, b, c, d):
    return (a.astype(F32) + c.astype(F32)) + (b.astype(F32) + d.astype(F32))


def k3_body(
    xc, own, r1, r2, r3, d_outer, dsilu, inner, st, w_down_t, ot, gup, edge_grad, keep, send, d_pre
):
    c = xc[1]
    dd = total4(own[...], r1[...], r2[...], r3[...]).astype(BF)
    for h, w in enumerate((left(w_down_t[...]), right(w_down_t[...]))):
        for i in range(2):
            rows = slice(256 * i, 256 * i + 256)
            ch = slice(512 * h + 256 * i, 512 * h + 256 * i + 256)
            d_inner = d_outer[ch, :].astype(F32) + dot(dd[rows, :], w)
            edge_grad[ch, :] = d_inner.astype(BF)
            d_pre[ch, :] = (d_inner * dsilu[ch, :].astype(F32)).astype(BF)
    for i in range(2):
        rows = slice(256 * i, 256 * i + 256)
        send[rows, :] = dot(st[at(2 * (1 - c) + i, 256), :], d_pre[...]).astype(BF)
        keep[rows, :] = dot(st[at(2 * c + i, 256), :], d_pre[...])
    ddt = dd.T
    gdown = dot(ddt[0:64, :], inner[0:512, :]) + dot(ddt[64:128, :], inner[512:1024, :])
    keep[512:576, :] = jnp.where(c == 0, gup[...], gdown)
    send[512:576, :] = jnp.where(c == 0, gdown, gup[...]).astype(BF)
    for i in range(4):
        rows = slice(576 + 64 * i, 640 + 64 * i)
        keep[rows, :] = ot[at(2 * i + c, 64), :].astype(F32)
        send[rows, :] = ot[at(2 * i + 1 - c, 64), :]


def kb_body(xc, keep, recv, own, s1, s2, s3):
    x = xc[0]
    for k, ref in enumerate((own, s1, s2, s3)):
        b = lax.rem(x + k, 4)
        ch = at(b, 128)
        ref[0:576, :] = (keep[0:576, ch] + recv[0:576, ch].astype(F32)).astype(BF)
        rows = pl.ds(pl.multiple_of(576 + 64 * b, 64), 64)
        part = (keep[rows, :] + recv[rows, :].astype(F32)).astype(BF)
        for j in range(4):
            ref[576 + 64 * j : 640 + 64 * j, :] = part[:, 128 * j : 128 * j + 128]


def k4_body(yz, own, r1, r2, r3, nodes_t, all_grad, g0, s1, s2, s3, whole):
    y = yz[0]
    sums = total4(own[...], r1[...], r2[...], r3[...])
    whole[0:1024, :] = dot(nodes_t[...], sums[0:512, :].astype(BF)).astype(BF)
    ot = sums[576:832, :].astype(BF)
    ot = jnp.concatenate([ot[64 * j : 64 * j + 64, :] for j in range(4)], axis=1)
    gen = dot(ot, all_grad[...]).astype(BF)
    for j in range(8):
        whole[1024 + 64 * j : 1088 + 64 * j, :] = gen[:, 128 * j : 128 * j + 128]
    whole[1536:1600, :] = sums[512:576, :].astype(BF)
    for k, ref in enumerate((g0, s1, s2, s3)):
        ref[...] = whole[at(lax.rem(y + k, 4), 400), :]


def sum_body(a, b, c, d, out):
    out[...] = total4(a[...], b[...], c[...], d[...]).astype(BF)


def place_body(i, own, r1, r2, r3, out):
    rows = own.shape[0]
    for k, ref in enumerate((own, r1, r2, r3)):
        out[at(lax.rem(i[0] + 4 - k, 4), rows), :] = ref[...]


def end_body(xc, *refs):
    gne_far, gdt_far, gup_far, gen_far, gne, gdt, gup, gen, sems = refs[8:]
    x, c = xc[0], xc[1]
    copies = []

    def send(near, far):
        copy = pltpu.make_async_copy(near, far, sems.at[len(copies)])
        copy.start()
        copies.append(copy)

    for k in range(4):
        b = lax.rem(x + 4 - k, 4)
        ch = at(b, 128)
        mine, other = refs[k], refs[4 + k]
        for i, (ref, core) in enumerate(((mine, c), (other, 1 - c))):
            slot = 2 * k + i
            gne[slot] = ref[0:1024, :].astype(F32)
            send(gne.at[slot], gne_far.at[at(core, 1024), ch])
            for j in range(8):
                gen[slot, :, 128 * j : 128 * j + 128] = ref[
                    1024 + 64 * j : 1088 + 64 * j, :
                ].astype(F32)
            send(gen.at[slot], gen_far.at[at(2 * b + core, 64), :])
        mine, other = mine[1536:1600, :].astype(F32), other[1536:1600, :].astype(F32)
        gup[:, ch] = jnp.where(c == 0, mine, other)
        gdt[:, ch] = jnp.where(c == 0, other, mine)
    send(gup, gup_far)
    send(gdt, gdt_far)
    for copy in copies:
        copy.wait()


def over_x(value, k):
    perm = [(2 * x + c, 2 * ((x + k) % 4) + c) for x in range(4) for c in range(2)]
    return lax.ppermute(value, "graph", perm)


def over_core(value):
    return lax.ppermute(value, "graph", [(i, i ^ 1) for i in range(8)])


def over_y(value, k):
    perm = [(4 * y + z, 4 * ((y + k) % 4) + z) for y in range(4) for z in range(4)]
    return lax.ppermute(value, "dp", perm)


def over_z(value, k):
    perm = [(4 * y + z, 4 * y + (z + k) % 4) for y in range(4) for z in range(4)]
    return lax.ppermute(value, "dp", perm)


def tie(*values):
    return lax.optimization_barrier(values)


def local(
    nodes, node_grad, edges, source, target, trip_in, trip_out, basis, trip_count,
    w_ne, w_down, w_up, w_en,
):
    g = lax.axis_index("graph")
    d = lax.axis_index("dp")
    xc = jnp.stack([g // 2, g % 2]).astype(jnp.int32)
    yz = jnp.stack([d // 4, d % 4]).astype(jnp.int32)
    near = (1, 2, 3)

    n = [nodes[0]] + [over_x(nodes[0], k) for k in near]
    m = [over_core(n[0])]
    p = [node_grad[0]] + [over_x(node_grad[0], k) for k in near]
    m += [over_core(v) for v in n[1:]]
    down, inner, dsilu = call(
        k1_body,
        [sds((512, 128)), sds((1024, 512)), sds((1024, 512))],
        [xc, source, target, edges[0], w_ne, w_down.T, *n, *m],
        scalars=1,
        scratch=[pltpu.VMEM((512, 1024), BF), pltpu.VMEM((1024, 512), BF),
                 pltpu.VMEM((2048, 512), BF), pltpu.VMEM((1024, 512), BF),
                 pltpu.VMEM((2, 1, 1024), jnp.int32), pltpu.VMEM((64, 512), BF),
                 pltpu.VMEM((1024, 512), BF), pltpu.VMEM((1024, 512), BF),
                 pltpu.SemaphoreType.DMA((24,))],
        vmem=24, far_in=13, far_out=2,
    )

    t = [down] + [over_x(down, k) for k in near]
    u = [over_core(down)]
    _, trip_in, p[1], p[2], p[3] = tie(down, trip_in, *p[1:])
    q = [over_core(v) for v in p]
    st, il, ilt, ol, olt, basis2, in_hi, out_hi = call(
        prep_body,
        [sds((1024, 1024)), sds((2048, 512)), sds((512, 2048)), sds((2048, 512)),
         sds((512, 2048)), sds((2048, 128)), sds((2048, 128), jnp.int32),
         sds((2048, 128), jnp.int32)],
        [trip_count, source, target, trip_in, trip_out, basis[0].T],
        scalars=1, vmem=24,
    )
    (d_outer,) = call(
        kq_body,
        [sds((1024, 512))],
        [xc, target, *p, *q, w_en],
        scalars=1,
        scratch=[pltpu.VMEM((512, 1024), BF), pltpu.VMEM((512, 1024), BF),
                 pltpu.VMEM((512, 512), BF), pltpu.SemaphoreType.DMA((9,))],
        vmem=24, far_in=9,
    )
    *t, il, d_outer = tie(*t, il, d_outer)
    u += [over_core(v) for v in t[1:]]
    keep, send, outer, summed, dzed = call(
        k2_body,
        [sds((512, 512), F32), sds((512, 512)), sds((1024, 512)), sds((512, 128)),
         sds((1024, 512))],
        [xc, *t, *u, il, ilt, ol, olt, in_hi, out_hi, basis2, inner, d_outer, w_up],
        scalars=1,
        scratch=[pltpu.VMEM((512, 1024), BF), pltpu.VMEM((2048, 128), BF),
                 pltpu.VMEM((2048, 1024), BF)], vmem=32,
    )

    recv = over_core(send)
    parts = call(ka_body, [sds((512, 128))] * 4, [xc, keep, recv], scalars=1, vmem=8)
    dd = [parts[0]] + [over_x(parts[k], k) for k in near]
    ot, gup, o_keep, o_send = call(
        ko_body,
        [sds((512, 512)), sds((64, 512), F32), sds((256, 512), F32), sds((256, 512))],
        [xc, outer, st, summed, dzed], scalars=1, vmem=16,
    )
    o_recv = over_core(o_send)
    edge_grad, keep, send = call(
        k3_body,
        [sds((1024, 512)), sds((832, 512), F32), sds((832, 512))],
        [xc, *dd, d_outer, dsilu, inner, st, w_down.T, ot, gup],
        scalars=1, scratch=[pltpu.VMEM((1024, 512), BF)], vmem=24,
    )

    recv = over_core(send)
    parts = call(kb_body, [sds((832, 128))] * 4, [xc, keep, recv], scalars=1, vmem=12)
    recv, o_recv, *held = tie(recv, o_recv, *n, *m, *p, *q)
    o_parts = call(kr_body, [sds((64, 512))] * 4, [xc, o_keep, o_recv], scalars=1, vmem=8)
    nodes_t, all_grad = call(
        kw_body,
        [sds((1024, 512)), sds((512, 1024))],
        [xc, *held],
        scalars=1, scratch=[pltpu.VMEM((512, 1024), BF), pltpu.SemaphoreType.DMA((16,))],
        vmem=16, far_in=16,
    )
    parts = [parts[0]] + [over_x(parts[k], k) for k in near]
    *parts, nodes_t, all_grad = tie(*parts, nodes_t, all_grad)
    parts = call(
        k4_body, [sds((400, 128))] * 4, [yz, *parts, nodes_t, all_grad],
        scalars=1, scratch=[pltpu.VMEM((1600, 128), BF)], vmem=16,
    )
    parts = [parts[0]] + [over_y(parts[k], k) for k in near]
    (part,) = call(sum_body, [sds((400, 128))], parts, vmem=8)
    parts = [part] + [over_z(part, k) for k in near]
    o_parts = [o_parts[0]] + [over_x(o_parts[k], k) for k in near]
    *o_parts, p0, p1, p2, p3 = tie(*o_parts, *parts)
    (part,) = call(sum_body, [sds((400, 128))], [p0, p1, p2, p3], vmem=8)
    (new_nodes,) = call(kn_body, [sds((64, 1024))], [*o_parts, nodes[0], w_en], vmem=16)
    parts = [part] + [over_y(part, k) for k in near]
    new_nodes, *parts = tie(new_nodes, *parts)
    (part,) = call(place_body, [sds((1600, 128))], [yz, *parts], scalars=1, vmem=8)
    parts = [part] + [over_x(part, k) for k in near]
    parts += [over_core(v) for v in parts]
    grad_ne, grad_down_t, grad_up, grad_en = call(
        end_body,
        [sds((2048, 512), F32), sds((64, 512), F32), sds((64, 512), F32), sds((512, 1024), F32)],
        [xc, *parts],
        scalars=1,
        scratch=[pltpu.VMEM((8, 1024, 128), F32), pltpu.VMEM((64, 512), F32),
                 pltpu.VMEM((64, 512), F32), pltpu.VMEM((8, 64, 1024), F32),
                 pltpu.SemaphoreType.DMA((18,))],
        vmem=24, far_out=4,
    )
    return (new_nodes[None], edge_grad[None], grad_ne, grad_down_t.T, grad_up, grad_en)


def solution(mesh):
    split3, split2 = P("dp", "graph", None), P("dp", "graph")
    in_specs = (split3,) * 3 + (split2,) * 4 + (split3, split2) + (P(),) * 4
    out_specs = (split3, split3, P(), P(), P(), P())
    return jax.shard_map(local, mesh=mesh, in_specs=in_specs, out_specs=out_specs, check_vma=False)
```

profile of v0, /device:TPU:1, one launch (start us, length us, event | category | flops | bytes accessed | tf_op | source)
XLA Modules:
  0.0 140.2 jit_solution(1755113755257414928)
XLA Ops:
  0.6 3.4 %collective-permute-start.2 = (bf16[64,1024]{1,0:T(8,128)(2,1)}, bf16[64,1024]{1,0:T(8,128)(2,1)S(1)}, u32[]{:S(2)}, u32[]{:S(2)}) collective-permute-start(bf16[64,1024]{1,0:T(8,128)(2,1)} %bitcast.14), channel_id=1, source_target_pairs={{0,6},{1,7},{2,0},{3,1},{4,2},{5,3},{6,4},{7,5},{8,14},{9,15},{10,... | collective-permute-start | bytes 393224 | tf_op jit(solution)/shard_map/ppermute | solution.py:378
  6.7 2.6 %collective-permute-done.2.refs_8_.refs_3_ = bf16[64,1024]{1,0:T(8,128)(2,1)S(1)} collective-permute-done((bf16[64,1024]{1,0:T(8,128)(2,1)}, bf16[64,1024]{1,0:T(8,128)(2,1)S(1)}, u32[]{:S(2)}, u32[]{:S(2)}) %collective-permute-start.2) | collective-permute-done | bytes 131104 | tf_op jit(solution)/shard_map/ppermute | solution.py:378
  10.9 2.2 %collective-permute-start.5 = (bf16[64,1024]{1,0:T(8,128)(2,1)S(1)}, bf16[64,1024]{1,0:T(8,128)(2,1)S(1)}, u32[]{:S(2)}, u32[]{:S(2)}) collective-permute-start(bf16[64,1024]{1,0:T(8,128)(2,1)S(1)} %collective-permute-done.1.refs_7_.refs_2_), channel_id=1, source_target_pairs={{0,1},{1,0},{2,3},{3,2},{4,5},{5,4},{6,7},{7,6},{8,9},{9,8},{10,11... | collective-permute-start | bytes 393224 | tf_op jit(solution)/shard_map/ppermute | solution.py:382
  17.5 6.9 %shard_map.172 = (bf16[512,128]{1,0:T(8,128)(2,1)S(1)}, bf16[1024,512]{1,0:T(8,128)(2,1)}, bf16[1024,512]{1,0:T(8,128)(2,1)}) custom-call(s32[2]{0:T(128)S(1)} %pad_add_fusion.xc, s32[1,1024]{1,0:T(1,128)} %src_r.1, s32[1,1024]{1,0:T(1,128)} %tgt_r.3, bf16[1024,512]{1,0:T(8,128)(2,1)} %bitcast.24, bf16[2048,512]{1,0:T(8,128)(2,1)} %refs_3_.1, ...), custom_call_target="tpu_custom_call" | custom-call | flops 1 | bytes 1 | tf_op jit(solution)/shard_map/pallas_call | solution.py:32
  30.4 2.8 %shard_map.173 = (bf16[1024,1024]{1,0:T(8,128)(2,1)S(1)}, bf16[2048,512]{1,0:T(8,128)(2,1)S(1)}, bf16[512,2048]{1,0:T(8,128)(2,1)S(1)}, bf16[2048,512]{1,0:T(8,1...) custom-call(s32[1,1]{1,0:T(1,128)S(6)} %copy.19.cnt, ...), custom_call_target="tpu_custom_call" | custom-call | flops 1 | bytes 1 | tf_op jit(solution)/shard_map/pallas_call | solution.py:32
  35.4 3.5 %shard_map.174.d_outer = bf16[1024,512]{1,0:T(8,128)(2,1)S(1)} custom-call(s32[2]{0:T(128)S(1)} %pad_add_fusion.xc, s32[1,1024]{1,0:T(1,128)S(1)} %copy-done.7, bf16[64,1024]{1,0:T(8,128)(2,1)} %bitcast.29, bf16[64,1024]{1,0:T(8,128)(2,1)} %copy-done.20, bf16[64,1024]{1,0:T(8,128)(2,1)} %copy-done.19, bf16[64,1024]{1,0:T(8,128)(2,1)} %copy-done.18, ...), custom_call_target="tpu_custom_call" | custom-call | flops 1 | bytes 1 | tf_op jit(solution)/shard_map/pallas_call | solution.py:32
  40.9 9.5 %shard_map.175 = (f32[512,512]{1,0:T(8,128)S(1)}, bf16[512,512]{1,0:T(8,128)(2,1)S(1)}, bf16[1024,512]{1,0:T(8,128)(2,1)S(1)}, bf16[512,128]{1,0:T(8,128)(2,1)S(1)}, bf16[1024,512]{1,0:T(8,128)(2,1)S(1)}) custom-call(s32[2]{0:T(128)S(1)} %pad_add_fusion.xc, bf16[512,128]{1,0:T(8,128)(2,1)S(1)} %get-tuple-element.103.d0, ...), custom_call_target="tpu_custom_call" | custom-call | flops 1 | bytes 1 | tf_op jit(solution)/shard_map/pallas_call | solution.py:32
  53.5 2.4 %collective-permute-start.23 = (bf16[512,128]{1,0:T(8,128)(2,1)S(1)}, bf16[512,128]{1,0:T(8,128)(2,1)S(1)}, u32[]{:S(2)}, u32[]{:S(2)}) collective-permute-start(bf16[512,128]{1,0:T(8,128)(2,1)S(1)} %get-tuple-element.125), channel_id=1, source_target_pairs={{0,4},{1,5},{2,6},{3,7},{4,0},{5,1},{6,2},{7,3},{8,12},{9,13},{10,... | collective-permute-start | bytes 393224 | tf_op jit(solution)/shard_map/ppermute | solution.py:378
  59.1 2.9 %collective-permute-done.23.r2 = bf16[512,128]{1,0:T(8,128)(2,1)S(1)} collective-permute-done((bf16[512,128]{1,0:T(8,128)(2,1)S(1)}, bf16[512,128]{1,0:T(8,128)(2,1)S(1)}, u32[]{:S(2)}, u32[]{:S(2)}) %collective-permute-start.23) | collective-permute-done | bytes 131104 | tf_op jit(solution)/shard_map/ppermute | solution.py:378
  62.3 2.5 %shard_map.178 = (bf16[1024,512]{1,0:T(8,128)(2,1)}, f32[832,512]{1,0:T(8,128)S(1)}, bf16[832,512]{1,0:T(8,128)(2,1)S(1)}) custom-call(s32[2]{0:T(128)S(1)} %pad_add_fusion.xc, bf16[512,128]{1,0:T(8,128)(2,1)S(1)} %get-tuple-element.123.own, bf16[512,128]{1,0:T(8,128)(2,1)S(1)} %collective-permute-done.22.r1, ...), custom_call_target="tpu_custom_call" | custom-call | flops 1 | bytes 1 | tf_op jit(solution)/shard_map/pallas_call | solution.py:32
  66.3 2.0 %collective-permute-done.25.recv = bf16[832,512]{1,0:T(8,128)(2,1)S(1)} collective-permute-done((bf16[832,512]{1,0:T(8,128)(2,1)S(1)}, bf16[832,512]{1,0:T(8,128)(2,1)S(1)}, u32[]{:S(2)}, u32[]{:S(2)}) %collective-permute-start.25) | collective-permute-done | bytes 852000 | tf_op jit(solution)/shard_map/ppermute | solution.py:382
  69.3 3.3 %collective-permute-start.31 = (bf16[832,128]{1,0:T(8,128)(2,1)S(1)}, bf16[832,128]{1,0:T(8,128)(2,1)S(1)}, u32[]{:S(2)}, u32[]{:S(2)}) collective-permute-start(bf16[832,128]{1,0:T(8,128)(2,1)S(1)} %get-tuple-element.140), channel_id=1, source_target_pairs={{0,4},{1,5},{2,6},{3,7},{4,0},{5,1},{6,2},{7,3},{8,12},{9,13},{10,... | collective-permute-start | bytes 638984 | tf_op jit(solution)/shard_map/ppermute | solution.py:378
  72.6 2.3 %shard_map.181 = (bf16[1024,512]{1,0:T(8,128)(2,1)S(1)}, bf16[512,1024]{1,0:T(8,128)(2,1)S(1)}) custom-call(s32[2]{0:T(128)S(1)} %pad_add_fusion.xc, bf16[64,1024]{1,0:T(8,128)(2,1)} %bitcast.19, bf16[64,1024]{1,0:T(8,128)(2,1)} %copy-done.13, bf16[64,1024]{1,0:T(8,128)(2,1)} %copy-done.12, bf16[64,1024]{1,0:T(8,128)(2,1)} %copy-done.11, ...), custom_call_target="tpu_custom_call" | custom-call | flops 1 | bytes 1 | tf_op jit(solution)/shard_map/pallas_call | solution.py:32
  75.0 1.9 %collective-permute-done.30.r1 = bf16[832,128]{1,0:T(8,128)(2,1)S(1)} collective-permute-done((bf16[832,128]{1,0:T(8,128)(2,1)S(1)}, bf16[832,128]{1,0:T(8,128)(2,1)S(1)}, u32[]{:S(2)}, u32[]{:S(2)}) %collective-permute-start.30) | collective-permute-done | bytes 213024 | tf_op jit(solution)/shard_map/ppermute | solution.py:378
  76.8 5.3 %collective-permute-done.31.r2 = bf16[832,128]{1,0:T(8,128)(2,1)S(1)} collective-permute-done((bf16[832,128]{1,0:T(8,128)(2,1)S(1)}, bf16[832,128]{1,0:T(8,128)(2,1)S(1)}, u32[]{:S(2)}, u32[]{:S(2)}) %collective-permute-start.31) | collective-permute-done | bytes 213024 | tf_op jit(solution)/shard_map/ppermute | solution.py:378
  84.7 2.6 %collective-permute-start.34 = (bf16[400,128]{1,0:T(8,128)(2,1)S(1)}, bf16[400,128]{1,0:T(8,128)(2,1)S(1)}, u32[]{:S(2)}, u32[]{:S(2)}) collective-permute-start(bf16[400,128]{1,0:T(8,128)(2,1)S(1)} %get-tuple-element.168), channel_id=1, source_target_pairs={{0,64},{8,72},{16,80},{24,88},{32,96},{40,104},{48,112},{56,120},{... | collective-permute-start | bytes 307208 | tf_op jit(solution)/shard_map/ppermute | solution.py:387
  92.1 3.8 %collective-permute-start.38 = (bf16[400,128]{1,0:T(8,128)(2,1)S(1)}, bf16[400,128]{1,0:T(8,128)(2,1)S(1)}, u32[]{:S(2)}, u32[]{:S(2)}) collective-permute-start(bf16[400,128]{1,0:T(8,128)(2,1)S(1)} %shard_map.183.a), channel_id=1, source_target_pairs={{0,24},{8,0},{16,8},{24,16},{32,56},{40,32},{48,40},{56,48},{64,88... | collective-permute-start | bytes 307208 | tf_op jit(solution)/shard_map/ppermute | solution.py:392
  97.8 1.9 %collective-permute-start.29 = (bf16[64,512]{1,0:T(8,128)(2,1)S(1)}, bf16[64,512]{1,0:T(8,128)(2,1)S(1)}, u32[]{:S(2)}, u32[]{:S(2)}) collective-permute-start(bf16[64,512]{1,0:T(8,128)(2,1)S(1)} %get-tuple-element.136), channel_id=1, source_target_pairs={{0,6},{1,7},{2,0},{3,1},{4,2},{5,3},{6,4},{7,5},{8,14},{9,15},{10,... | collective-permute-start | bytes 196616 | tf_op jit(solution)/shard_map/ppermute | solution.py:378
  106.8 2.3 %collective-permute-done.40.r2 = bf16[400,128]{1,0:T(8,128)(2,1)S(1)} collective-permute-done((bf16[400,128]{1,0:T(8,128)(2,1)S(1)}, bf16[400,128]{1,0:T(8,128)(2,1)S(1)}, u32[]{:S(2)}, u32[]{:S(2)}) %collective-permute-start.40) | collective-permute-done | bytes 102432 | tf_op jit(solution)/shard_map/ppermute | solution.py:387
  110.8 2.3 %collective-permute-start.44 = (bf16[1600,128]{1,0:T(8,128)(2,1)S(1)}, bf16[1600,128]{1,0:T(8,128)(2,1)S(1)}, u32[]{:S(2)}, u32[]{:S(2)}) collective-permute-start(bf16[1600,128]{1,0:T(8,128)(2,1)S(1)} %shard_map.186.refs_0_), channel_id=1, source_target_pairs={{0,6},{1,7},{2,0},{3,1},{4,2},{5,3},{6,4},{7,5},{8,14},{9,15},{10,... | collective-permute-start | bytes 1228808 | tf_op jit(solution)/shard_map/ppermute | solution.py:378
  113.7 6.0 %collective-permute-start.45 = (bf16[1600,128]{1,0:T(8,128)(2,1)S(1)}, bf16[1600,128]{1,0:T(8,128)(2,1)S(1)}, u32[]{:S(2)}, u32[]{:S(2)}) collective-permute-start(bf16[1600,128]{1,0:T(8,128)(2,1)S(1)} %shard_map.186.refs_0_), channel_id=1, source_target_pairs={{0,1},{1,0},{2,3},{3,2},{4,5},{5,4},{6,7},{7,6},{8,9},{9,8},{10,11... | collective-permute-start | bytes 1228808 | tf_op jit(solution)/shard_map/ppermute | solution.py:382
  120.4 11.1 %collective-permute-start.48 = (bf16[1600,128]{1,0:T(8,128)(2,1)S(1)}, bf16[1600,128]{1,0:T(8,128)(2,1)S(1)}, u32[]{:S(2)}, u32[]{:S(2)}) collective-permute-start(bf16[1600,128]{1,0:T(8,128)(2,1)S(1)} %collective-permute-done.44.refs_3_), channel_id=1, source_target_pairs={{0,1},{1,0},{2,3},{3,2},{4,5},{5,4},{6,7},{7,6},{8,9},{9,8},{10,11... | collective-permute-start | bytes 1228808 | tf_op jit(solution)/shard_map/ppermute | solution.py:382
  132.7 2.5 %collective-permute-start.46 = (bf16[1600,128]{1,0:T(8,128)(2,1)S(1)}, bf16[1600,128]{1,0:T(8,128)(2,1)S(1)}, u32[]{:S(2)}, u32[]{:S(2)}) collective-permute-start(bf16[1600,128]{1,0:T(8,128)(2,1)S(1)} %collective-permute-done.42.refs_1_), channel_id=1, source_target_pairs={{0,1},{1,0},{2,3},{3,2},{4,5},{5,4},{6,7},{7,6},{8,9},{9,8},{10,11... | collective-permute-start | bytes 1228808 | tf_op jit(solution)/shard_map/ppermute | solution.py:382
  136.6 3.4 %shard_map.187 = (f32[2048,512]{1,0:T(8,128)}, f32[64,512]{1,0:T(8,128)}, f32[64,512]{1,0:T(8,128)}, f32[512,1024]{1,0:T(8,128)}) custom-call(s32[2]{0:T(128)S(1)} %pad_add_fusion.xc, bf16[1600,128]{1,0:T(8,128)(2,1)S(1)} %shard_map.186.refs_0_, bf16[1600,128]{1,0:T(8,128)(2,1)S(1)} %collective-permute-done.42.refs_1_, ...), custom_call_target="tpu_custom_call" | custom-call | flops 1 | bytes 1 | tf_op jit(solution)/shard_map/pallas_call | solution.py:32
  (142 shorter events, 48.9 us)
Async XLA Ops:
  0.6 8.7 %collective-permute-start.2 = (bf16[64,1024]{1,0:T(8,128)(2,1)}, bf16[64,1024]{1,0:T(8,128)(2,1)S(1)}, u32[]{:S(2)}, u32[]{:S(2)}) collective-permute-start(bf16[64,1024]{1,0:T(8,128)(2,1)} %bitcast.14), channel_id=1, source_target_pairs={{0,6},{1,7},{2,0},{3,1},{4,2},{5,3},{6,4},{7,5},{8,14},{9,15},{10,... | collective-permute-start | bytes 393224 | tf_op jit(solution)/shard_map/ppermute | solution.py:378
  4.5 9.2 %collective-permute-start = (bf16[64,1024]{1,0:T(8,128)(2,1)}, bf16[64,1024]{1,0:T(8,128)(2,1)S(1)}, u32[]{:S(2)}, u32[]{:S(2)}) collective-permute-start(bf16[64,1024]{1,0:T(8,128)(2,1)} %bitcast.16), channel_id=1, source_target_pairs={{0,2},{1,3},{2,4},{3,5},{4,6},{5,7},{6,0},{7,1},{8,10},{9,11},{10,... | collective-permute-start | bytes 393224 | tf_op jit(solution)/shard_map/ppermute | solution.py:378
  5.1 9.6 %collective-permute-start.3 = (bf16[64,1024]{1,0:T(8,128)(2,1)}, bf16[64,1024]{1,0:T(8,128)(2,1)S(1)}, u32[]{:S(2)}, u32[]{:S(2)}) collective-permute-start(bf16[64,1024]{1,0:T(8,128)(2,1)} %bitcast.17), channel_id=1, source_target_pairs={{0,1},{1,0},{2,3},{3,2},{4,5},{5,4},{6,7},{7,6},{8,9},{9,8},{10,11... | collective-permute-start | bytes 393224 | tf_op jit(solution)/shard_map/ppermute | solution.py:382
  14.4 9.9 %collective-permute-start.12 = (bf16[64,1024]{1,0:T(8,128)(2,1)}, bf16[64,1024]{1,0:T(8,128)(2,1)S(1)}, u32[]{:S(2)}, u32[]{:S(2)}) collective-permute-start(bf16[64,1024]{1,0:T(8,128)(2,1)} %bitcast.25), channel_id=1, source_target_pairs={{0,6},{1,7},{2,0},{3,1},{4,2},{5,3},{6,4},{7,5},{8,14},{9,15},{10,... | collective-permute-start | bytes 393224 | tf_op jit(solution)/shard_map/ppermute | solution.py:378
  14.7 9.7 %collective-permute-start.11 = (bf16[64,1024]{1,0:T(8,128)(2,1)}, bf16[64,1024]{1,0:T(8,128)(2,1)S(1)}, u32[]{:S(2)}, u32[]{:S(2)}) collective-permute-start(bf16[64,1024]{1,0:T(8,128)(2,1)} %bitcast.26), channel_id=1, source_target_pairs={{0,4},{1,5},{2,6},{3,7},{4,0},{5,1},{6,2},{7,3},{8,12},{9,13},{10,... | collective-permute-start | bytes 393224 | tf_op jit(solution)/shard_map/ppermute | solution.py:378
  15.3 9.4 %collective-permute-start.10 = (bf16[64,1024]{1,0:T(8,128)(2,1)}, bf16[64,1024]{1,0:T(8,128)(2,1)S(1)}, u32[]{:S(2)}, u32[]{:S(2)}) collective-permute-start(bf16[64,1024]{1,0:T(8,128)(2,1)} %bitcast.27), channel_id=1, source_target_pairs={{0,2},{1,3},{2,4},{3,5},{4,6},{5,7},{6,0},{7,1},{8,10},{9,11},{10,... | collective-permute-start | bytes 393224 | tf_op jit(solution)/shard_map/ppermute | solution.py:378
  16.1 11.3 %collective-permute-start.13 = (bf16[64,1024]{1,0:T(8,128)(2,1)}, bf16[64,1024]{1,0:T(8,128)(2,1)S(1)}, u32[]{:S(2)}, u32[]{:S(2)}) collective-permute-start(bf16[64,1024]{1,0:T(8,128)(2,1)} %bitcast.28), channel_id=1, source_target_pairs={{0,1},{1,0},{2,3},{3,2},{4,5},{5,4},{6,7},{7,6},{8,9},{9,8},{10,11... | collective-permute-start | bytes 393224 | tf_op jit(solution)/shard_map/ppermute | solution.py:382
  25.2 8.0 %collective-permute-start.15 = (bf16[64,1024]{1,0:T(8,128)(2,1)S(1)}, bf16[64,1024]{1,0:T(8,128)(2,1)S(1)}, u32[]{:S(2)}, u32[]{:S(2)}) collective-permute-start(bf16[64,1024]{1,0:T(8,128)(2,1)S(1)} %collective-permute-done.11.refs_2_.refs_10_), channel_id=1, source_target_pairs={{0,1},{1,0},{2,3},{3,2},{4,5},{5,4},{6,7},{7,6},{8,9},{9,8},{10,11... | collective-permute-start | bytes 393224 | tf_op jit(solution)/shard_map/ppermute | solution.py:382
  25.2 9.5 %collective-permute-start.16 = (bf16[64,1024]{1,0:T(8,128)(2,1)S(1)}, bf16[64,1024]{1,0:T(8,128)(2,1)S(1)}, u32[]{:S(2)}, u32[]{:S(2)}) collective-permute-start(bf16[64,1024]{1,0:T(8,128)(2,1)S(1)} %collective-permute-done.12.refs_3_.refs_11_), channel_id=1, source_target_pairs={{0,1},{1,0},{2,3},{3,2},{4,5},{5,4},{6,7},{7,6},{8,9},{9,8},{10,11... | collective-permute-start | bytes 393224 | tf_op jit(solution)/shard_map/ppermute | solution.py:382
  25.7 13.2 %collective-permute-start.9 = (bf16[512,128]{1,0:T(8,128)(2,1)S(1)}, bf16[512,128]{1,0:T(8,128)(2,1)S(1)}, u32[]{:S(2)}, u32[]{:S(2)}) collective-permute-start(bf16[512,128]{1,0:T(8,128)(2,1)S(1)} %get-tuple-element.103.d0), channel_id=1, source_target_pairs={{0,6},{1,7},{2,0},{3,1},{4,2},{5,3},{6,4},{7,5},{8,14},{9,15},{10,... | collective-permute-start | bytes 393224 | tf_op jit(solution)/shard_map/ppermute | solution.py:378
  27.4 11.5 %collective-permute-start.8 = (bf16[512,128]{1,0:T(8,128)(2,1)S(1)}, bf16[512,128]{1,0:T(8,128)(2,1)S(1)}, u32[]{:S(2)}, u32[]{:S(2)}) collective-permute-start(bf16[512,128]{1,0:T(8,128)(2,1)S(1)} %get-tuple-element.103.d0), channel_id=1, source_target_pairs={{0,4},{1,5},{2,6},{3,7},{4,0},{5,1},{6,2},{7,3},{8,12},{9,13},{10,... | collective-permute-start | bytes 393224 | tf_op jit(solution)/shard_map/ppermute | solution.py:378
  28.9 10.0 %collective-permute-start.7 = (bf16[512,128]{1,0:T(8,128)(2,1)S(1)}, bf16[512,128]{1,0:T(8,128)(2,1)S(1)}, u32[]{:S(2)}, u32[]{:S(2)}) collective-permute-start(bf16[512,128]{1,0:T(8,128)(2,1)S(1)} %get-tuple-element.103.d0), channel_id=1, source_target_pairs={{0,2},{1,3},{2,4},{3,5},{4,6},{5,7},{6,0},{7,1},{8,10},{9,11},{10,... | collective-permute-start | bytes 393224 | tf_op jit(solution)/shard_map/ppermute | solution.py:378
  53.5 8.5 %collective-permute-start.23 = (bf16[512,128]{1,0:T(8,128)(2,1)S(1)}, bf16[512,128]{1,0:T(8,128)(2,1)S(1)}, u32[]{:S(2)}, u32[]{:S(2)}) collective-permute-start(bf16[512,128]{1,0:T(8,128)(2,1)S(1)} %get-tuple-element.125), channel_id=1, source_target_pairs={{0,4},{1,5},{2,6},{3,7},{4,0},{5,1},{6,2},{7,3},{8,12},{9,13},{10,... | collective-permute-start | bytes 393224 | tf_op jit(solution)/shard_map/ppermute | solution.py:378
  69.1 7.7 %collective-permute-start.30 = (bf16[832,128]{1,0:T(8,128)(2,1)S(1)}, bf16[832,128]{1,0:T(8,128)(2,1)S(1)}, u32[]{:S(2)}, u32[]{:S(2)}) collective-permute-start(bf16[832,128]{1,0:T(8,128)(2,1)S(1)} %get-tuple-element.139), channel_id=1, source_target_pairs={{0,2},{1,3},{2,4},{3,5},{4,6},{5,7},{6,0},{7,1},{8,10},{9,11},{10,... | collective-permute-start | bytes 638984 | tf_op jit(solution)/shard_map/ppermute | solution.py:378
  69.3 12.8 %collective-permute-start.31 = (bf16[832,128]{1,0:T(8,128)(2,1)S(1)}, bf16[832,128]{1,0:T(8,128)(2,1)S(1)}, u32[]{:S(2)}, u32[]{:S(2)}) collective-permute-start(bf16[832,128]{1,0:T(8,128)(2,1)S(1)} %get-tuple-element.140), channel_id=1, source_target_pairs={{0,4},{1,5},{2,6},{3,7},{4,0},{5,1},{6,2},{7,3},{8,12},{9,13},{10,... | collective-permute-start | bytes 638984 | tf_op jit(solution)/shard_map/ppermute | solution.py:378
  72.6 9.6 %collective-permute-start.32 = (bf16[832,128]{1,0:T(8,128)(2,1)S(1)}, bf16[832,128]{1,0:T(8,128)(2,1)S(1)}, u32[]{:S(2)}, u32[]{:S(2)}) collective-permute-start(bf16[832,128]{1,0:T(8,128)(2,1)S(1)} %get-tuple-element.141), channel_id=1, source_target_pairs={{0,6},{1,7},{2,0},{3,1},{4,2},{5,3},{6,4},{7,5},{8,14},{9,15},{10,... | collective-permute-start | bytes 638984 | tf_op jit(solution)/shard_map/ppermute | solution.py:378
  89.0 8.8 %collective-permute-start.27 = (bf16[64,512]{1,0:T(8,128)(2,1)S(1)}, bf16[64,512]{1,0:T(8,128)(2,1)S(1)}, u32[]{:S(2)}, u32[]{:S(2)}) collective-permute-start(bf16[64,512]{1,0:T(8,128)(2,1)S(1)} %get-tuple-element.134), channel_id=1, source_target_pairs={{0,2},{1,3},{2,4},{3,5},{4,6},{5,7},{6,0},{7,1},{8,10},{9,11},{10,... | collective-permute-start | bytes 196616 | tf_op jit(solution)/shard_map/ppermute | solution.py:378
  92.1 10.7 %collective-permute-start.38 = (bf16[400,128]{1,0:T(8,128)(2,1)S(1)}, bf16[400,128]{1,0:T(8,128)(2,1)S(1)}, u32[]{:S(2)}, u32[]{:S(2)}) collective-permute-start(bf16[400,128]{1,0:T(8,128)(2,1)S(1)} %shard_map.183.a), channel_id=1, source_target_pairs={{0,24},{8,0},{16,8},{24,16},{32,56},{40,32},{48,40},{56,48},{64,88... | collective-permute-start | bytes 307208 | tf_op jit(solution)/shard_map/ppermute | solution.py:392
  95.9 6.8 %collective-permute-start.37 = (bf16[400,128]{1,0:T(8,128)(2,1)S(1)}, bf16[400,128]{1,0:T(8,128)(2,1)S(1)}, u32[]{:S(2)}, u32[]{:S(2)}) collective-permute-start(bf16[400,128]{1,0:T(8,128)(2,1)S(1)} %shard_map.183.a), channel_id=1, source_target_pairs={{0,16},{8,24},{16,0},{24,8},{32,48},{40,56},{48,32},{56,40},{64,80... | collective-permute-start | bytes 307208 | tf_op jit(solution)/shard_map/ppermute | solution.py:392
  110.8 9.6 %collective-permute-start.44 = (bf16[1600,128]{1,0:T(8,128)(2,1)S(1)}, bf16[1600,128]{1,0:T(8,128)(2,1)S(1)}, u32[]{:S(2)}, u32[]{:S(2)}) collective-permute-start(bf16[1600,128]{1,0:T(8,128)(2,1)S(1)} %shard_map.186.refs_0_), channel_id=1, source_target_pairs={{0,6},{1,7},{2,0},{3,1},{4,2},{5,3},{6,4},{7,5},{8,14},{9,15},{10,... | collective-permute-start | bytes 1228808 | tf_op jit(solution)/shard_map/ppermute | solution.py:378
  113.1 18.5 %collective-permute-start.43 = (bf16[1600,128]{1,0:T(8,128)(2,1)S(1)}, bf16[1600,128]{1,0:T(8,128)(2,1)S(1)}, u32[]{:S(2)}, u32[]{:S(2)}) collective-permute-start(bf16[1600,128]{1,0:T(8,128)(2,1)S(1)} %shard_map.186.refs_0_), channel_id=1, source_target_pairs={{0,4},{1,5},{2,6},{3,7},{4,0},{5,1},{6,2},{7,3},{8,12},{9,13},{10,... | collective-permute-start | bytes 1228808 | tf_op jit(solution)/shard_map/ppermute | solution.py:378
  113.7 19.0 %collective-permute-start.42 = (bf16[1600,128]{1,0:T(8,128)(2,1)S(1)}, bf16[1600,128]{1,0:T(8,128)(2,1)S(1)}, u32[]{:S(2)}, u32[]{:S(2)}) collective-permute-start(bf16[1600,128]{1,0:T(8,128)(2,1)S(1)} %shard_map.186.refs_0_), channel_id=1, source_target_pairs={{0,2},{1,3},{2,4},{3,5},{4,6},{5,7},{6,0},{7,1},{8,10},{9,11},{10,... | collective-permute-start | bytes 1228808 | tf_op jit(solution)/shard_map/ppermute | solution.py:378
  113.7 21.5 %collective-permute-start.45 = (bf16[1600,128]{1,0:T(8,128)(2,1)S(1)}, bf16[1600,128]{1,0:T(8,128)(2,1)S(1)}, u32[]{:S(2)}, u32[]{:S(2)}) collective-permute-start(bf16[1600,128]{1,0:T(8,128)(2,1)S(1)} %shard_map.186.refs_0_), channel_id=1, source_target_pairs={{0,1},{1,0},{2,3},{3,2},{4,5},{5,4},{6,7},{7,6},{8,9},{9,8},{10,11... | collective-permute-start | bytes 1228808 | tf_op jit(solution)/shard_map/ppermute | solution.py:382
  120.4 14.8 %collective-permute-start.48 = (bf16[1600,128]{1,0:T(8,128)(2,1)S(1)}, bf16[1600,128]{1,0:T(8,128)(2,1)S(1)}, u32[]{:S(2)}, u32[]{:S(2)}) collective-permute-start(bf16[1600,128]{1,0:T(8,128)(2,1)S(1)} %collective-permute-done.44.refs_3_), channel_id=1, source_target_pairs={{0,1},{1,0},{2,3},{3,2},{4,5},{5,4},{6,7},{7,6},{8,9},{9,8},{10,11... | collective-permute-start | bytes 1228808 | tf_op jit(solution)/shard_map/ppermute | solution.py:382
  (50 other events, 340.7 us)
where the time goes:
time: 140 us
  starting transfers between devices  67.3 us (48%)
  Pallas kernels  37.3 us (27%)
  waiting for transfers between devices  32.3 us (23%)
  between operations  1.83 us (1%)
    pallas_call x16, Pallas kernels, call(): pl.pallas_call(body, out_shape=[pltpu.HBM(o.shape, o.dtype) if i >= len(o...  37.3 us
    ppermute x19, starting transfers between devices, over_core(): return lax.ppermute(value, 'graph', [(i, i ^ 1) for i in range(8)])  31.6 us
    ppermute x21, starting transfers between devices, over_x(): return lax.ppermute(value, 'graph', perm)  23.1 us
    ppermute x21, waiting for transfers between devices, over_x(): return lax.ppermute(value, 'graph', perm)  20.6 us
    ppermute x6, starting transfers between devices, over_y(): return lax.ppermute(value, 'dp', perm)  8.04 us
    ppermute x19, waiting for transfers between devices, over_core(): return lax.ppermute(value, 'graph', [(i, i ^ 1) for i in range(8)])  5.97 us
    ppermute x6, waiting for transfers between devices, over_y(): return lax.ppermute(value, 'dp', perm)  5.69 us
    ppermute x3, starting transfers between devices, over_z(): return lax.ppermute(value, 'dp', perm)  4.53 us
  transfers between devices with their start and end apart: 49, of which 22 were waited for; matrix products, arithmetic and copies ran while one was open for 0% of the time, Pallas kernels for 14%

commit v1 on v0

--- a/solution.py
+++ b/solution.py
@@ -18,34 +18,28 @@
     return lax.dot_general(a, b, NT, preferred_element_type=F32)
 
 
-def call(body, outs, args, scalars=0, scratch=(), vmem=40, far_in=0, far_out=0):
-    def places(count, first, last):
-        return [
-            pl.BlockSpec(
-                memory_space=pltpu.SMEM
-                if i < first
-                else (pltpu.HBM if i >= count - last else pltpu.VMEM)
-            )
-            for i in range(count)
-        ]
-
+def call(
+    body, outs, args, scalars=0, scratch=(), vmem=40, any_in=0, far_in=0, far_out=0
+):
+    n_in, n_out = len(args), len(outs)
+    in_specs = [pl.BlockSpec(memory_space=pltpu.SMEM)] * scalars
+    in_specs += [pl.BlockSpec(memory_space=pltpu.VMEM)] * (n_in - scalars - any_in - far_in)
+    in_specs += [pl.BlockSpec(memory_space=pl.ANY)] * any_in
+    in_specs += [pl.BlockSpec(memory_space=pltpu.HBM)] * far_in
+    out_specs = [pl.BlockSpec(memory_space=pltpu.VMEM)] * (n_out - far_out)
+    out_specs += [pl.BlockSpec(memory_space=pltpu.HBM)] * far_out
+    near, far = args[: n_in - far_in], args[n_in - far_in :]
     return pl.pallas_call(
         body,
         out_shape=[
-            pltpu.HBM(o.shape, o.dtype) if i >= len(outs) - far_out else o
-            for i, o in enumerate(outs)
+            pltpu.HBM(o.shape, o.dtype) if i >= n_out - far_out else o for i, o in enumerate(outs)
         ],
-        in_specs=places(len(args), scalars, far_in),
-        out_specs=places(len(outs), 0, far_out),
+        in_specs=in_specs,
+        out_specs=out_specs,
         scratch_shapes=list(scratch),
         compiler_params=pltpu.CompilerParams(vmem_limit_bytes=vmem << 20),
         cost_estimate=pl.CostEstimate(flops=1, bytes_accessed=1, transcendentals=0),
-    )(
-        *(
-            pltpu.with_memory_space_constraint(a, pltpu.HBM) if i >= len(args) - far_in else a
-            for i, a in enumerate(args)
-        )
-    )
+    )(*near, *(pltpu.with_memory_space_constraint(a, pltpu.HBM) for a in far))
 
 
 def sds(shape, dtype=BF):
@@ -121,16 +115,24 @@
 
 def k1_body(xc, *refs):
     ends_far, edges_far, w_far = refs[0:2], refs[2], refs[3]
-    down, inner_far, dsilu_far, nodes, ab, w_ne, edges, ends, wd_t, inner, dsilu, sems = refs[13:]
+    down, inner_far, dsilu_far, nodes, ab, w_ne, edges, ends, wd_t, inner, dsilu, s, sems = refs[13:]
     loads = [fetch(ends_far[i], ends.at[i], sems.at[i]) for i in range(2)]
     loads.append(fetch(refs[4], wd_t, sems.at[2]))
+    blocks = gathered(xc, refs[5:13], nodes, sems.at[pl.ds(8, 8)])
     halves_of_w = [
         fetch(w_far.at[rows, :], w_ne.at[rows, :], sems.at[3 + h])
         for h, rows in enumerate((slice(0, 1024), slice(1024, 2048)))
     ]
-    for copy in gathered(xc, refs[5:13], nodes, sems.at[pl.ds(8, 8)]):
+    load_edges = fetch(edges_far, edges, sems.at[5])
+    for copy in loads:
         copy.wait()
-    load_edges = fetch(edges_far, edges, sems.at[5])
+    wd = (left(wd_t[...]), right(wd_t[...]))
+    for i in range(4):
+        ch = slice(256 * i, 256 * i + 256)
+        for j in range(2):
+            s[ch, 512 * j : 512 * j + 512] = hot_rows(column(ends[j, :, ch]), 512)
+    for copy in blocks:
+        copy.wait()
     for h in range(2):
         halves_of_w[h].wait()
         for i in range(2):
@@ -138,19 +140,13 @@
             ab[rows, :] = dot(
                 nodes[256 * i : 256 * i + 256, :], w_ne[1024 * h : 1024 * h + 1024, :]
             ).astype(BF)
-    for copy in loads:
-        copy.wait()
-    wd = (left(wd_t[...]), right(wd_t[...]))
     load_edges.wait()
     copies = []
     for i in range(2):
         total = None
         for h in range(2):
             ch = slice(512 * h + 256 * i, 512 * h + 256 * i + 256)
-            s = jnp.concatenate(
-                [hot_rows(column(ends[j, :, ch]), 512) for j in range(2)], axis=1
-            )
-            pre = dot(s, ab[...])
+            pre = dot(s[ch, :], ab[...])
             sig = jax.nn.sigmoid(pre)
             held = (edges[ch, :].astype(F32) + pre * sig).astype(BF)
             inner[ch, :] = held
@@ -165,9 +161,13 @@
 
 
 def kq_body(xc, tgt_r, *refs):
-    w_far, d_outer, all_grad, w_en, q, sems = refs[8:]
+    w_far, d_outer, all_grad, w_en, q, s, sems = refs[8:]
     load = fetch(w_far, w_en, sems.at[8])
-    for copy in gathered(xc, refs[:8], all_grad, sems):
+    blocks = gathered(xc, refs[:8], all_grad, sems)
+    for i in range(4):
+        ch = slice(256 * i, 256 * i + 256)
+        s[ch, :] = hot_rows(column(tgt_r[:, ch]), 512)
+    for copy in blocks:
         copy.wait()
     load.wait()
     for i in range(2):
@@ -175,7 +175,7 @@
         q[ch, :] = dot_nt(all_grad[ch, :], w_en[...]).astype(BF)
     for i in range(4):
         ch = slice(256 * i, 256 * i + 256)
-        d_outer[ch, :] = dot(hot_rows(column(tgt_r[:, ch]), 512), q[...]).astype(BF)
+        d_outer[ch, :] = dot(s[ch, :], q[...]).astype(BF)
 
 
 def kw_body(xc, *refs):
@@ -230,12 +230,14 @@
         got = dot(ol[ch, :], d_sum)
         term = halves(got, out_hi[ch, :] == 1, upper) * basis[ch, :].astype(F32)
         hi = in_hi[ch, :]
-        term = jnp.where(upper == ((hi & 1) == 1), term, 0.0)
+        term = jnp.where(upper == ((hi & 1) == 1), term, 0.0).astype(BF)
+        owner = (hi >> 1).astype(F32).astype(BF)
         for g in range(8):
-            spread[ch, 128 * g : 128 * g + 128] = jnp.where((hi >> 1) == g, term, 0.0).astype(BF)
+            spread[ch, 128 * g : 128 * g + 128] = jnp.where(owner == g, term, jnp.zeros_like(term))
+    whole = [dot(ilt[...], spread[:, 512 * i : 512 * i + 512]) for i in range(2)]
     for i in range(4):
         ch = slice(128 * i, 128 * i + 128)
-        part = dot(ilt[...], spread[:, 256 * i : 256 * i + 256])
+        part = whole[i // 2][:, 256 * (i % 2) : 256 * (i % 2) + 256]
         low, high = part[:, 0:128], part[:, 128:256]
         keep[:, ch] = jnp.where(c == 0, low, high)
         send[:, ch] = jnp.where(c == 0, high, low).astype(BF)
@@ -317,18 +319,21 @@
             ref[576 + 64 * j : 640 + 64 * j, :] = part[:, 128 * j : 128 * j + 128]
 
 
-def k4_body(yz, own, r1, r2, r3, nodes_t, all_grad, g0, s1, s2, s3, whole):
-    y = yz[0]
+def k4_body(i, own, r1, r2, r3, nodes_t, all_grad, g0, s1, s2, s3, whole):
     sums = total4(own[...], r1[...], r2[...], r3[...])
-    whole[0:1024, :] = dot(nodes_t[...], sums[0:512, :].astype(BF)).astype(BF)
+    gne = dot(nodes_t[...], sums[0:512, :].astype(BF)).astype(BF)
     ot = sums[576:832, :].astype(BF)
     ot = jnp.concatenate([ot[64 * j : 64 * j + 64, :] for j in range(4)], axis=1)
     gen = dot(ot, all_grad[...]).astype(BF)
-    for j in range(8):
-        whole[1024 + 64 * j : 1088 + 64 * j, :] = gen[:, 128 * j : 128 * j + 128]
-    whole[1536:1600, :] = sums[512:576, :].astype(BF)
+    for q in range(4):
+        at_q = 400 * q
+        whole[at_q : at_q + 256, :] = gne[256 * q : 256 * q + 256, :]
+        for j in range(2):
+            rows = slice(at_q + 256 + 64 * j, at_q + 320 + 64 * j)
+            whole[rows, :] = gen[:, 256 * q + 128 * j : 256 * q + 128 * j + 128]
+        whole[at_q + 384 : at_q + 400, :] = sums[512 + 16 * q : 528 + 16 * q, :].astype(BF)
     for k, ref in enumerate((g0, s1, s2, s3)):
-        ref[...] = whole[at(lax.rem(y + k, 4), 400), :]
+        ref[...] = whole[at(lax.rem(i[0] + k, 4), 400), :]
 
 
 def sum_body(a, b, c, d, out):
@@ -341,36 +346,56 @@
         out[at(lax.rem(i[0] + 4 - k, 4), rows), :] = ref[...]
 
 
-def end_body(xc, *refs):
-    gne_far, gdt_far, gup_far, gen_far, gne, gdt, gup, gen, sems = refs[8:]
-    x, c = xc[0], xc[1]
-    copies = []
-
-    def send(near, far):
-        copy = pltpu.make_async_copy(near, far, sems.at[len(copies)])
-        copy.start()
-        copies.append(copy)
-
-    for k in range(4):
-        b = lax.rem(x + 4 - k, 4)
-        ch = at(b, 128)
-        mine, other = refs[k], refs[4 + k]
-        for i, (ref, core) in enumerate(((mine, c), (other, 1 - c))):
-            slot = 2 * k + i
-            gne[slot] = ref[0:1024, :].astype(F32)
-            send(gne.at[slot], gne_far.at[at(core, 1024), ch])
-            for j in range(8):
-                gen[slot, :, 128 * j : 128 * j + 128] = ref[
-                    1024 + 64 * j : 1088 + 64 * j, :
-                ].astype(F32)
-            send(gen.at[slot], gen_far.at[at(2 * b + core, 64), :])
-        mine, other = mine[1536:1600, :].astype(F32), other[1536:1600, :].astype(F32)
-        gup[:, ch] = jnp.where(c == 0, mine, other)
-        gdt[:, ch] = jnp.where(c == 0, other, mine)
-    send(gup, gup_far)
-    send(gdt, gdt_far)
-    for copy in copies:
-        copy.wait()
+def spread_out(taken, xc, yz, mine, other, gne_far, gen_far, small, rows, cols, gen, sems):
+    x, c, z = xc[0], xc[1], yz[1]
+
+    def run(zeros, ones):
+        copies = []
+
+        def send(near, far):
+            copies.append(fetch(near, far, sems.at[len(copies)]))
+
+        for i, k in enumerate(taken):
+            b, q = lax.rem(x + 4 - k, 4), lax.rem(z + 4 - k, 4)
+            for j in range(4):
+                value = zeros[i][400 * j : 400 * j + 400, :].astype(F32)
+                cols[i, 256 * j : 256 * j + 256, :] = value[0:256]
+                for h in range(2):
+                    gen[0, i, :, 256 * j + 128 * h : 256 * j + 128 * h + 128] = value[
+                        256 + 64 * h : 320 + 64 * h
+                    ]
+                small[0, 16 * j : 16 * j + 16, at(b, 128)] = value[384:400]
+            send(cols.at[i], gne_far.at[0:1024, at(b, 128)])
+            send(gen.at[0, i], gen_far.at[b, 0])
+            for j in range(4):
+                value = ones[i][400 * j : 400 * j + 400, :].astype(F32)
+                rows[i, :, 128 * j : 128 * j + 128] = value[0:256]
+                for h in range(2):
+                    gen[1, i, :, 256 * j + 128 * h : 256 * j + 128 * h + 128] = value[
+                        256 + 64 * h : 320 + 64 * h
+                    ]
+                small[1, at(q, 16), 128 * j : 128 * j + 128] = value[384:400]
+            send(rows.at[i], gne_far.at[at(4 + q, 256), :])
+            for j in range(4):
+                send(gen.at[1, i, :, 256 * j : 256 * j + 256], gen_far.at[j, 1, :, at(q, 256)])
+        for copy in copies:
+            copy.wait()
+
+    @pl.when(c == 0)
+    def _():
+        run(mine, other)
+
+    @pl.when(c == 1)
+    def _():
+        run(other, mine)
+
+
+def end_body(xc, yz, *refs):
+    gup, gdt, gne_far, gen_far, small, rows, cols, gen, sems = refs[8:]
+    mine, other = refs[0:4], refs[4:8]
+    spread_out(range(4), xc, yz, mine, other, gne_far, gen_far, small, rows, cols, gen, sems)
+    gup[...] = small[0]
+    gdt[...] = small[1]
 
 
 def over_x(value, k):
@@ -382,14 +407,17 @@
     return lax.ppermute(value, "graph", [(i, i ^ 1) for i in range(8)])
 
 
-def over_y(value, k):
-    perm = [(4 * y + z, 4 * ((y + k) % 4) + z) for y in range(4) for z in range(4)]
-    return lax.ppermute(value, "dp", perm)
-
-
-def over_z(value, k):
-    perm = [(4 * y + z, 4 * y + (z + k) % 4) for y in range(4) for z in range(4)]
-    return lax.ppermute(value, "dp", perm)
+def over_dp(value, k, axes):
+    perm = []
+    for y in range(4):
+        for z in range(4):
+            for x in range(4):
+                for c in range(2):
+                    at = {"x": x, "y": y, "z": z}
+                    at[axes[c]] = (at[axes[c]] + k) % 4
+                    to = 8 * (4 * at["y"] + at["z"]) + 2 * at["x"] + c
+                    perm.append((8 * (4 * y + z) + 2 * x + c, to))
+    return lax.ppermute(value, ("dp", "graph"), perm)
 
 
 def tie(*values):
@@ -404,6 +432,8 @@
     d = lax.axis_index("dp")
     xc = jnp.stack([g // 2, g % 2]).astype(jnp.int32)
     yz = jnp.stack([d // 4, d % 4]).astype(jnp.int32)
+    of_part = jnp.where(xc[1] == 0, yz[0], yz[1])[None]
+    of_place = jnp.where(xc[1] == 0, yz[0], xc[0])[None]
     near = (1, 2, 3)
 
     n = [nodes[0]] + [over_x(nodes[0], k) for k in near]
@@ -419,7 +449,7 @@
                  pltpu.VMEM((2048, 512), BF), pltpu.VMEM((1024, 512), BF),
                  pltpu.VMEM((2, 1, 1024), jnp.int32), pltpu.VMEM((64, 512), BF),
                  pltpu.VMEM((1024, 512), BF), pltpu.VMEM((1024, 512), BF),
-                 pltpu.SemaphoreType.DMA((24,))],
+                 pltpu.VMEM((1024, 1024), BF), pltpu.SemaphoreType.DMA((24,))],
         vmem=24, far_in=13, far_out=2,
     )
 
@@ -441,7 +471,8 @@
         [xc, target, *p, *q, w_en],
         scalars=1,
         scratch=[pltpu.VMEM((512, 1024), BF), pltpu.VMEM((512, 1024), BF),
-                 pltpu.VMEM((512, 512), BF), pltpu.SemaphoreType.DMA((9,))],
+                 pltpu.VMEM((512, 512), BF), pltpu.VMEM((1024, 512), BF),
+                 pltpu.SemaphoreType.DMA((9,))],
         vmem=24, far_in=9,
     )
     *t, il, d_outer = tie(*t, il, d_outer)
@@ -486,31 +517,32 @@
     parts = [parts[0]] + [over_x(parts[k], k) for k in near]
     *parts, nodes_t, all_grad = tie(*parts, nodes_t, all_grad)
     parts = call(
-        k4_body, [sds((400, 128))] * 4, [yz, *parts, nodes_t, all_grad],
+        k4_body, [sds((400, 128))] * 4, [of_part, *parts, nodes_t, all_grad],
         scalars=1, scratch=[pltpu.VMEM((1600, 128), BF)], vmem=16,
     )
-    parts = [parts[0]] + [over_y(parts[k], k) for k in near]
+    parts = [parts[0]] + [over_dp(parts[k], k, "yz") for k in near]
     (part,) = call(sum_body, [sds((400, 128))], parts, vmem=8)
-    parts = [part] + [over_z(part, k) for k in near]
+    parts = [part] + [over_dp(part, k, "zy") for k in near]
     o_parts = [o_parts[0]] + [over_x(o_parts[k], k) for k in near]
     *o_parts, p0, p1, p2, p3 = tie(*o_parts, *parts)
     (part,) = call(sum_body, [sds((400, 128))], [p0, p1, p2, p3], vmem=8)
     (new_nodes,) = call(kn_body, [sds((64, 1024))], [*o_parts, nodes[0], w_en], vmem=16)
-    parts = [part] + [over_y(part, k) for k in near]
+    parts = [part] + [over_dp(part, k, "yx") for k in near]
     new_nodes, *parts = tie(new_nodes, *parts)
-    (part,) = call(place_body, [sds((1600, 128))], [yz, *parts], scalars=1, vmem=8)
-    parts = [part] + [over_x(part, k) for k in near]
-    parts += [over_core(v) for v in parts]
-    grad_ne, grad_down_t, grad_up, grad_en = call(
+    (part,) = call(place_body, [sds((1600, 128))], [of_place, *parts], scalars=1, vmem=8)
+    parts = [part] + [over_dp(part, k, "xz") for k in near]
+    grad_up, grad_down_t, grad_ne, grad_en = call(
         end_body,
-        [sds((2048, 512), F32), sds((64, 512), F32), sds((64, 512), F32), sds((512, 1024), F32)],
-        [xc, *parts],
-        scalars=1,
-        scratch=[pltpu.VMEM((8, 1024, 128), F32), pltpu.VMEM((64, 512), F32),
-                 pltpu.VMEM((64, 512), F32), pltpu.VMEM((8, 64, 1024), F32),
-                 pltpu.SemaphoreType.DMA((18,))],
-        vmem=24, far_out=4,
-    )
+        [sds((64, 512), F32), sds((64, 512), F32), sds((2048, 512), F32),
+         sds((4, 2, 64, 1024), F32)],
+        [xc, yz, *parts, *[over_core(v) for v in parts]],
+        scalars=2,
+        scratch=[pltpu.VMEM((2, 64, 512), F32), pltpu.VMEM((4, 256, 512), F32),
+                 pltpu.VMEM((4, 1024, 128), F32), pltpu.VMEM((2, 4, 64, 1024), F32),
+                 pltpu.SemaphoreType.DMA((28,))],
+        vmem=24, far_out=2,
+    )
+    grad_en = grad_en.reshape(512, 1024)
     return (new_nodes[None], edge_grad[None], grad_ne, grad_down_t.T, grad_up, grad_en)
 
 

time: 140 us -> 137 us (0.979)
  starting transfers between devices: 67.3 us -> 64 us
    ppermute x19, starting transfers between devices: 31.6 us -> 28 us  [over_core(): return lax.ppermute(value, 'graph', [(i, i ^ 1) for i in range(8)])]
    ppermute x9 -> x12, starting transfers between devices: 12.6 us -> 15.6 us  [over_dp(): return lax.ppermute(value, ('dp', 'graph'), perm)]
    ppermute x9 -> x12, waiting for transfers between devices: 5.7 us -> 8.7 us  [over_dp(): return lax.ppermute(value, ('dp', 'graph'), perm)]
    ppermute x21 -> x18, starting transfers between devices: 23.1 us -> 20.4 us  [over_x(): return lax.ppermute(value, 'graph', perm)]
    ppermute x21 -> x18, waiting for transfers between devices: 20.6 us -> 18.2 us  [over_x(): return lax.ppermute(value, 'graph', perm)]
where the time goes in v1:
time: 137 us; the launch traced here: 136 us
  starting transfers between devices  64 us (47%)
  Pallas kernels  36.3 us (26%)
  waiting for transfers between devices  32.8 us (24%)
  between operations  1.83 us (1%)
    pallas_call x16, Pallas kernels, call(): pl.pallas_call(body, out_shape=[pltpu.HBM(o.shape, o.dtype) if i >= n_out...  36.3 us
    ppermute x19, starting transfers between devices, over_core(): return lax.ppermute(value, 'graph', [(i, i ^ 1) for i in range(8)])  28 us
    ppermute x18, starting transfers between devices, over_x(): return lax.ppermute(value, 'graph', perm)  20.4 us
    ppermute x18, waiting for transfers between devices, over_x(): return lax.ppermute(value, 'graph', perm)  18.2 us
    ppermute x12, starting transfers between devices, over_dp(): return lax.ppermute(value, ('dp', 'graph'), perm)  15.6 us
    ppermute x12, waiting for transfers between devices, over_dp(): return lax.ppermute(value, ('dp', 'graph'), perm)  8.7 us
    ppermute x19, waiting for transfers between devices, over_core(): return lax.ppermute(value, 'graph', [(i, i ^ 1) for i in range(8)])  5.89 us
  transfers between devices with their start and end apart: 49, of which 22 were waited for; matrix products, arithmetic and copies ran while one was open for 0% of the time, Pallas kernels for 14%

profile of v1, /device:TPU:1, one launch (start us, length us, event | category | flops | bytes accessed | tf_op | source)
XLA Modules:
  0.0 136.5 jit_solution(16074898107918779938)
XLA Ops:
  0.6 3.4 %collective-permute-start.2 = (bf16[64,1024]{1,0:T(8,128)(2,1)}, bf16[64,1024]{1,0:T(8,128)(2,1)S(1)}, u32[]{:S(2)}, u32[]{:S(2)}) collective-permute-start(bf16[64,1024]{1,0:T(8,128)(2,1)} %bitcast.17), channel_id=1, source_target_pairs={{0,6},{1,7},{2,0},{3,1},{4,2},{5,3},{6,4},{7,5},{8,14},{9,15},{10,... | collective-permute-start | bytes 393224 | tf_op jit(solution)/shard_map/ppermute | solution.py:403
  6.7 2.6 %collective-permute-done.2.refs_8_.refs_3_ = bf16[64,1024]{1,0:T(8,128)(2,1)S(1)} collective-permute-done((bf16[64,1024]{1,0:T(8,128)(2,1)}, bf16[64,1024]{1,0:T(8,128)(2,1)S(1)}, u32[]{:S(2)}, u32[]{:S(2)}) %collective-permute-start.2) | collective-permute-done | bytes 131104 | tf_op jit(solution)/shard_map/ppermute | solution.py:403
  10.9 2.2 %collective-permute-start.5 = (bf16[64,1024]{1,0:T(8,128)(2,1)S(1)}, bf16[64,1024]{1,0:T(8,128)(2,1)S(1)}, u32[]{:S(2)}, u32[]{:S(2)}) collective-permute-start(bf16[64,1024]{1,0:T(8,128)(2,1)S(1)} %collective-permute-done.1.refs_7_.refs_2_), channel_id=1, source_target_pairs={{0,1},{1,0},{2,3},{3,2},{4,5},{5,4},{6,7},{7,6},{8,9},{9,8},{10,11... | collective-permute-start | bytes 393224 | tf_op jit(solution)/shard_map/ppermute | solution.py:407
  17.5 6.5 %shard_map.172 = (bf16[512,128]{1,0:T(8,128)(2,1)S(1)}, bf16[1024,512]{1,0:T(8,128)(2,1)}, bf16[1024,512]{1,0:T(8,128)(2,1)}) custom-call(s32[2]{0:T(128)S(1)} %pad_add_fusion.xc, s32[1,1024]{1,0:T(1,128)} %src_r.1, s32[1,1024]{1,0:T(1,128)} %tgt_r.3, bf16[1024,512]{1,0:T(8,128)(2,1)} %bitcast.27, bf16[2048,512]{1,0:T(8,128)(2,1)} %refs_3_.1, ...), custom_call_target="tpu_custom_call" | custom-call | flops 1 | bytes 1 | tf_op jit(solution)/shard_map/pallas_call | solution.py:32
  30.0 2.8 %shard_map.173 = (bf16[1024,1024]{1,0:T(8,128)(2,1)S(1)}, bf16[2048,512]{1,0:T(8,128)(2,1)S(1)}, bf16[512,2048]{1,0:T(8,128)(2,1)S(1)}, bf16[2048,512]{1,0:T(8,1...) custom-call(s32[1,1]{1,0:T(1,128)S(6)} %copy.19.cnt, ...), custom_call_target="tpu_custom_call" | custom-call | flops 1 | bytes 1 | tf_op jit(solution)/shard_map/pallas_call | solution.py:32
  35.1 3.5 %shard_map.174.d_outer = bf16[1024,512]{1,0:T(8,128)(2,1)S(1)} custom-call(s32[2]{0:T(128)S(1)} %pad_add_fusion.xc, s32[1,1024]{1,0:T(1,128)S(1)} %copy-done.7, bf16[64,1024]{1,0:T(8,128)(2,1)} %bitcast.32, bf16[64,1024]{1,0:T(8,128)(2,1)} %copy-done.20, bf16[64,1024]{1,0:T(8,128)(2,1)} %copy-done.19, bf16[64,1024]{1,0:T(8,128)(2,1)} %copy-done.18, ...), custom_call_target="tpu_custom_call" | custom-call | flops 1 | bytes 1 | tf_op jit(solution)/shard_map/pallas_call | solution.py:32
  40.5 9.1 %shard_map.175 = (f32[512,512]{1,0:T(8,128)S(1)}, bf16[512,512]{1,0:T(8,128)(2,1)S(1)}, bf16[1024,512]{1,0:T(8,128)(2,1)S(1)}, bf16[512,128]{1,0:T(8,128)(2,1)S(1)}, bf16[1024,512]{1,0:T(8,128)(2,1)S(1)}) custom-call(s32[2]{0:T(128)S(1)} %pad_add_fusion.xc, bf16[512,128]{1,0:T(8,128)(2,1)S(1)} %get-tuple-element.103.d0, ...), custom_call_target="tpu_custom_call" | custom-call | flops 1 | bytes 1 | tf_op jit(solution)/shard_map/pallas_call | solution.py:32
  52.9 2.4 %collective-permute-start.23 = (bf16[512,128]{1,0:T(8,128)(2,1)S(1)}, bf16[512,128]{1,0:T(8,128)(2,1)S(1)}, u32[]{:S(2)}, u32[]{:S(2)}) collective-permute-start(bf16[512,128]{1,0:T(8,128)(2,1)S(1)} %get-tuple-element.125), channel_id=1, source_target_pairs={{0,4},{1,5},{2,6},{3,7},{4,0},{5,1},{6,2},{7,3},{8,12},{9,13},{10,... | collective-permute-start | bytes 393224 | tf_op jit(solution)/shard_map/ppermute | solution.py:403
  58.5 2.9 %collective-permute-done.23.r2 = bf16[512,128]{1,0:T(8,128)(2,1)S(1)} collective-permute-done((bf16[512,128]{1,0:T(8,128)(2,1)S(1)}, bf16[512,128]{1,0:T(8,128)(2,1)S(1)}, u32[]{:S(2)}, u32[]{:S(2)}) %collective-permute-start.23) | collective-permute-done | bytes 131104 | tf_op jit(solution)/shard_map/ppermute | solution.py:403
  61.6 2.5 %shard_map.178 = (bf16[1024,512]{1,0:T(8,128)(2,1)}, f32[832,512]{1,0:T(8,128)S(1)}, bf16[832,512]{1,0:T(8,128)(2,1)S(1)}) custom-call(s32[2]{0:T(128)S(1)} %pad_add_fusion.xc, bf16[512,128]{1,0:T(8,128)(2,1)S(1)} %get-tuple-element.123.own, bf16[512,128]{1,0:T(8,128)(2,1)S(1)} %collective-permute-done.22.r1, ...), custom_call_target="tpu_custom_call" | custom-call | flops 1 | bytes 1 | tf_op jit(solution)/shard_map/pallas_call | solution.py:32
  65.6 2.0 %collective-permute-done.25.recv = bf16[832,512]{1,0:T(8,128)(2,1)S(1)} collective-permute-done((bf16[832,512]{1,0:T(8,128)(2,1)S(1)}, bf16[832,512]{1,0:T(8,128)(2,1)S(1)}, u32[]{:S(2)}, u32[]{:S(2)}) %collective-permute-start.25) | collective-permute-done | bytes 852000 | tf_op jit(solution)/shard_map/ppermute | solution.py:407
  68.9 3.1 %collective-permute-start.31 = (bf16[832,128]{1,0:T(8,128)(2,1)S(1)}, bf16[832,128]{1,0:T(8,128)(2,1)S(1)}, u32[]{:S(2)}, u32[]{:S(2)}) collective-permute-start(bf16[832,128]{1,0:T(8,128)(2,1)S(1)} %get-tuple-element.140), channel_id=1, source_target_pairs={{0,4},{1,5},{2,6},{3,7},{4,0},{5,1},{6,2},{7,3},{8,12},{9,13},{10,... | collective-permute-start | bytes 638984 | tf_op jit(solution)/shard_map/ppermute | solution.py:403
  72.0 2.3 %shard_map.181 = (bf16[1024,512]{1,0:T(8,128)(2,1)S(1)}, bf16[512,1024]{1,0:T(8,128)(2,1)S(1)}) custom-call(s32[2]{0:T(128)S(1)} %pad_add_fusion.xc, bf16[64,1024]{1,0:T(8,128)(2,1)} %bitcast.22, bf16[64,1024]{1,0:T(8,128)(2,1)} %copy-done.13, bf16[64,1024]{1,0:T(8,128)(2,1)} %copy-done.12, bf16[64,1024]{1,0:T(8,128)(2,1)} %copy-done.11, ...), custom_call_target="tpu_custom_call" | custom-call | flops 1 | bytes 1 | tf_op jit(solution)/shard_map/pallas_call | solution.py:32
  76.1 5.5 %collective-permute-done.31.r2 = bf16[832,128]{1,0:T(8,128)(2,1)S(1)} collective-permute-done((bf16[832,128]{1,0:T(8,128)(2,1)S(1)}, bf16[832,128]{1,0:T(8,128)(2,1)S(1)}, u32[]{:S(2)}, u32[]{:S(2)}) %collective-permute-start.31) | collective-permute-done | bytes 213024 | tf_op jit(solution)/shard_map/ppermute | solution.py:403
  84.0 3.3 %collective-permute-start.34 = (bf16[400,128]{1,0:T(8,128)(2,1)S(1)}, bf16[400,128]{1,0:T(8,128)(2,1)S(1)}, u32[]{:S(2)}, u32[]{:S(2)}) collective-permute-start(bf16[400,128]{1,0:T(8,128)(2,1)S(1)} %get-tuple-element.168), channel_id=1, source_target_pairs={{0,64},{1,17},{2,66},{3,19},{4,68},{5,21},{6,70},{7,23},{8,72},{9,... | collective-permute-start | bytes 307208 | tf_op jit(solution)/shard_map/ppermute | solution.py:420
  91.2 2.8 %collective-permute-start.38 = (bf16[400,128]{1,0:T(8,128)(2,1)S(1)}, bf16[400,128]{1,0:T(8,128)(2,1)S(1)}, u32[]{:S(2)}, u32[]{:S(2)}) collective-permute-start(bf16[400,128]{1,0:T(8,128)(2,1)S(1)} %shard_map.183.a), channel_id=1, source_target_pairs={{0,24},{1,97},{2,26},{3,99},{4,28},{5,101},{6,30},{7,103},{8,0},{9... | collective-permute-start | bytes 307208 | tf_op jit(solution)/shard_map/ppermute | solution.py:420
  100.5 2.5 %collective-permute-start.41 = (bf16[400,128]{1,0:T(8,128)(2,1)S(1)}, bf16[400,128]{1,0:T(8,128)(2,1)S(1)}, u32[]{:S(2)}, u32[]{:S(2)}) collective-permute-start(bf16[400,128]{1,0:T(8,128)(2,1)S(1)} %shard_map.185.own), channel_id=1, source_target_pairs={{0,96},{1,7},{2,98},{3,1},{4,100},{5,3},{6,102},{7,5},{8,104},{9,1... | collective-permute-start | bytes 307208 | tf_op jit(solution)/shard_map/ppermute | solution.py:420
  105.7 2.4 %collective-permute-done.40.r2 = bf16[400,128]{1,0:T(8,128)(2,1)S(1)} collective-permute-done((bf16[400,128]{1,0:T(8,128)(2,1)S(1)}, bf16[400,128]{1,0:T(8,128)(2,1)S(1)}, u32[]{:S(2)}, u32[]{:S(2)}) %collective-permute-start.40) | collective-permute-done | bytes 102432 | tf_op jit(solution)/shard_map/ppermute | solution.py:420
  109.1 2.3 %collective-permute-start.44 = (bf16[1600,128]{1,0:T(8,128)(2,1)S(1)}, bf16[1600,128]{1,0:T(8,128)(2,1)S(1)}, u32[]{:S(2)}, u32[]{:S(2)}) collective-permute-start(bf16[1600,128]{1,0:T(8,128)(2,1)S(1)} %shard_map.186.refs_0_), channel_id=1, source_target_pairs={{0,6},{1,25},{2,0},{3,27},{4,2},{5,29},{6,4},{7,31},{8,14},{9,1},{... | collective-permute-start | bytes 1228808 | tf_op jit(solution)/shard_map/ppermute | solution.py:420
  112.1 6.0 %collective-permute-start.45 = (bf16[1600,128]{1,0:T(8,128)(2,1)S(1)}, bf16[1600,128]{1,0:T(8,128)(2,1)S(1)}, u32[]{:S(2)}, u32[]{:S(2)}) collective-permute-start(bf16[1600,128]{1,0:T(8,128)(2,1)S(1)} %shard_map.186.refs_0_), channel_id=1, source_target_pairs={{0,1},{1,0},{2,3},{3,2},{4,5},{5,4},{6,7},{7,6},{8,9},{9,8},{10,11... | collective-permute-start | bytes 1228808 | tf_op jit(solution)/shard_map/ppermute | solution.py:407
  118.1 2.6 %collective-permute-done.44.refs_3_ = bf16[1600,128]{1,0:T(8,128)(2,1)S(1)} collective-permute-done((bf16[1600,128]{1,0:T(8,128)(2,1)S(1)}, bf16[1600,128]{1,0:T(8,128)(2,1)S(1)}, u32[]{:S(2)}, u32[]{:S(2)}) %collective-permute-start.44) | collective-permute-done | bytes 409632 | tf_op jit(solution)/shard_map/ppermute | solution.py:420
  120.7 6.1 %collective-permute-start.48 = (bf16[1600,128]{1,0:T(8,128)(2,1)S(1)}, bf16[1600,128]{1,0:T(8,128)(2,1)S(1)}, u32[]{:S(2)}, u32[]{:S(2)}) collective-permute-start(bf16[1600,128]{1,0:T(8,128)(2,1)S(1)} %collective-permute-done.44.refs_3_), channel_id=1, source_target_pairs={{0,1},{1,0},{2,3},{3,2},{4,5},{5,4},{6,7},{7,6},{8,9},{9,8},{10,11... | collective-permute-start | bytes 1228808 | tf_op jit(solution)/shard_map/ppermute | solution.py:407
  126.8 3.9 %collective-permute-start.46 = (bf16[1600,128]{1,0:T(8,128)(2,1)S(1)}, bf16[1600,128]{1,0:T(8,128)(2,1)S(1)}, u32[]{:S(2)}, u32[]{:S(2)}) collective-permute-start(bf16[1600,128]{1,0:T(8,128)(2,1)S(1)} %collective-permute-done.42.refs_1_), channel_id=1, source_target_pairs={{0,1},{1,0},{2,3},{3,2},{4,5},{5,4},{6,7},{7,6},{8,9},{9,8},{10,11... | collective-permute-start | bytes 1228808 | tf_op jit(solution)/shard_map/ppermute | solution.py:407
  132.2 4.2 %shard_map.187 = (f32[64,512]{1,0:T(8,128)}, f32[64,512]{1,0:T(8,128)}, f32[2048,512]{1,0:T(8,128)}, f32[4,2,64,1024]{3,2,1,0:T(8,128)}) custom-call(s32[2]{0:T(128)S(1)} %pad_add_fusion.xc, s32[2]{0:T(128)S(1)} %pad_add_fusion.1.yz, bf16[1600,128]{1,0:T(8,128)(2,1)S(1)} %shard_map.186.refs_0_, bf16[1600,128]{1,0:T(8,128)(2,1)S(1)} %collective-permute-done.42.refs_1_, ...), custom_call_target="tpu_custom_call" | custom-call | flops 1 | bytes 1 | tf_op jit(solution)/shard_map/pallas_call | solution.py:32
  (142 shorter events, 47.6 us)
Async XLA Ops:
  0.6 8.7 %collective-permute-start.2 = (bf16[64,1024]{1,0:T(8,128)(2,1)}, bf16[64,1024]{1,0:T(8,128)(2,1)S(1)}, u32[]{:S(2)}, u32[]{:S(2)}) collective-permute-start(bf16[64,1024]{1,0:T(8,128)(2,1)} %bitcast.17), channel_id=1, source_target_pairs={{0,6},{1,7},{2,0},{3,1},{4,2},{5,3},{6,4},{7,5},{8,14},{9,15},{10,... | collective-permute-start | bytes 393224 | tf_op jit(solution)/shard_map/ppermute | solution.py:403
  4.5 9.2 %collective-permute-start = (bf16[64,1024]{1,0:T(8,128)(2,1)}, bf16[64,1024]{1,0:T(8,128)(2,1)S(1)}, u32[]{:S(2)}, u32[]{:S(2)}) collective-permute-start(bf16[64,1024]{1,0:T(8,128)(2,1)} %bitcast.19), channel_id=1, source_target_pairs={{0,2},{1,3},{2,4},{3,5},{4,6},{5,7},{6,0},{7,1},{8,10},{9,11},{10,... | collective-permute-start | bytes 393224 | tf_op jit(solution)/shard_map/ppermute | solution.py:403
  5.1 9.6 %collective-permute-start.3 = (bf16[64,1024]{1,0:T(8,128)(2,1)}, bf16[64,1024]{1,0:T(8,128)(2,1)S(1)}, u32[]{:S(2)}, u32[]{:S(2)}) collective-permute-start(bf16[64,1024]{1,0:T(8,128)(2,1)} %bitcast.20), channel_id=1, source_target_pairs={{0,1},{1,0},{2,3},{3,2},{4,5},{5,4},{6,7},{7,6},{8,9},{9,8},{10,11... | collective-permute-start | bytes 393224 | tf_op jit(solution)/shard_map/ppermute | solution.py:407
  14.4 9.6 %collective-permute-start.12 = (bf16[64,1024]{1,0:T(8,128)(2,1)}, bf16[64,1024]{1,0:T(8,128)(2,1)S(1)}, u32[]{:S(2)}, u32[]{:S(2)}) collective-permute-start(bf16[64,1024]{1,0:T(8,128)(2,1)} %bitcast.28), channel_id=1, source_target_pairs={{0,6},{1,7},{2,0},{3,1},{4,2},{5,3},{6,4},{7,5},{8,14},{9,15},{10,... | collective-permute-start | bytes 393224 | tf_op jit(solution)/shard_map/ppermute | solution.py:403
  14.7 9.3 %collective-permute-start.11 = (bf16[64,1024]{1,0:T(8,128)(2,1)}, bf16[64,1024]{1,0:T(8,128)(2,1)S(1)}, u32[]{:S(2)}, u32[]{:S(2)}) collective-permute-start(bf16[64,1024]{1,0:T(8,128)(2,1)} %bitcast.29), channel_id=1, source_target_pairs={{0,4},{1,5},{2,6},{3,7},{4,0},{5,1},{6,2},{7,3},{8,12},{9,13},{10,... | collective-permute-start | bytes 393224 | tf_op jit(solution)/shard_map/ppermute | solution.py:403
  15.3 9.4 %collective-permute-start.10 = (bf16[64,1024]{1,0:T(8,128)(2,1)}, bf16[64,1024]{1,0:T(8,128)(2,1)S(1)}, u32[]{:S(2)}, u32[]{:S(2)}) collective-permute-start(bf16[64,1024]{1,0:T(8,128)(2,1)} %bitcast.30), channel_id=1, source_target_pairs={{0,2},{1,3},{2,4},{3,5},{4,6},{5,7},{6,0},{7,1},{8,10},{9,11},{10,... | collective-permute-start | bytes 393224 | tf_op jit(solution)/shard_map/ppermute | solution.py:403
  16.1 10.9 %collective-permute-start.13 = (bf16[64,1024]{1,0:T(8,128)(2,1)}, bf16[64,1024]{1,0:T(8,128)(2,1)S(1)}, u32[]{:S(2)}, u32[]{:S(2)}) collective-permute-start(bf16[64,1024]{1,0:T(8,128)(2,1)} %bitcast.31), channel_id=1, source_target_pairs={{0,1},{1,0},{2,3},{3,2},{4,5},{5,4},{6,7},{7,6},{8,9},{9,8},{10,11... | collective-permute-start | bytes 393224 | tf_op jit(solution)/shard_map/ppermute | solution.py:407
  25.2 7.6 %collective-permute-start.15 = (bf16[64,1024]{1,0:T(8,128)(2,1)S(1)}, bf16[64,1024]{1,0:T(8,128)(2,1)S(1)}, u32[]{:S(2)}, u32[]{:S(2)}) collective-permute-start(bf16[64,1024]{1,0:T(8,128)(2,1)S(1)} %collective-permute-done.11.refs_2_.refs_10_), channel_id=1, source_target_pairs={{0,1},{1,0},{2,3},{3,2},{4,5},{5,4},{6,7},{7,6},{8,9},{9,8},{10,11... | collective-permute-start | bytes 393224 | tf_op jit(solution)/shard_map/ppermute | solution.py:407
  25.2 9.1 %collective-permute-start.16 = (bf16[64,1024]{1,0:T(8,128)(2,1)S(1)}, bf16[64,1024]{1,0:T(8,128)(2,1)S(1)}, u32[]{:S(2)}, u32[]{:S(2)}) collective-permute-start(bf16[64,1024]{1,0:T(8,128)(2,1)S(1)} %collective-permute-done.12.refs_3_.refs_11_), channel_id=1, source_target_pairs={{0,1},{1,0},{2,3},{3,2},{4,5},{5,4},{6,7},{7,6},{8,9},{9,8},{10,11... | collective-permute-start | bytes 393224 | tf_op jit(solution)/shard_map/ppermute | solution.py:407
  25.7 12.9 %collective-permute-start.9 = (bf16[512,128]{1,0:T(8,128)(2,1)S(1)}, bf16[512,128]{1,0:T(8,128)(2,1)S(1)}, u32[]{:S(2)}, u32[]{:S(2)}) collective-permute-start(bf16[512,128]{1,0:T(8,128)(2,1)S(1)} %get-tuple-element.103.d0), channel_id=1, source_target_pairs={{0,6},{1,7},{2,0},{3,1},{4,2},{5,3},{6,4},{7,5},{8,14},{9,15},{10,... | collective-permute-start | bytes 393224 | tf_op jit(solution)/shard_map/ppermute | solution.py:403
  27.0 11.6 %collective-permute-start.8 = (bf16[512,128]{1,0:T(8,128)(2,1)S(1)}, bf16[512,128]{1,0:T(8,128)(2,1)S(1)}, u32[]{:S(2)}, u32[]{:S(2)}) collective-permute-start(bf16[512,128]{1,0:T(8,128)(2,1)S(1)} %get-tuple-element.103.d0), channel_id=1, source_target_pairs={{0,4},{1,5},{2,6},{3,7},{4,0},{5,1},{6,2},{7,3},{8,12},{9,13},{10,... | collective-permute-start | bytes 393224 | tf_op jit(solution)/shard_map/ppermute | solution.py:403
  28.5 10.1 %collective-permute-start.7 = (bf16[512,128]{1,0:T(8,128)(2,1)S(1)}, bf16[512,128]{1,0:T(8,128)(2,1)S(1)}, u32[]{:S(2)}, u32[]{:S(2)}) collective-permute-start(bf16[512,128]{1,0:T(8,128)(2,1)S(1)} %get-tuple-element.103.d0), channel_id=1, source_target_pairs={{0,2},{1,3},{2,4},{3,5},{4,6},{5,7},{6,0},{7,1},{8,10},{9,11},{10,... | collective-permute-start | bytes 393224 | tf_op jit(solution)/shard_map/ppermute | solution.py:403
  52.9 8.6 %collective-permute-start.23 = (bf16[512,128]{1,0:T(8,128)(2,1)S(1)}, bf16[512,128]{1,0:T(8,128)(2,1)S(1)}, u32[]{:S(2)}, u32[]{:S(2)}) collective-permute-start(bf16[512,128]{1,0:T(8,128)(2,1)S(1)} %get-tuple-element.125), channel_id=1, source_target_pairs={{0,4},{1,5},{2,6},{3,7},{4,0},{5,1},{6,2},{7,3},{8,12},{9,13},{10,... | collective-permute-start | bytes 393224 | tf_op jit(solution)/shard_map/ppermute | solution.py:403
  68.4 7.7 %collective-permute-start.30 = (bf16[832,128]{1,0:T(8,128)(2,1)S(1)}, bf16[832,128]{1,0:T(8,128)(2,1)S(1)}, u32[]{:S(2)}, u32[]{:S(2)}) collective-permute-start(bf16[832,128]{1,0:T(8,128)(2,1)S(1)} %get-tuple-element.139), channel_id=1, source_target_pairs={{0,2},{1,3},{2,4},{3,5},{4,6},{5,7},{6,0},{7,1},{8,10},{9,11},{10,... | collective-permute-start | bytes 638984 | tf_op jit(solution)/shard_map/ppermute | solution.py:403
  68.9 12.7 %collective-permute-start.31 = (bf16[832,128]{1,0:T(8,128)(2,1)S(1)}, bf16[832,128]{1,0:T(8,128)(2,1)S(1)}, u32[]{:S(2)}, u32[]{:S(2)}) collective-permute-start(bf16[832,128]{1,0:T(8,128)(2,1)S(1)} %get-tuple-element.140), channel_id=1, source_target_pairs={{0,4},{1,5},{2,6},{3,7},{4,0},{5,1},{6,2},{7,3},{8,12},{9,13},{10,... | collective-permute-start | bytes 638984 | tf_op jit(solution)/shard_map/ppermute | solution.py:403
  72.0 9.6 %collective-permute-start.32 = (bf16[832,128]{1,0:T(8,128)(2,1)S(1)}, bf16[832,128]{1,0:T(8,128)(2,1)S(1)}, u32[]{:S(2)}, u32[]{:S(2)}) collective-permute-start(bf16[832,128]{1,0:T(8,128)(2,1)S(1)} %get-tuple-element.141), channel_id=1, source_target_pairs={{0,6},{1,7},{2,0},{3,1},{4,2},{5,3},{6,4},{7,5},{8,14},{9,15},{10,... | collective-permute-start | bytes 638984 | tf_op jit(solution)/shard_map/ppermute | solution.py:403
  82.3 7.3 %collective-permute-start.33 = (bf16[400,128]{1,0:T(8,128)(2,1)S(1)}, bf16[400,128]{1,0:T(8,128)(2,1)S(1)}, u32[]{:S(2)}, u32[]{:S(2)}) collective-permute-start(bf16[400,128]{1,0:T(8,128)(2,1)S(1)} %get-tuple-element.167), channel_id=1, source_target_pairs={{0,32},{1,9},{2,34},{3,11},{4,36},{5,13},{6,38},{7,15},{8,40},{9,1... | collective-permute-start | bytes 307208 | tf_op jit(solution)/shard_map/ppermute | solution.py:420
  88.6 8.0 %collective-permute-start.27 = (bf16[64,512]{1,0:T(8,128)(2,1)S(1)}, bf16[64,512]{1,0:T(8,128)(2,1)S(1)}, u32[]{:S(2)}, u32[]{:S(2)}) collective-permute-start(bf16[64,512]{1,0:T(8,128)(2,1)S(1)} %get-tuple-element.134), channel_id=1, source_target_pairs={{0,2},{1,3},{2,4},{3,5},{4,6},{5,7},{6,0},{7,1},{8,10},{9,11},{10,... | collective-permute-start | bytes 196616 | tf_op jit(solution)/shard_map/ppermute | solution.py:403
  91.2 9.3 %collective-permute-start.38 = (bf16[400,128]{1,0:T(8,128)(2,1)S(1)}, bf16[400,128]{1,0:T(8,128)(2,1)S(1)}, u32[]{:S(2)}, u32[]{:S(2)}) collective-permute-start(bf16[400,128]{1,0:T(8,128)(2,1)S(1)} %shard_map.183.a), channel_id=1, source_target_pairs={{0,24},{1,97},{2,26},{3,99},{4,28},{5,101},{6,30},{7,103},{8,0},{9... | collective-permute-start | bytes 307208 | tf_op jit(solution)/shard_map/ppermute | solution.py:420
  109.1 11.6 %collective-permute-start.44 = (bf16[1600,128]{1,0:T(8,128)(2,1)S(1)}, bf16[1600,128]{1,0:T(8,128)(2,1)S(1)}, u32[]{:S(2)}, u32[]{:S(2)}) collective-permute-start(bf16[1600,128]{1,0:T(8,128)(2,1)S(1)} %shard_map.186.refs_0_), channel_id=1, source_target_pairs={{0,6},{1,25},{2,0},{3,27},{4,2},{5,29},{6,4},{7,31},{8,14},{9,1},{... | collective-permute-start | bytes 1228808 | tf_op jit(solution)/shard_map/ppermute | solution.py:420
  111.4 15.4 %collective-permute-start.43 = (bf16[1600,128]{1,0:T(8,128)(2,1)S(1)}, bf16[1600,128]{1,0:T(8,128)(2,1)S(1)}, u32[]{:S(2)}, u32[]{:S(2)}) collective-permute-start(bf16[1600,128]{1,0:T(8,128)(2,1)S(1)} %shard_map.186.refs_0_), channel_id=1, source_target_pairs={{0,4},{1,17},{2,6},{3,19},{4,0},{5,21},{6,2},{7,23},{8,12},{9,25},... | collective-permute-start | bytes 1228808 | tf_op jit(solution)/shard_map/ppermute | solution.py:420
  111.9 15.0 %collective-permute-start.42 = (bf16[1600,128]{1,0:T(8,128)(2,1)S(1)}, bf16[1600,128]{1,0:T(8,128)(2,1)S(1)}, u32[]{:S(2)}, u32[]{:S(2)}) collective-permute-start(bf16[1600,128]{1,0:T(8,128)(2,1)S(1)} %shard_map.186.refs_0_), channel_id=1, source_target_pairs={{0,2},{1,9},{2,4},{3,11},{4,6},{5,13},{6,0},{7,15},{8,10},{9,17},{... | collective-permute-start | bytes 1228808 | tf_op jit(solution)/shard_map/ppermute | solution.py:420
  112.1 18.8 %collective-permute-start.45 = (bf16[1600,128]{1,0:T(8,128)(2,1)S(1)}, bf16[1600,128]{1,0:T(8,128)(2,1)S(1)}, u32[]{:S(2)}, u32[]{:S(2)}) collective-permute-start(bf16[1600,128]{1,0:T(8,128)(2,1)S(1)} %shard_map.186.refs_0_), channel_id=1, source_target_pairs={{0,1},{1,0},{2,3},{3,2},{4,5},{5,4},{6,7},{7,6},{8,9},{9,8},{10,11... | collective-permute-start | bytes 1228808 | tf_op jit(solution)/shard_map/ppermute | solution.py:407
  120.7 10.2 %collective-permute-start.48 = (bf16[1600,128]{1,0:T(8,128)(2,1)S(1)}, bf16[1600,128]{1,0:T(8,128)(2,1)S(1)}, u32[]{:S(2)}, u32[]{:S(2)}) collective-permute-start(bf16[1600,128]{1,0:T(8,128)(2,1)S(1)} %collective-permute-done.44.refs_3_), channel_id=1, source_target_pairs={{0,1},{1,0},{2,3},{3,2},{4,5},{5,4},{6,7},{7,6},{8,9},{9,8},{10,11... | collective-permute-start | bytes 1228808 | tf_op jit(solution)/shard_map/ppermute | solution.py:407
  (50 other events, 335.8 us)

commit v2 on v1

--- a/solution.py
+++ b/solution.py
@@ -19,9 +19,19 @@
 
 
 def call(
-    body, outs, args, scalars=0, scratch=(), vmem=40, any_in=0, far_in=0, far_out=0
+    body, outs, args, here="", scalars=0, scratch=(), vmem=40, any_in=0, far_in=0, far_out=0
 ):
     n_in, n_out = len(args), len(outs)
+
+    def placed(*refs):
+        g, d = lax.axis_index("graph"), lax.axis_index("dp")
+        x, c, y, z = g >> 1, g & 1, d >> 2, d & 3
+        names = {
+            "": (), "x": ((x, c),), "xy": ((x, c), (y, z)),
+            "part": ((jnp.where(c == 0, y, z),),), "place": ((jnp.where(c == 0, y, x),),),
+        }
+        body(*names[here], *refs)
+
     in_specs = [pl.BlockSpec(memory_space=pltpu.SMEM)] * scalars
     in_specs += [pl.BlockSpec(memory_space=pltpu.VMEM)] * (n_in - scalars - any_in - far_in)
     in_specs += [pl.BlockSpec(memory_space=pl.ANY)] * any_in
@@ -30,7 +40,7 @@
     out_specs += [pl.BlockSpec(memory_space=pltpu.HBM)] * far_out
     near, far = args[: n_in - far_in], args[n_in - far_in :]
     return pl.pallas_call(
-        body,
+        placed if here else body,
         out_shape=[
             pltpu.HBM(o.shape, o.dtype) if i >= n_out - far_out else o for i, o in enumerate(outs)
         ],
@@ -71,9 +81,17 @@
     return jnp.concatenate([hot(col == lane + j) for j in range(0, width, 128)], axis=1)
 
 
-def prep_body(
-    cnt, src_r, tgt_r, in_r, out_r, basis_t, st, il, ilt, ol, olt, basis, in_hi, out_hi
-):
+def prep_body(cnt, *refs):
+    s, st, il, ilt, ol, olt, basis, in_hi, out_hi, w_ne, edges = refs[7:18]
+    src_r, tgt_r, in_r, out_r, basis_t, sems = refs[18:]
+    nears = (src_r, tgt_r, in_r, out_r, basis_t, w_ne, edges)
+    loads = [fetch(refs[i], near, sems.at[i]) for i, near in enumerate(nears)]
+    for copy in loads[:4]:
+        copy.wait()
+    for i in range(4):
+        ch = slice(256 * i, 256 * i + 256)
+        s[ch, 0:512] = hot_rows(column(src_r[:, ch]), 512)
+        s[ch, 512:1024] = hot_rows(column(tgt_r[:, ch]), 512)
     row = lax.broadcasted_iota(jnp.int32, (128, 1024), 0)
     for i in range(4):
         ch = slice(128 * i, 128 * i + 128)
@@ -94,6 +112,8 @@
         ch = slice(64 * i, 64 * i + 64)
         ilt[ch, :] = hot(in_lo == row + 64 * i)
         olt[ch, :] = hot(out_lo == row + 64 * i)
+    for copy in loads[4:]:
+        copy.wait()
     basis[...] = jnp.concatenate([basis_t[...], basis_t[...]], axis=0).T
 
 
@@ -103,45 +123,24 @@
     return copy
 
 
-def gathered(xc, refs, out, sems):
-    x, c = xc[0], xc[1]
-    copies = []
+def gathered(xc, refs, out):
+    x, c = xc
     for k in range(4):
         g = 2 * lax.rem(x + 4 - k, 4)
-        copies.append(fetch(refs[k], out.at[at(g + c, 64), :], sems.at[2 * k]))
-        copies.append(fetch(refs[4 + k], out.at[at(g + 1 - c, 64), :], sems.at[2 * k + 1]))
-    return copies
+        out[at(g + c, 64), :] = refs[k][...]
+        out[at(g + 1 - c, 64), :] = refs[4 + k][...]
 
 
 def k1_body(xc, *refs):
-    ends_far, edges_far, w_far = refs[0:2], refs[2], refs[3]
-    down, inner_far, dsilu_far, nodes, ab, w_ne, edges, ends, wd_t, inner, dsilu, s, sems = refs[13:]
-    loads = [fetch(ends_far[i], ends.at[i], sems.at[i]) for i in range(2)]
-    loads.append(fetch(refs[4], wd_t, sems.at[2]))
-    blocks = gathered(xc, refs[5:13], nodes, sems.at[pl.ds(8, 8)])
-    halves_of_w = [
-        fetch(w_far.at[rows, :], w_ne.at[rows, :], sems.at[3 + h])
-        for h, rows in enumerate((slice(0, 1024), slice(1024, 2048)))
-    ]
-    load_edges = fetch(edges_far, edges, sems.at[5])
-    for copy in loads:
-        copy.wait()
-    wd = (left(wd_t[...]), right(wd_t[...]))
-    for i in range(4):
-        ch = slice(256 * i, 256 * i + 256)
-        for j in range(2):
-            s[ch, 512 * j : 512 * j + 512] = hot_rows(column(ends[j, :, ch]), 512)
-    for copy in blocks:
-        copy.wait()
+    s, edges, w_ne, w_down_t, down, inner, dsilu, nodes, ab = refs[8:]
+    gathered(xc, refs[:8], nodes)
     for h in range(2):
-        halves_of_w[h].wait()
         for i in range(2):
             rows = slice(512 * h + 256 * i, 512 * h + 256 * i + 256)
             ab[rows, :] = dot(
                 nodes[256 * i : 256 * i + 256, :], w_ne[1024 * h : 1024 * h + 1024, :]
             ).astype(BF)
-    load_edges.wait()
-    copies = []
+    wd = (left(w_down_t[...]), right(w_down_t[...]))
     for i in range(2):
         total = None
         for h in range(2):
@@ -151,42 +150,24 @@
             held = (edges[ch, :].astype(F32) + pre * sig).astype(BF)
             inner[ch, :] = held
             dsilu[ch, :] = (sig * (1.0 + pre * (1.0 - sig))).astype(BF)
-            for near, far in ((inner, inner_far), (dsilu, dsilu_far)):
-                copies.append(fetch(near.at[ch, :], far.at[ch, :], sems.at[16 + len(copies)]))
             part = dot_nt(held, wd[h])
             total = part if total is None else total + part
         down[256 * i : 256 * i + 256, :] = total.astype(BF)
-    for copy in copies:
-        copy.wait()
-
-
-def kq_body(xc, tgt_r, *refs):
-    w_far, d_outer, all_grad, w_en, q, s, sems = refs[8:]
-    load = fetch(w_far, w_en, sems.at[8])
-    blocks = gathered(xc, refs[:8], all_grad, sems)
-    for i in range(4):
-        ch = slice(256 * i, 256 * i + 256)
-        s[ch, :] = hot_rows(column(tgt_r[:, ch]), 512)
-    for copy in blocks:
-        copy.wait()
-    load.wait()
+
+
+def kq_body(xc, *refs):
+    w_en, s, d_outer, all_grad, q = refs[8:]
+    gathered(xc, refs[:8], all_grad)
     for i in range(2):
         ch = slice(256 * i, 256 * i + 256)
         q[ch, :] = dot_nt(all_grad[ch, :], w_en[...]).astype(BF)
     for i in range(4):
         ch = slice(256 * i, 256 * i + 256)
-        d_outer[ch, :] = dot(s[ch, :], q[...]).astype(BF)
-
-
-def kw_body(xc, *refs):
-    nodes_t, all_grad, nodes, sems = refs[16:]
-    copies = gathered(xc, refs[:8], nodes, sems)
-    late = gathered(xc, refs[8:16], all_grad, sems.at[pl.ds(8, 8)])
-    for copy in copies:
-        copy.wait()
+        d_outer[ch, :] = dot(s[ch, 512:1024], q[...]).astype(BF)
+
+
+def kw_body(nodes, nodes_t):
     nodes_t[...] = nodes[...].T
-    for copy in late:
-        copy.wait()
 
 
 def halves(value, odd, upper):
@@ -346,7 +327,8 @@
         out[at(lax.rem(i[0] + 4 - k, 4), rows), :] = ref[...]
 
 
-def spread_out(taken, xc, yz, mine, other, gne_far, gen_far, small, rows, cols, gen, sems):
+def end_body(xc, yz, *refs):
+    gup, gdt, gne_far, gen_far, gne, gen, sems = refs[8:]
     x, c, z = xc[0], xc[1], yz[1]
 
     def run(zeros, ones):
@@ -355,47 +337,45 @@
         def send(near, far):
             copies.append(fetch(near, far, sems.at[len(copies)]))
 
-        for i, k in enumerate(taken):
-            b, q = lax.rem(x + 4 - k, 4), lax.rem(z + 4 - k, 4)
+        def take(ref, j, rows, lanes, far_row, far_lane, small, small_row):
+            value = ref[400 * j : 400 * j + 400, :].astype(F32)
+            gne[rows, lanes] = value[0:256]
+            for h in range(2):
+                gen[far_row, :, far_lane(h)] = value[256 + 64 * h : 320 + 64 * h]
+            small[small_row, lanes] = value[384:400]
+
+        for k in range(4):
+            q = lax.rem(z + 4 - k, 4)
             for j in range(4):
-                value = zeros[i][400 * j : 400 * j + 400, :].astype(F32)
-                cols[i, 256 * j : 256 * j + 256, :] = value[0:256]
-                for h in range(2):
-                    gen[0, i, :, 256 * j + 128 * h : 256 * j + 128 * h + 128] = value[
-                        256 + 64 * h : 320 + 64 * h
-                    ]
-                small[0, 16 * j : 16 * j + 16, at(b, 128)] = value[384:400]
-            send(cols.at[i], gne_far.at[0:1024, at(b, 128)])
-            send(gen.at[0, i], gen_far.at[b, 0])
-            for j in range(4):
-                value = ones[i][400 * j : 400 * j + 400, :].astype(F32)
-                rows[i, :, 128 * j : 128 * j + 128] = value[0:256]
-                for h in range(2):
-                    gen[1, i, :, 256 * j + 128 * h : 256 * j + 128 * h + 128] = value[
-                        256 + 64 * h : 320 + 64 * h
-                    ]
-                small[1, at(q, 16), 128 * j : 128 * j + 128] = value[384:400]
-            send(rows.at[i], gne_far.at[at(4 + q, 256), :])
-            for j in range(4):
-                send(gen.at[1, i, :, 256 * j : 256 * j + 256], gen_far.at[j, 1, :, at(q, 256)])
+                take(
+                    ones[k], j, at(4 + q, 256), slice(128 * j, 128 * j + 128),
+                    2 * j + 1, lambda h: at(2 * q + h, 128), gdt, at(q, 16),
+                )
+            send(gne.at[at(4 + q, 256), :], gne_far.at[at(4 + q, 256), :])
+        for j in range(4):
+            send(gen.at[2 * j + 1], gen_far.at[2 * j + 1])
+        for j in range(4):
+            for k in range(4):
+                b = lax.rem(x + 4 - k, 4)
+                take(
+                    zeros[k], j, slice(256 * j, 256 * j + 256), at(b, 128),
+                    2 * b, lambda h: slice(256 * j + 128 * h, 256 * j + 128 * h + 128),
+                    gup, slice(16 * j, 16 * j + 16),
+                )
+            rows = slice(256 * j, 256 * j + 256)
+            send(gne.at[rows, :], gne_far.at[rows, :])
+        for j in range(4):
+            send(gen.at[2 * j], gen_far.at[2 * j])
         for copy in copies:
             copy.wait()
 
     @pl.when(c == 0)
     def _():
-        run(mine, other)
+        run(refs[0:4], refs[4:8])
 
     @pl.when(c == 1)
     def _():
-        run(other, mine)
-
-
-def end_body(xc, yz, *refs):
-    gup, gdt, gne_far, gen_far, small, rows, cols, gen, sems = refs[8:]
-    mine, other = refs[0:4], refs[4:8]
-    spread_out(range(4), xc, yz, mine, other, gne_far, gen_far, small, rows, cols, gen, sems)
-    gup[...] = small[0]
-    gdt[...] = small[1]
+        run(refs[4:8], refs[0:4])
 
 
 def over_x(value, k):
@@ -428,52 +408,41 @@
     nodes, node_grad, edges, source, target, trip_in, trip_out, basis, trip_count,
     w_ne, w_down, w_up, w_en,
 ):
-    g = lax.axis_index("graph")
-    d = lax.axis_index("dp")
-    xc = jnp.stack([g // 2, g % 2]).astype(jnp.int32)
-    yz = jnp.stack([d // 4, d % 4]).astype(jnp.int32)
-    of_part = jnp.where(xc[1] == 0, yz[0], yz[1])[None]
-    of_place = jnp.where(xc[1] == 0, yz[0], xc[0])[None]
     near = (1, 2, 3)
 
     n = [nodes[0]] + [over_x(nodes[0], k) for k in near]
     m = [over_core(n[0])]
     p = [node_grad[0]] + [over_x(node_grad[0], k) for k in near]
+    s, st, il, ilt, ol, olt, basis2, in_hi, out_hi, w_near, edges_near = call(
+        prep_body,
+        [sds((1024, 1024)), sds((1024, 1024)), sds((2048, 512)), sds((512, 2048)),
+         sds((2048, 512)), sds((512, 2048)), sds((2048, 128)), sds((2048, 128), jnp.int32),
+         sds((2048, 128), jnp.int32), sds((2048, 512)), sds((1024, 512))],
+        [trip_count, source, target, trip_in, trip_out, basis[0].T, w_ne, edges[0]],
+        scalars=1,
+        scratch=[pltpu.VMEM((1, 1024), jnp.int32), pltpu.VMEM((1, 1024), jnp.int32),
+                 pltpu.VMEM((1, 2048), jnp.int32), pltpu.VMEM((1, 2048), jnp.int32),
+                 pltpu.VMEM((64, 2048), BF), pltpu.SemaphoreType.DMA((7,))],
+        vmem=12, far_in=7,
+    )
+    *n, s = tie(*n, s)
     m += [over_core(v) for v in n[1:]]
-    down, inner, dsilu = call(
+    down, inner, dsilu, all_nodes = call(
         k1_body,
-        [sds((512, 128)), sds((1024, 512)), sds((1024, 512))],
-        [xc, source, target, edges[0], w_ne, w_down.T, *n, *m],
-        scalars=1,
-        scratch=[pltpu.VMEM((512, 1024), BF), pltpu.VMEM((1024, 512), BF),
-                 pltpu.VMEM((2048, 512), BF), pltpu.VMEM((1024, 512), BF),
-                 pltpu.VMEM((2, 1, 1024), jnp.int32), pltpu.VMEM((64, 512), BF),
-                 pltpu.VMEM((1024, 512), BF), pltpu.VMEM((1024, 512), BF),
-                 pltpu.VMEM((1024, 1024), BF), pltpu.SemaphoreType.DMA((24,))],
-        vmem=24, far_in=13, far_out=2,
+        [sds((512, 128)), sds((1024, 512)), sds((1024, 512)), sds((512, 1024))],
+        [*n, *m, s, edges_near, w_near, w_down.T],
+        here="x", scratch=[pltpu.VMEM((1024, 512), BF)], vmem=12,
     )
 
     t = [down] + [over_x(down, k) for k in near]
     u = [over_core(down)]
-    _, trip_in, p[1], p[2], p[3] = tie(down, trip_in, *p[1:])
+    t[1], t[2], t[3], p[1], p[2], p[3] = tie(*t[1:], *p[1:])
     q = [over_core(v) for v in p]
-    st, il, ilt, ol, olt, basis2, in_hi, out_hi = call(
-        prep_body,
-        [sds((1024, 1024)), sds((2048, 512)), sds((512, 2048)), sds((2048, 512)),
-         sds((512, 2048)), sds((2048, 128)), sds((2048, 128), jnp.int32),
-         sds((2048, 128), jnp.int32)],
-        [trip_count, source, target, trip_in, trip_out, basis[0].T],
-        scalars=1, vmem=24,
-    )
-    (d_outer,) = call(
+    d_outer, all_grad = call(
         kq_body,
-        [sds((1024, 512))],
-        [xc, target, *p, *q, w_en],
-        scalars=1,
-        scratch=[pltpu.VMEM((512, 1024), BF), pltpu.VMEM((512, 1024), BF),
-                 pltpu.VMEM((512, 512), BF), pltpu.VMEM((1024, 512), BF),
-                 pltpu.SemaphoreType.DMA((9,))],
-        vmem=24, far_in=9,
+        [sds((1024, 512)), sds((512, 1024))],
+        [*p, *q, w_en, s],
+        here="x", scratch=[pltpu.VMEM((512, 512), BF)], vmem=12,
     )
     *t, il, d_outer = tie(*t, il, d_outer)
     u += [over_core(v) for v in t[1:]]
@@ -481,44 +450,38 @@
         k2_body,
         [sds((512, 512), F32), sds((512, 512)), sds((1024, 512)), sds((512, 128)),
          sds((1024, 512))],
-        [xc, *t, *u, il, ilt, ol, olt, in_hi, out_hi, basis2, inner, d_outer, w_up],
-        scalars=1,
+        [*t, *u, il, ilt, ol, olt, in_hi, out_hi, basis2, inner, d_outer, w_up],
+        here="x",
         scratch=[pltpu.VMEM((512, 1024), BF), pltpu.VMEM((2048, 128), BF),
-                 pltpu.VMEM((2048, 1024), BF)], vmem=32,
+                 pltpu.VMEM((2048, 1024), BF)], vmem=20,
     )
 
     recv = over_core(send)
-    parts = call(ka_body, [sds((512, 128))] * 4, [xc, keep, recv], scalars=1, vmem=8)
+    parts = call(ka_body, [sds((512, 128))] * 4, [keep, recv], here="x", vmem=8)
     dd = [parts[0]] + [over_x(parts[k], k) for k in near]
     ot, gup, o_keep, o_send = call(
         ko_body,
         [sds((512, 512)), sds((64, 512), F32), sds((256, 512), F32), sds((256, 512))],
-        [xc, outer, st, summed, dzed], scalars=1, vmem=16,
+        [outer, st, summed, dzed], here="x", vmem=16,
     )
     o_recv = over_core(o_send)
     edge_grad, keep, send = call(
         k3_body,
         [sds((1024, 512)), sds((832, 512), F32), sds((832, 512))],
-        [xc, *dd, d_outer, dsilu, inner, st, w_down.T, ot, gup],
-        scalars=1, scratch=[pltpu.VMEM((1024, 512), BF)], vmem=24,
+        [*dd, d_outer, dsilu, inner, st, w_down.T, ot, gup],
+        here="x", scratch=[pltpu.VMEM((1024, 512), BF)], vmem=16,
     )
 
     recv = over_core(send)
-    parts = call(kb_body, [sds((832, 128))] * 4, [xc, keep, recv], scalars=1, vmem=12)
-    recv, o_recv, *held = tie(recv, o_recv, *n, *m, *p, *q)
-    o_parts = call(kr_body, [sds((64, 512))] * 4, [xc, o_keep, o_recv], scalars=1, vmem=8)
-    nodes_t, all_grad = call(
-        kw_body,
-        [sds((1024, 512)), sds((512, 1024))],
-        [xc, *held],
-        scalars=1, scratch=[pltpu.VMEM((512, 1024), BF), pltpu.SemaphoreType.DMA((16,))],
-        vmem=16, far_in=16,
-    )
+    parts = call(kb_body, [sds((832, 128))] * 4, [keep, recv], here="x", vmem=12)
+    recv, o_recv, all_nodes = tie(recv, o_recv, all_nodes)
+    o_parts = call(kr_body, [sds((64, 512))] * 4, [o_keep, o_recv], here="x", vmem=8)
+    (nodes_t,) = call(kw_body, [sds((1024, 512))], [all_nodes], vmem=8)
     parts = [parts[0]] + [over_x(parts[k], k) for k in near]
-    *parts, nodes_t, all_grad = tie(*parts, nodes_t, all_grad)
+    *parts, nodes_t = tie(*parts, nodes_t)
     parts = call(
-        k4_body, [sds((400, 128))] * 4, [of_part, *parts, nodes_t, all_grad],
-        scalars=1, scratch=[pltpu.VMEM((1600, 128), BF)], vmem=16,
+        k4_body, [sds((400, 128))] * 4, [*parts, nodes_t, all_grad],
+        here="part", scratch=[pltpu.VMEM((1600, 128), BF)], vmem=16,
     )
     parts = [parts[0]] + [over_dp(parts[k], k, "yz") for k in near]
     (part,) = call(sum_body, [sds((400, 128))], parts, vmem=8)
@@ -529,18 +492,16 @@
     (new_nodes,) = call(kn_body, [sds((64, 1024))], [*o_parts, nodes[0], w_en], vmem=16)
     parts = [part] + [over_dp(part, k, "yx") for k in near]
     new_nodes, *parts = tie(new_nodes, *parts)
-    (part,) = call(place_body, [sds((1600, 128))], [of_place, *parts], scalars=1, vmem=8)
+    (part,) = call(place_body, [sds((1600, 128))], [*parts], here="place", vmem=8)
     parts = [part] + [over_dp(part, k, "xz") for k in near]
     grad_up, grad_down_t, grad_ne, grad_en = call(
         end_body,
-        [sds((64, 512), F32), sds((64, 512), F32), sds((2048, 512), F32),
-         sds((4, 2, 64, 1024), F32)],
-        [xc, yz, *parts, *[over_core(v) for v in parts]],
-        scalars=2,
-        scratch=[pltpu.VMEM((2, 64, 512), F32), pltpu.VMEM((4, 256, 512), F32),
-                 pltpu.VMEM((4, 1024, 128), F32), pltpu.VMEM((2, 4, 64, 1024), F32),
-                 pltpu.SemaphoreType.DMA((28,))],
-        vmem=24, far_out=2,
+        [sds((64, 512), F32), sds((64, 512), F32), sds((2048, 512), F32), sds((8, 64, 1024), F32)],
+        [*parts, *[over_core(v) for v in parts]],
+        here="xy",
+        scratch=[pltpu.VMEM((2048, 512), F32), pltpu.VMEM((8, 64, 1024), F32),
+                 pltpu.SemaphoreType.DMA((16,))],
+        vmem=16, far_out=2,
     )
     grad_en = grad_en.reshape(512, 1024)
     return (new_nodes[None], edge_grad[None], grad_ne, grad_down_t.T, grad_up, grad_en)

time: 137 us -> 131 us (0.956)
  Pallas kernels: 36.3 us -> 26.2 us
  waiting for transfers between devices: 32.8 us -> 39.5 us
  starting transfers between devices: 64 us -> 62.6 us
    pallas_call x16, Pallas kernels: 36.3 us -> 26.2 us  [call(): pl.pallas_call(placed if here else body, out_shape=[pltpu.HBM(o.shape, o....]
    ppermute x18, waiting for transfers between devices: 18.2 us -> 23.7 us  [over_x(): return lax.ppermute(value, 'graph', perm)]
    ppermute x19, starting transfers between devices: 28 us -> 25 us  [over_core(): return lax.ppermute(value, 'graph', [(i, i ^ 1) for i in range(8)])]
  transfers between devices with their start and end apart: 49 -> 49, of which waited for: 22 -> 24; matrix products, arithmetic and copies ran while one was open for 0% -> 0% of each run, Pallas kernels for 14% -> 9%
where the time goes in v2:
time: 131 us; the launch traced here: 130 us
  starting transfers between devices  62.6 us (48%)
  waiting for transfers between devices  39.5 us (30%)
  Pallas kernels  26.2 us (20%)
  between operations  1.67 us (1%)
    pallas_call x16, Pallas kernels, call(): pl.pallas_call(placed if here else body, out_shape=[pltpu.HBM(o.shape, o....  26.2 us
    ppermute x19, starting transfers between devices, over_core(): return lax.ppermute(value, 'graph', [(i, i ^ 1) for i in range(8)])  25 us
    ppermute x18, waiting for transfers between devices, over_x(): return lax.ppermute(value, 'graph', perm)  23.7 us
    ppermute x18, starting transfers between devices, over_x(): return lax.ppermute(value, 'graph', perm)  21.7 us
    ppermute x12, starting transfers between devices, over_dp(): return lax.ppermute(value, ('dp', 'graph'), perm)  15.9 us
    ppermute x12, waiting for transfers between devices, over_dp(): return lax.ppermute(value, ('dp', 'graph'), perm)  8.81 us
    ppermute x19, waiting for transfers between devices, over_core(): return lax.ppermute(value, 'graph', [(i, i ^ 1) for i in range(8)])  6.99 us
  transfers between devices with their start and end apart: 49, of which 24 were waited for; matrix products, arithmetic and copies ran while one was open for 0% of the time, Pallas kernels for 9%

profile of v2, /device:TPU:1, one launch (start us, length us, event | category | flops | bytes accessed | tf_op | source)
XLA Modules:
  0.0 130.0 jit_solution(2254087050536016663)
XLA Ops:
  0.7 3.4 %collective-permute-start.2 = (bf16[64,1024]{1,0:T(8,128)(2,1)}, bf16[64,1024]{1,0:T(8,128)(2,1)S(1)}, u32[]{:S(2)}, u32[]{:S(2)}) collective-permute-start(bf16[64,1024]{1,0:T(8,128)(2,1)} %bitcast.11), channel_id=1, source_target_pairs={{0,6},{1,7},{2,0},{3,1},{4,2},{5,3},{6,4},{7,5},{8,14},{9,15},{10,... | collective-permute-start | bytes 393224 | tf_op jit(solution)/shard_map/ppermute | solution.py:383
  7.3 4.4 %shard_map.172 = (bf16[1024,1024]{1,0:T(8,128)(2,1)S(1)}, bf16[1024,1024]{1,0:T(8,128)(2,1)S(1)}, bf16[2048,512]{1,0:T(8,128)(2,1)S(1)}, bf16[512,2048]{1,0:T(8,...) custom-call(s32[1,1]{1,0:T(1,128)S(6)} %copy.19.cnt, ...), custom_call_target="tpu_custom_call" | custom-call | flops 1 | bytes 1 | tf_op jit(solution)/shard_map/pallas_call | solution.py:42
  11.8 2.0 %collective-permute-done.refs_1_ = bf16[64,1024]{1,0:T(8,128)(2,1)S(1)} collective-permute-done((bf16[64,1024]{1,0:T(8,128)(2,1)}, bf16[64,1024]{1,0:T(8,128)(2,1)S(1)}, u32[]{:S(2)}, u32[]{:S(2)}) %collective-permute-start) | collective-permute-done | bytes 131104 | tf_op jit(solution)/shard_map/ppermute | solution.py:383
  16.6 3.1 %shard_map.173 = (bf16[512,128]{1,0:T(8,128)(2,1)S(1)}, bf16[1024,512]{1,0:T(8,128)(2,1)S(1)}, bf16[1024,512]{1,0:T(8,128)(2,1)S(1)}, bf16[512,1024]{1,0:T(8,128)(2,1)S(1)}) custom-call(bf16[64,1024]{1,0:T(8,128)(2,1)S(1)} %bitcast.15, bf16[64,1024]{1,0:T(8,128)(2,1)S(1)} %collective-permute-done.refs_1_, ...), custom_call_target="tpu_custom_call" | custom-call | flops 1 | bytes 1 | tf_op jit(solution)/shard_map/pallas_call | solution.py:42
  19.7 2.4 %collective-permute-start.9 = (bf16[512,128]{1,0:T(8,128)(2,1)S(1)}, bf16[512,128]{1,0:T(8,128)(2,1)S(1)}, u32[]{:S(2)}, u32[]{:S(2)}) collective-permute-start(bf16[512,128]{1,0:T(8,128)(2,1)S(1)} %get-tuple-element.109.refs_0_), channel_id=1, source_target_pairs={{0,6},{1,7},{2,0},{3,1},{4,2},{5,3},{6,4},{7,5},{8,14},{9,15},{10,... | collective-permute-start | bytes 393224 | tf_op jit(solution)/shard_map/ppermute | solution.py:383
  27.5 3.7 %collective-permute-done.7.refs_1_ = bf16[512,128]{1,0:T(8,128)(2,1)S(1)} collective-permute-done((bf16[512,128]{1,0:T(8,128)(2,1)S(1)}, bf16[512,128]{1,0:T(8,128)(2,1)S(1)}, u32[]{:S(2)}, u32[]{:S(2)}) %collective-permute-start.7) | collective-permute-done | bytes 131104 | tf_op jit(solution)/shard_map/ppermute | solution.py:383
  37.2 8.3 %shard_map.175 = (f32[512,512]{1,0:T(8,128)S(1)}, bf16[512,512]{1,0:T(8,128)(2,1)S(1)}, bf16[1024,512]{1,0:T(8,128)(2,1)S(1)}, bf16[512,128]{1,0:T(8,128)(2,1)S(1)}, bf16[1024,512]{1,0:T(8,128)(2,1)S(1)}) custom-call(bf16[512,128]{1,0:T(8,128)(2,1)S(1)} %get-tuple-element.109.refs_0_, bf16[512,128]{1,0:T(8,128)(2,1)S(1)} %collective-permute-done.7.refs_1_, ...), custom_call_target="tpu_custom_call" | custom-call | flops 1 | bytes 1 | tf_op jit(solution)/shard_map/pallas_call | solution.py:42
  52.0 4.6 %collective-permute-done.22.refs_1_ = bf16[512,128]{1,0:T(8,128)(2,1)S(1)} collective-permute-done((bf16[512,128]{1,0:T(8,128)(2,1)S(1)}, bf16[512,128]{1,0:T(8,128)(2,1)S(1)}, u32[]{:S(2)}, u32[]{:S(2)}) %collective-permute-start.22) | collective-permute-done | bytes 131104 | tf_op jit(solution)/shard_map/ppermute | solution.py:383
  56.8 1.9 %shard_map.178 = (bf16[1024,512]{1,0:T(8,128)(2,1)}, f32[832,512]{1,0:T(8,128)S(1)}, bf16[832,512]{1,0:T(8,128)(2,1)S(1)}) custom-call(bf16[512,128]{1,0:T(8,128)(2,1)S(1)} %get-tuple-element.129.refs_0_, bf16[512,128]{1,0:T(8,128)(2,1)S(1)} %collective-permute-done.22.refs_1_, bf16[512,128]{1,0:T(8,128)(2,1)S(1)} %collective-permute-done.23.refs_2_, ...), custom_call_target="tpu_custom_call" | custom-call | flops 1 | bytes 1 | tf_op jit(solution)/shard_map/pallas_call | solution.py:42
  60.3 2.0 %collective-permute-done.25.refs_1_ = bf16[832,512]{1,0:T(8,128)(2,1)S(1)} collective-permute-done((bf16[832,512]{1,0:T(8,128)(2,1)S(1)}, bf16[832,512]{1,0:T(8,128)(2,1)S(1)}, u32[]{:S(2)}, u32[]{:S(2)}) %collective-permute-start.25) | collective-permute-done | bytes 852000 | tf_op jit(solution)/shard_map/ppermute | solution.py:387
  63.2 2.9 %collective-permute-start.31 = (bf16[832,128]{1,0:T(8,128)(2,1)S(1)}, bf16[832,128]{1,0:T(8,128)(2,1)S(1)}, u32[]{:S(2)}, u32[]{:S(2)}) collective-permute-start(bf16[832,128]{1,0:T(8,128)(2,1)S(1)} %get-tuple-element.147), channel_id=1, source_target_pairs={{0,4},{1,5},{2,6},{3,7},{4,0},{5,1},{6,2},{7,3},{8,12},{9,13},{10,... | collective-permute-start | bytes 638984 | tf_op jit(solution)/shard_map/ppermute | solution.py:383
  66.5 3.8 %collective-permute-done.30.refs_1_ = bf16[832,128]{1,0:T(8,128)(2,1)S(1)} collective-permute-done((bf16[832,128]{1,0:T(8,128)(2,1)S(1)}, bf16[832,128]{1,0:T(8,128)(2,1)S(1)}, u32[]{:S(2)}, u32[]{:S(2)}) %collective-permute-start.30) | collective-permute-done | bytes 213024 | tf_op jit(solution)/shard_map/ppermute | solution.py:383
  70.3 5.5 %collective-permute-done.31.refs_2_ = bf16[832,128]{1,0:T(8,128)(2,1)S(1)} collective-permute-done((bf16[832,128]{1,0:T(8,128)(2,1)S(1)}, bf16[832,128]{1,0:T(8,128)(2,1)S(1)}, u32[]{:S(2)}, u32[]{:S(2)}) %collective-permute-start.31) | collective-permute-done | bytes 213024 | tf_op jit(solution)/shard_map/ppermute | solution.py:383
  78.1 3.3 %collective-permute-start.34 = (bf16[400,128]{1,0:T(8,128)(2,1)S(1)}, bf16[400,128]{1,0:T(8,128)(2,1)S(1)}, u32[]{:S(2)}, u32[]{:S(2)}) collective-permute-start(bf16[400,128]{1,0:T(8,128)(2,1)S(1)} %get-tuple-element.158), channel_id=1, source_target_pairs={{0,64},{1,17},{2,66},{3,19},{4,68},{5,21},{6,70},{7,23},{8,72},{9,... | collective-permute-start | bytes 307208 | tf_op jit(solution)/shard_map/ppermute | solution.py:400
  85.3 2.8 %collective-permute-start.38 = (bf16[400,128]{1,0:T(8,128)(2,1)S(1)}, bf16[400,128]{1,0:T(8,128)(2,1)S(1)}, u32[]{:S(2)}, u32[]{:S(2)}) collective-permute-start(bf16[400,128]{1,0:T(8,128)(2,1)S(1)} %shard_map.183.a), channel_id=1, source_target_pairs={{0,24},{1,97},{2,26},{3,99},{4,28},{5,101},{6,30},{7,103},{8,0},{9... | collective-permute-start | bytes 307208 | tf_op jit(solution)/shard_map/ppermute | solution.py:400
  90.2 2.1 %collective-permute-start.29 = (bf16[64,512]{1,0:T(8,128)(2,1)S(1)}, bf16[64,512]{1,0:T(8,128)(2,1)S(1)}, u32[]{:S(2)}, u32[]{:S(2)}) collective-permute-start(bf16[64,512]{1,0:T(8,128)(2,1)S(1)} %get-tuple-element.143), channel_id=1, source_target_pairs={{0,6},{1,7},{2,0},{3,1},{4,2},{5,3},{6,4},{7,5},{8,14},{9,15},{10,... | collective-permute-start | bytes 196616 | tf_op jit(solution)/shard_map/ppermute | solution.py:383
  94.6 2.5 %collective-permute-start.41 = (bf16[400,128]{1,0:T(8,128)(2,1)S(1)}, bf16[400,128]{1,0:T(8,128)(2,1)S(1)}, u32[]{:S(2)}, u32[]{:S(2)}) collective-permute-start(bf16[400,128]{1,0:T(8,128)(2,1)S(1)} %shard_map.185.refs_0_), channel_id=1, source_target_pairs={{0,96},{1,7},{2,98},{3,1},{4,100},{5,3},{6,102},{7,5},{8,104},{9,1... | collective-permute-start | bytes 307208 | tf_op jit(solution)/shard_map/ppermute | solution.py:400
  99.8 2.4 %collective-permute-done.40.refs_2_ = bf16[400,128]{1,0:T(8,128)(2,1)S(1)} collective-permute-done((bf16[400,128]{1,0:T(8,128)(2,1)S(1)}, bf16[400,128]{1,0:T(8,128)(2,1)S(1)}, u32[]{:S(2)}, u32[]{:S(2)}) %collective-permute-start.40) | collective-permute-done | bytes 102432 | tf_op jit(solution)/shard_map/ppermute | solution.py:400
  103.1 2.4 %collective-permute-start.44 = (bf16[1600,128]{1,0:T(8,128)(2,1)S(1)}, bf16[1600,128]{1,0:T(8,128)(2,1)S(1)}, u32[]{:S(2)}, u32[]{:S(2)}) collective-permute-start(bf16[1600,128]{1,0:T(8,128)(2,1)S(1)} %shard_map.186.refs_0_), channel_id=1, source_target_pairs={{0,6},{1,25},{2,0},{3,27},{4,2},{5,29},{6,4},{7,31},{8,14},{9,1},{... | collective-permute-start | bytes 1228808 | tf_op jit(solution)/shard_map/ppermute | solution.py:400
  106.2 6.1 %collective-permute-start.45 = (bf16[1600,128]{1,0:T(8,128)(2,1)S(1)}, bf16[1600,128]{1,0:T(8,128)(2,1)S(1)}, u32[]{:S(2)}, u32[]{:S(2)}) collective-permute-start(bf16[1600,128]{1,0:T(8,128)(2,1)S(1)} %shard_map.186.refs_0_), channel_id=1, source_target_pairs={{0,1},{1,0},{2,3},{3,2},{4,5},{5,4},{6,7},{7,6},{8,9},{9,8},{10,11... | collective-permute-start | bytes 1228808 | tf_op jit(solution)/shard_map/ppermute | solution.py:387
  112.3 2.5 %collective-permute-done.44.refs_3_ = bf16[1600,128]{1,0:T(8,128)(2,1)S(1)} collective-permute-done((bf16[1600,128]{1,0:T(8,128)(2,1)S(1)}, bf16[1600,128]{1,0:T(8,128)(2,1)S(1)}, u32[]{:S(2)}, u32[]{:S(2)}) %collective-permute-start.44) | collective-permute-done | bytes 409632 | tf_op jit(solution)/shard_map/ppermute | solution.py:400
  114.8 6.1 %collective-permute-start.48 = (bf16[1600,128]{1,0:T(8,128)(2,1)S(1)}, bf16[1600,128]{1,0:T(8,128)(2,1)S(1)}, u32[]{:S(2)}, u32[]{:S(2)}) collective-permute-start(bf16[1600,128]{1,0:T(8,128)(2,1)S(1)} %collective-permute-done.44.refs_3_), channel_id=1, source_target_pairs={{0,1},{1,0},{2,3},{3,2},{4,5},{5,4},{6,7},{7,6},{8,9},{9,8},{10,11... | collective-permute-start | bytes 1228808 | tf_op jit(solution)/shard_map/ppermute | solution.py:387
  121.0 3.9 %collective-permute-start.46 = (bf16[1600,128]{1,0:T(8,128)(2,1)S(1)}, bf16[1600,128]{1,0:T(8,128)(2,1)S(1)}, u32[]{:S(2)}, u32[]{:S(2)}) collective-permute-start(bf16[1600,128]{1,0:T(8,128)(2,1)S(1)} %collective-permute-done.42.refs_1_), channel_id=1, source_target_pairs={{0,1},{1,0},{2,3},{3,2},{4,5},{5,4},{6,7},{7,6},{8,9},{9,8},{10,11... | collective-permute-start | bytes 1228808 | tf_op jit(solution)/shard_map/ppermute | solution.py:387
  126.3 3.5 %shard_map.187 = (f32[64,512]{1,0:T(8,128)}, f32[64,512]{1,0:T(8,128)}, f32[2048,512]{1,0:T(8,128)}, f32[8,64,1024]{2,1,0:T(8,128)}) custom-call(bf16[1600,128]{1,0:T(8,128)(2,1)S(1)} %shard_map.186.refs_0_, bf16[1600,128]{1,0:T(8,128)(2,1)S(1)} %collective-permute-done.42.refs_1_, bf16[1600,128]{1,0:T(8,128)(2,1)S(1)} %collective-permute-done.43.refs_2_, ...), custom_call_target="tpu_custom_call" | custom-call | flops 1 | bytes 1 | tf_op jit(solution)/shard_map/pallas_call | solution.py:42
  (100 shorter events, 42.6 us)
Async XLA Ops:
  0.7 11.1 %collective-permute-start.2 = (bf16[64,1024]{1,0:T(8,128)(2,1)}, bf16[64,1024]{1,0:T(8,128)(2,1)S(1)}, u32[]{:S(2)}, u32[]{:S(2)}) collective-permute-start(bf16[64,1024]{1,0:T(8,128)(2,1)} %bitcast.11), channel_id=1, source_target_pairs={{0,6},{1,7},{2,0},{3,1},{4,2},{5,3},{6,4},{7,5},{8,14},{9,15},{10,... | collective-permute-start | bytes 393224 | tf_op jit(solution)/shard_map/ppermute | solution.py:383
  4.0 7.8 %collective-permute-start.1 = (bf16[64,1024]{1,0:T(8,128)(2,1)}, bf16[64,1024]{1,0:T(8,128)(2,1)S(1)}, u32[]{:S(2)}, u32[]{:S(2)}) collective-permute-start(bf16[64,1024]{1,0:T(8,128)(2,1)} %bitcast.12), channel_id=1, source_target_pairs={{0,4},{1,5},{2,6},{3,7},{4,0},{5,1},{6,2},{7,3},{8,12},{9,13},{10,... | collective-permute-start | bytes 393224 | tf_op jit(solution)/shard_map/ppermute | solution.py:383
  4.6 9.2 %collective-permute-start = (bf16[64,1024]{1,0:T(8,128)(2,1)}, bf16[64,1024]{1,0:T(8,128)(2,1)S(1)}, u32[]{:S(2)}, u32[]{:S(2)}) collective-permute-start(bf16[64,1024]{1,0:T(8,128)(2,1)} %bitcast.13), channel_id=1, source_target_pairs={{0,2},{1,3},{2,4},{3,5},{4,6},{5,7},{6,0},{7,1},{8,10},{9,11},{10,... | collective-permute-start | bytes 393224 | tf_op jit(solution)/shard_map/ppermute | solution.py:383
  5.2 10.1 %collective-permute-start.3 = (bf16[64,1024]{1,0:T(8,128)(2,1)}, bf16[64,1024]{1,0:T(8,128)(2,1)S(1)}, u32[]{:S(2)}, u32[]{:S(2)}) collective-permute-start(bf16[64,1024]{1,0:T(8,128)(2,1)} %bitcast.14), channel_id=1, source_target_pairs={{0,1},{1,0},{2,3},{3,2},{4,5},{5,4},{6,7},{7,6},{8,9},{9,8},{10,11... | collective-permute-start | bytes 393224 | tf_op jit(solution)/shard_map/ppermute | solution.py:387
  15.0 8.4 %collective-permute-start.12 = (bf16[64,1024]{1,0:T(8,128)(2,1)S(1)}, bf16[64,1024]{1,0:T(8,128)(2,1)S(1)}, u32[]{:S(2)}, u32[]{:S(2)}) collective-permute-start(bf16[64,1024]{1,0:T(8,128)(2,1)S(1)} %bitcast.19), channel_id=1, source_target_pairs={{0,6},{1,7},{2,0},{3,1},{4,2},{5,3},{6,4},{7,5},{8,14},{9,15},{10,... | collective-permute-start | bytes 393224 | tf_op jit(solution)/shard_map/ppermute | solution.py:383
  15.3 8.9 %collective-permute-start.11 = (bf16[64,1024]{1,0:T(8,128)(2,1)S(1)}, bf16[64,1024]{1,0:T(8,128)(2,1)S(1)}, u32[]{:S(2)}, u32[]{:S(2)}) collective-permute-start(bf16[64,1024]{1,0:T(8,128)(2,1)S(1)} %bitcast.20), channel_id=1, source_target_pairs={{0,4},{1,5},{2,6},{3,7},{4,0},{5,1},{6,2},{7,3},{8,12},{9,13},{10,... | collective-permute-start | bytes 393224 | tf_op jit(solution)/shard_map/ppermute | solution.py:383
  15.8 10.0 %collective-permute-start.10 = (bf16[64,1024]{1,0:T(8,128)(2,1)S(1)}, bf16[64,1024]{1,0:T(8,128)(2,1)S(1)}, u32[]{:S(2)}, u32[]{:S(2)}) collective-permute-start(bf16[64,1024]{1,0:T(8,128)(2,1)S(1)} %bitcast.21), channel_id=1, source_target_pairs={{0,2},{1,3},{2,4},{3,5},{4,6},{5,7},{6,0},{7,1},{8,10},{9,11},{10,... | collective-permute-start | bytes 393224 | tf_op jit(solution)/shard_map/ppermute | solution.py:383
  23.4 7.8 %collective-permute-start.7 = (bf16[512,128]{1,0:T(8,128)(2,1)S(1)}, bf16[512,128]{1,0:T(8,128)(2,1)S(1)}, u32[]{:S(2)}, u32[]{:S(2)}) collective-permute-start(bf16[512,128]{1,0:T(8,128)(2,1)S(1)} %get-tuple-element.109.refs_0_), channel_id=1, source_target_pairs={{0,2},{1,3},{2,4},{3,5},{4,6},{5,7},{6,0},{7,1},{8,10},{9,11},{10,... | collective-permute-start | bytes 393224 | tf_op jit(solution)/shard_map/ppermute | solution.py:383
  24.2 8.7 %collective-permute-start.13 = (bf16[64,1024]{1,0:T(8,128)(2,1)S(1)}, bf16[64,1024]{1,0:T(8,128)(2,1)S(1)}, u32[]{:S(2)}, u32[]{:S(2)}) collective-permute-start(bf16[64,1024]{1,0:T(8,128)(2,1)S(1)} %bitcast.22), channel_id=1, source_target_pairs={{0,1},{1,0},{2,3},{3,2},{4,5},{5,4},{6,7},{7,6},{8,9},{9,8},{10,11... | collective-permute-start | bytes 393224 | tf_op jit(solution)/shard_map/ppermute | solution.py:387
  47.7 8.9 %collective-permute-start.22 = (bf16[512,128]{1,0:T(8,128)(2,1)S(1)}, bf16[512,128]{1,0:T(8,128)(2,1)S(1)}, u32[]{:S(2)}, u32[]{:S(2)}) collective-permute-start(bf16[512,128]{1,0:T(8,128)(2,1)S(1)} %get-tuple-element.130), channel_id=1, source_target_pairs={{0,2},{1,3},{2,4},{3,5},{4,6},{5,7},{6,0},{7,1},{8,10},{9,11},{10,... | collective-permute-start | bytes 393224 | tf_op jit(solution)/shard_map/ppermute | solution.py:383
  47.8 8.8 %collective-permute-start.23 = (bf16[512,128]{1,0:T(8,128)(2,1)S(1)}, bf16[512,128]{1,0:T(8,128)(2,1)S(1)}, u32[]{:S(2)}, u32[]{:S(2)}) collective-permute-start(bf16[512,128]{1,0:T(8,128)(2,1)S(1)} %get-tuple-element.131), channel_id=1, source_target_pairs={{0,4},{1,5},{2,6},{3,7},{4,0},{5,1},{6,2},{7,3},{8,12},{9,13},{10,... | collective-permute-start | bytes 393224 | tf_op jit(solution)/shard_map/ppermute | solution.py:383
  49.3 7.6 %collective-permute-start.24 = (bf16[512,128]{1,0:T(8,128)(2,1)S(1)}, bf16[512,128]{1,0:T(8,128)(2,1)S(1)}, u32[]{:S(2)}, u32[]{:S(2)}) collective-permute-start(bf16[512,128]{1,0:T(8,128)(2,1)S(1)} %get-tuple-element.132), channel_id=1, source_target_pairs={{0,6},{1,7},{2,0},{3,1},{4,2},{5,3},{6,4},{7,5},{8,14},{9,15},{10,... | collective-permute-start | bytes 393224 | tf_op jit(solution)/shard_map/ppermute | solution.py:383
  62.5 7.7 %collective-permute-start.30 = (bf16[832,128]{1,0:T(8,128)(2,1)S(1)}, bf16[832,128]{1,0:T(8,128)(2,1)S(1)}, u32[]{:S(2)}, u32[]{:S(2)}) collective-permute-start(bf16[832,128]{1,0:T(8,128)(2,1)S(1)} %get-tuple-element.146), channel_id=1, source_target_pairs={{0,2},{1,3},{2,4},{3,5},{4,6},{5,7},{6,0},{7,1},{8,10},{9,11},{10,... | collective-permute-start | bytes 638984 | tf_op jit(solution)/shard_map/ppermute | solution.py:383
  63.2 12.5 %collective-permute-start.31 = (bf16[832,128]{1,0:T(8,128)(2,1)S(1)}, bf16[832,128]{1,0:T(8,128)(2,1)S(1)}, u32[]{:S(2)}, u32[]{:S(2)}) collective-permute-start(bf16[832,128]{1,0:T(8,128)(2,1)S(1)} %get-tuple-element.147), channel_id=1, source_target_pairs={{0,4},{1,5},{2,6},{3,7},{4,0},{5,1},{6,2},{7,3},{8,12},{9,13},{10,... | collective-permute-start | bytes 638984 | tf_op jit(solution)/shard_map/ppermute | solution.py:383
  66.2 9.6 %collective-permute-start.32 = (bf16[832,128]{1,0:T(8,128)(2,1)S(1)}, bf16[832,128]{1,0:T(8,128)(2,1)S(1)}, u32[]{:S(2)}, u32[]{:S(2)}) collective-permute-start(bf16[832,128]{1,0:T(8,128)(2,1)S(1)} %get-tuple-element.148), channel_id=1, source_target_pairs={{0,6},{1,7},{2,0},{3,1},{4,2},{5,3},{6,4},{7,5},{8,14},{9,15},{10,... | collective-permute-start | bytes 638984 | tf_op jit(solution)/shard_map/ppermute | solution.py:383
  76.4 6.9 %collective-permute-start.33 = (bf16[400,128]{1,0:T(8,128)(2,1)S(1)}, bf16[400,128]{1,0:T(8,128)(2,1)S(1)}, u32[]{:S(2)}, u32[]{:S(2)}) collective-permute-start(bf16[400,128]{1,0:T(8,128)(2,1)S(1)} %get-tuple-element.157), channel_id=1, source_target_pairs={{0,32},{1,9},{2,34},{3,11},{4,36},{5,13},{6,38},{7,15},{8,40},{9,1... | collective-permute-start | bytes 307208 | tf_op jit(solution)/shard_map/ppermute | solution.py:400
  78.1 6.7 %collective-permute-start.34 = (bf16[400,128]{1,0:T(8,128)(2,1)S(1)}, bf16[400,128]{1,0:T(8,128)(2,1)S(1)}, u32[]{:S(2)}, u32[]{:S(2)}) collective-permute-start(bf16[400,128]{1,0:T(8,128)(2,1)S(1)} %get-tuple-element.158), channel_id=1, source_target_pairs={{0,64},{1,17},{2,66},{3,19},{4,68},{5,21},{6,70},{7,23},{8,72},{9,... | collective-permute-start | bytes 307208 | tf_op jit(solution)/shard_map/ppermute | solution.py:400
  82.2 7.9 %collective-permute-start.27 = (bf16[64,512]{1,0:T(8,128)(2,1)S(1)}, bf16[64,512]{1,0:T(8,128)(2,1)S(1)}, u32[]{:S(2)}, u32[]{:S(2)}) collective-permute-start(bf16[64,512]{1,0:T(8,128)(2,1)S(1)} %get-tuple-element.141), channel_id=1, source_target_pairs={{0,2},{1,3},{2,4},{3,5},{4,6},{5,7},{6,0},{7,1},{8,10},{9,11},{10,... | collective-permute-start | bytes 196616 | tf_op jit(solution)/shard_map/ppermute | solution.py:383
  85.3 9.3 %collective-permute-start.38 = (bf16[400,128]{1,0:T(8,128)(2,1)S(1)}, bf16[400,128]{1,0:T(8,128)(2,1)S(1)}, u32[]{:S(2)}, u32[]{:S(2)}) collective-permute-start(bf16[400,128]{1,0:T(8,128)(2,1)S(1)} %shard_map.183.a), channel_id=1, source_target_pairs={{0,24},{1,97},{2,26},{3,99},{4,28},{5,101},{6,30},{7,103},{8,0},{9... | collective-permute-start | bytes 307208 | tf_op jit(solution)/shard_map/ppermute | solution.py:400
  103.1 11.7 %collective-permute-start.44 = (bf16[1600,128]{1,0:T(8,128)(2,1)S(1)}, bf16[1600,128]{1,0:T(8,128)(2,1)S(1)}, u32[]{:S(2)}, u32[]{:S(2)}) collective-permute-start(bf16[1600,128]{1,0:T(8,128)(2,1)S(1)} %shard_map.186.refs_0_), channel_id=1, source_target_pairs={{0,6},{1,25},{2,0},{3,27},{4,2},{5,29},{6,4},{7,31},{8,14},{9,1},{... | collective-permute-start | bytes 1228808 | tf_op jit(solution)/shard_map/ppermute | solution.py:400
  105.6 15.4 %collective-permute-start.43 = (bf16[1600,128]{1,0:T(8,128)(2,1)S(1)}, bf16[1600,128]{1,0:T(8,128)(2,1)S(1)}, u32[]{:S(2)}, u32[]{:S(2)}) collective-permute-start(bf16[1600,128]{1,0:T(8,128)(2,1)S(1)} %shard_map.186.refs_0_), channel_id=1, source_target_pairs={{0,4},{1,17},{2,6},{3,19},{4,0},{5,21},{6,2},{7,23},{8,12},{9,25},... | collective-permute-start | bytes 1228808 | tf_op jit(solution)/shard_map/ppermute | solution.py:400
  106.0 15.0 %collective-permute-start.42 = (bf16[1600,128]{1,0:T(8,128)(2,1)S(1)}, bf16[1600,128]{1,0:T(8,128)(2,1)S(1)}, u32[]{:S(2)}, u32[]{:S(2)}) collective-permute-start(bf16[1600,128]{1,0:T(8,128)(2,1)S(1)} %shard_map.186.refs_0_), channel_id=1, source_target_pairs={{0,2},{1,9},{2,4},{3,11},{4,6},{5,13},{6,0},{7,15},{8,10},{9,17},{... | collective-permute-start | bytes 1228808 | tf_op jit(solution)/shard_map/ppermute | solution.py:400
  106.2 18.7 %collective-permute-start.45 = (bf16[1600,128]{1,0:T(8,128)(2,1)S(1)}, bf16[1600,128]{1,0:T(8,128)(2,1)S(1)}, u32[]{:S(2)}, u32[]{:S(2)}) collective-permute-start(bf16[1600,128]{1,0:T(8,128)(2,1)S(1)} %shard_map.186.refs_0_), channel_id=1, source_target_pairs={{0,1},{1,0},{2,3},{3,2},{4,5},{5,4},{6,7},{7,6},{8,9},{9,8},{10,11... | collective-permute-start | bytes 1228808 | tf_op jit(solution)/shard_map/ppermute | solution.py:387
  114.8 10.1 %collective-permute-start.48 = (bf16[1600,128]{1,0:T(8,128)(2,1)S(1)}, bf16[1600,128]{1,0:T(8,128)(2,1)S(1)}, u32[]{:S(2)}, u32[]{:S(2)}) collective-permute-start(bf16[1600,128]{1,0:T(8,128)(2,1)S(1)} %collective-permute-done.44.refs_3_), channel_id=1, source_target_pairs={{0,1},{1,0},{2,3},{3,2},{4,5},{5,4},{6,7},{7,6},{8,9},{9,8},{10,11... | collective-permute-start | bytes 1228808 | tf_op jit(solution)/shard_map/ppermute | solution.py:387
  (30 other events, 173.3 us)

commit v3 on v2

--- a/solution.py
+++ b/solution.py
@@ -99,11 +99,11 @@
         st[512 + 128 * i : 640 + 128 * i, :] = hot(tgt_r[...] == row + 128 * i)
     pos = lax.broadcasted_iota(jnp.int32, (1, 2048), 1)
     live = pos < cnt[0, 0]
-    in_lo = jnp.where(live, in_r[...] & 511, -1)
+    in_lo = jnp.where(live, in_r[...] & 1023, -1)
     out_lo = out_r[...] & 511
     for i in range(8):
         ch = slice(256 * i, 256 * i + 256)
-        il[ch, :] = hot_rows(column(in_lo[:, ch]), 512)
+        il[ch, :] = hot_rows(column(in_lo[:, ch]), 1024)
         ol[ch, :] = hot_rows(column(out_lo[:, ch]), 512)
         in_hi[ch, :] = column(in_r[:, ch] >> 9)
         out_hi[ch, :] = column(out_r[:, ch] >> 9)
@@ -111,6 +111,7 @@
     for i in range(8):
         ch = slice(64 * i, 64 * i + 64)
         ilt[ch, :] = hot(in_lo == row + 64 * i)
+        ilt[512 + 64 * i : 576 + 64 * i, :] = hot(in_lo == row + 512 + 64 * i)
         olt[ch, :] = hot(out_lo == row + 64 * i)
     for copy in loads[4:]:
         copy.wait()
@@ -140,7 +141,7 @@
             ab[rows, :] = dot(
                 nodes[256 * i : 256 * i + 256, :], w_ne[1024 * h : 1024 * h + 1024, :]
             ).astype(BF)
-    wd = (left(w_down_t[...]), right(w_down_t[...]))
+    wd = swapped(xc[1], left(w_down_t[...]), right(w_down_t[...]))
     for i in range(2):
         total = None
         for h in range(2):
@@ -155,44 +156,50 @@
         down[256 * i : 256 * i + 256, :] = total.astype(BF)
 
 
-def kq_body(xc, *refs):
-    w_en, s, d_outer, all_grad, q = refs[8:]
-    gathered(xc, refs[:8], all_grad)
+def kw_body(nodes, nodes_t):
+    nodes_t[...] = nodes[...].T
+
+
+def swapped(c, first, second):
+    a, b = first.astype(F32), second.astype(F32)
+    return jnp.where(c == 0, a, b).astype(BF), jnp.where(c == 0, b, a).astype(BF)
+
+
+def lane_key(c):
+    lane = lax.broadcasted_iota(jnp.int32, (512, 128), 1)
+    return jnp.where(c == 0, lane, 127 - lane)
+
+
+def halves(value, odd, upper):
+    kept = jnp.where(upper == odd, value, 0.0)
+    return kept + pltpu.roll(kept, 64, 1)
+
+
+def k2_body(xc, *refs):
+    pieces, grads = refs[0:8], refs[8:16]
+    il, ilt, ol, olt, in_hi, out_hi, basis, inner, w_up, w_en, s = refs[16:27]
+    keep, send, outer, summed, dzed, d_outer, all_grad, table, gath, spread, q = refs[27:]
+    x, c = xc
+    gathered(xc, grads, all_grad)
     for i in range(2):
         ch = slice(256 * i, 256 * i + 256)
         q[ch, :] = dot_nt(all_grad[ch, :], w_en[...]).astype(BF)
-    for i in range(4):
-        ch = slice(256 * i, 256 * i + 256)
-        d_outer[ch, :] = dot(s[ch, 512:1024], q[...]).astype(BF)
-
-
-def kw_body(nodes, nodes_t):
-    nodes_t[...] = nodes[...].T
-
-
-def halves(value, odd, upper):
-    kept = jnp.where(upper == odd, value, 0.0)
-    return kept + pltpu.roll(kept, 64, 1)
-
-
-def k2_body(
-    xc, d0, d1, d2, d3, e0, e1, e2, e3, il, ilt, ol, olt, in_hi, out_hi, basis, inner, d_outer, w_up,
-    keep, send, outer, summed, dzed, table, gath, spread,
-):
-    x, c = xc[0], xc[1]
-    for k, (mine, other) in enumerate(((d0, e0), (d1, e1), (d2, e2), (d3, e3))):
-        g = 2 * lax.rem(x + 4 - k, 4)
-        table[:, at(g + c, 128)] = mine[...]
-        table[:, at(g + 1 - c, 128)] = other[...]
+    key = lane_key(c)
+    is_mine = key.astype(F32).astype(BF) < 64
+    for k in range(4):
+        cols = at(lax.rem(x + 4 - k, 4), 128)
+        mine, other = pieces[k][...], pieces[4 + k][...]
+        table[0:512, cols] = jnp.where(is_mine, mine, other)
+        table[512:1024, cols] = jnp.where(is_mine, other, mine)
     upper = lax.broadcasted_iota(jnp.int32, (256, 128), 1) >= 64
     for i in range(8):
         ch = slice(256 * i, 256 * i + 256)
         got = dot(il[ch, :], table[...])
         hi = in_hi[ch, :]
         acc = jnp.zeros((256, 128), F32)
-        for g in range(8):
-            acc = jnp.where((hi >> 1) == g, got[:, 128 * g : 128 * g + 128], acc)
-        term = halves(acc, (hi & 1) == 1, upper) * basis[ch, :].astype(F32)
+        for b in range(4):
+            acc = jnp.where((hi >> 2) == b, got[:, 128 * b : 128 * b + 128], acc)
+        term = halves(acc, ((hi ^ (hi >> 1)) & 1) == 1, upper) * basis[ch, :].astype(F32)
         gath[ch, :] = jnp.where(upper == (out_hi[ch, :] == 1), term, 0.0).astype(BF)
     held = dot(olt[...], gath[...]).astype(BF)
     summed[...] = held
@@ -202,7 +209,9 @@
         zed = dot(held, w)
         sig = jax.nn.sigmoid(zed)
         outer[ch, :] = (inner[ch, :].astype(F32) + zed * sig).astype(BF)
-        dz = (d_outer[ch, :].astype(F32) * (sig * (1.0 + zed * (1.0 - sig)))).astype(BF)
+        back = dot(s[ch, 512:1024], q[...])
+        d_outer[ch, :] = back.astype(BF)
+        dz = (back * (sig * (1.0 + zed * (1.0 - sig)))).astype(BF)
         dzed[ch, :] = dz
         d_sum += dot_nt(dz, w)
     d_sum = d_sum.astype(BF)
@@ -211,17 +220,16 @@
         got = dot(ol[ch, :], d_sum)
         term = halves(got, out_hi[ch, :] == 1, upper) * basis[ch, :].astype(F32)
         hi = in_hi[ch, :]
-        term = jnp.where(upper == ((hi & 1) == 1), term, 0.0).astype(BF)
-        owner = (hi >> 1).astype(F32).astype(BF)
-        for g in range(8):
-            spread[ch, 128 * g : 128 * g + 128] = jnp.where(owner == g, term, jnp.zeros_like(term))
-    whole = [dot(ilt[...], spread[:, 512 * i : 512 * i + 512]) for i in range(2)]
-    for i in range(4):
-        ch = slice(128 * i, 128 * i + 128)
-        part = whole[i // 2][:, 256 * (i % 2) : 256 * (i % 2) + 256]
-        low, high = part[:, 0:128], part[:, 128:256]
-        keep[:, ch] = jnp.where(c == 0, low, high)
-        send[:, ch] = jnp.where(c == 0, high, low).astype(BF)
+        term = jnp.where(upper == (((hi ^ (hi >> 1)) & 1) == 1), term, 0.0).astype(BF)
+        owner = (hi >> 2).astype(F32).astype(BF)
+        for b in range(4):
+            spread[ch, 128 * b : 128 * b + 128] = jnp.where(owner == b, term, jnp.zeros_like(term))
+    part = dot(ilt[...], spread[...])
+    for b in range(4):
+        ch = slice(128 * b, 128 * b + 128)
+        low, high = part[0:512, ch], part[512:1024, ch]
+        keep[:, ch] = jnp.where(key < 64, low, high)
+        send[:, ch] = jnp.where(key < 64, high, low).astype(BF)
 
 
 def ko_body(xc, outer, st, summed, dzed, ot, gup, keep, send):
@@ -267,7 +275,7 @@
 ):
     c = xc[1]
     dd = total4(own[...], r1[...], r2[...], r3[...]).astype(BF)
-    for h, w in enumerate((left(w_down_t[...]), right(w_down_t[...]))):
+    for h, w in enumerate(swapped(c, left(w_down_t[...]), right(w_down_t[...]))):
         for i in range(2):
             rows = slice(256 * i, 256 * i + 256)
             ch = slice(512 * h + 256 * i, 512 * h + 256 * i + 256)
@@ -279,7 +287,8 @@
         send[rows, :] = dot(st[at(2 * (1 - c) + i, 256), :], d_pre[...]).astype(BF)
         keep[rows, :] = dot(st[at(2 * c + i, 256), :], d_pre[...])
     ddt = dd.T
-    gdown = dot(ddt[0:64, :], inner[0:512, :]) + dot(ddt[64:128, :], inner[512:1024, :])
+    first, second = swapped(c, ddt[0:64, :], ddt[64:128, :])
+    gdown = dot(first, inner[0:512, :]) + dot(second, inner[512:1024, :])
     keep[512:576, :] = jnp.where(c == 0, gup[...], gdown)
     send[512:576, :] = jnp.where(c == 0, gdown, gup[...]).astype(BF)
     for i in range(4):
@@ -415,7 +424,7 @@
     p = [node_grad[0]] + [over_x(node_grad[0], k) for k in near]
     s, st, il, ilt, ol, olt, basis2, in_hi, out_hi, w_near, edges_near = call(
         prep_body,
-        [sds((1024, 1024)), sds((1024, 1024)), sds((2048, 512)), sds((512, 2048)),
+        [sds((1024, 1024)), sds((1024, 1024)), sds((2048, 1024)), sds((1024, 2048)),
          sds((2048, 512)), sds((512, 2048)), sds((2048, 128)), sds((2048, 128), jnp.int32),
          sds((2048, 128), jnp.int32), sds((2048, 512)), sds((1024, 512))],
         [trip_count, source, target, trip_in, trip_out, basis[0].T, w_ne, edges[0]],
@@ -438,22 +447,16 @@
     u = [over_core(down)]
     t[1], t[2], t[3], p[1], p[2], p[3] = tie(*t[1:], *p[1:])
     q = [over_core(v) for v in p]
-    d_outer, all_grad = call(
-        kq_body,
-        [sds((1024, 512)), sds((512, 1024))],
-        [*p, *q, w_en, s],
-        here="x", scratch=[pltpu.VMEM((512, 512), BF)], vmem=12,
-    )
-    *t, il, d_outer = tie(*t, il, d_outer)
     u += [over_core(v) for v in t[1:]]
-    keep, send, outer, summed, dzed = call(
+    keep, send, outer, summed, dzed, d_outer, all_grad = call(
         k2_body,
         [sds((512, 512), F32), sds((512, 512)), sds((1024, 512)), sds((512, 128)),
-         sds((1024, 512))],
-        [*t, *u, il, ilt, ol, olt, in_hi, out_hi, basis2, inner, d_outer, w_up],
+         sds((1024, 512)), sds((1024, 512)), sds((512, 1024))],
+        [*t, *u, *p, *q, il, ilt, ol, olt, in_hi, out_hi, basis2, inner, w_up, w_en, s],
         here="x",
-        scratch=[pltpu.VMEM((512, 1024), BF), pltpu.VMEM((2048, 128), BF),
-                 pltpu.VMEM((2048, 1024), BF)], vmem=20,
+        scratch=[pltpu.VMEM((1024, 512), BF), pltpu.VMEM((2048, 128), BF),
+                 pltpu.VMEM((2048, 512), BF), pltpu.VMEM((512, 512), BF)],
+        vmem=20,
     )
 
     recv = over_core(send)

time: 131 us -> 129 us (0.985)
  starting transfers between devices: 62.6 us -> 61.2 us
    ppermute x18, starting transfers between devices: 21.7 us -> 20.2 us  [over_x(): return lax.ppermute(value, 'graph', perm)]
    pallas_call x16 -> x15, Pallas kernels: 26.2 us -> 26.6 us  [call(): pl.pallas_call(placed if here else body, out_shape=[pltpu.HBM(o.shape, o....]
  transfers between devices with their start and end apart: 49 -> 49, of which waited for: 24 -> 22; matrix products, arithmetic and copies ran while one was open for 0% -> 0% of each run, Pallas kernels for 9% -> 9%
where the time goes in v3:
time: 129 us
  starting transfers between devices  61.2 us (47%)
  waiting for transfers between devices  39.7 us (31%)
  Pallas kernels  26.6 us (21%)
  between operations  1.69 us (1%)
    pallas_call x15, Pallas kernels, call(): pl.pallas_call(placed if here else body, out_shape=[pltpu.HBM(o.shape, o....  26.6 us
    ppermute x19, starting transfers between devices, over_core(): return lax.ppermute(value, 'graph', [(i, i ^ 1) for i in range(8)])  25.3 us
    ppermute x18, waiting for transfers between devices, over_x(): return lax.ppermute(value, 'graph', perm)  24.3 us
    ppermute x18, starting transfers between devices, over_x(): return lax.ppermute(value, 'graph', perm)  20.2 us
    ppermute x12, starting transfers between devices, over_dp(): return lax.ppermute(value, ('dp', 'graph'), perm)  15.6 us
    ppermute x12, waiting for transfers between devices, over_dp(): return lax.ppermute(value, ('dp', 'graph'), perm)  9.44 us
    ppermute x19, waiting for transfers between devices, over_core(): return lax.ppermute(value, 'graph', [(i, i ^ 1) for i in range(8)])  5.93 us
  transfers between devices with their start and end apart: 49, of which 22 were waited for; matrix products, arithmetic and copies ran while one was open for 0% of the time, Pallas kernels for 9%

profile of v3, /device:TPU:1, one launch (start us, length us, event | category | flops | bytes accessed | tf_op | source)
XLA Modules:
  0.0 129.1 jit_solution(15844052842871423306)
XLA Ops:
  0.7 3.4 %collective-permute-start.2 = (bf16[64,1024]{1,0:T(8,128)(2,1)}, bf16[64,1024]{1,0:T(8,128)(2,1)S(1)}, u32[]{:S(2)}, u32[]{:S(2)}) collective-permute-start(bf16[64,1024]{1,0:T(8,128)(2,1)} %bitcast.11), channel_id=1, source_target_pairs={{0,6},{1,7},{2,0},{3,1},{4,2},{5,3},{6,4},{7,5},{8,14},{9,15},{10,... | collective-permute-start | bytes 393224 | tf_op jit(solution)/shard_map/ppermute | solution.py:392
  7.3 5.3 %shard_map.172 = (bf16[1024,1024]{1,0:T(8,128)(2,1)S(1)}, bf16[1024,1024]{1,0:T(8,128)(2,1)S(1)}, bf16[2048,1024]{1,0:T(8,128)(2,1)S(1)}, bf16[1024,2048]{1,0:T(...) custom-call(s32[1,1]{1,0:T(1,128)S(6)} %copy.19.cnt, ...), custom_call_target="tpu_custom_call" | custom-call | flops 1 | bytes 1 | tf_op jit(solution)/shard_map/pallas_call | solution.py:42
  16.8 3.2 %shard_map.173 = (bf16[512,128]{1,0:T(8,128)(2,1)S(1)}, bf16[1024,512]{1,0:T(8,128)(2,1)S(1)}, bf16[1024,512]{1,0:T(8,128)(2,1)S(1)}, bf16[512,1024]{1,0:T(8,128)(2,1)S(1)}) custom-call(bf16[64,1024]{1,0:T(8,128)(2,1)S(1)} %bitcast.15, bf16[64,1024]{1,0:T(8,128)(2,1)S(1)} %collective-permute-done.refs_1_, ...), custom_call_target="tpu_custom_call" | custom-call | flops 1 | bytes 1 | tf_op jit(solution)/shard_map/pallas_call | solution.py:42
  20.0 2.7 %collective-permute-start.9 = (bf16[512,128]{1,0:T(8,128)(2,1)S(1)}, bf16[512,128]{1,0:T(8,128)(2,1)S(1)}, u32[]{:S(2)}, u32[]{:S(2)}) collective-permute-start(bf16[512,128]{1,0:T(8,128)(2,1)S(1)} %get-tuple-element.94.refs_0_), channel_id=1, source_target_pairs={{0,6},{1,7},{2,0},{3,1},{4,2},{5,3},{6,4},{7,5},{8,14},{9,15},{10,... | collective-permute-start | bytes 393224 | tf_op jit(solution)/shard_map/ppermute | solution.py:392
  26.0 2.1 %collective-permute-done.8.refs_2_ = bf16[512,128]{1,0:T(8,128)(2,1)S(1)} collective-permute-done((bf16[512,128]{1,0:T(8,128)(2,1)S(1)}, bf16[512,128]{1,0:T(8,128)(2,1)S(1)}, u32[]{:S(2)}, u32[]{:S(2)}) %collective-permute-start.8) | collective-permute-done | bytes 131104 | tf_op jit(solution)/shard_map/ppermute | solution.py:392
  28.1 3.5 %collective-permute-done.7.refs_1_ = bf16[512,128]{1,0:T(8,128)(2,1)S(1)} collective-permute-done((bf16[512,128]{1,0:T(8,128)(2,1)S(1)}, bf16[512,128]{1,0:T(8,128)(2,1)S(1)}, u32[]{:S(2)}, u32[]{:S(2)}) %collective-permute-start.7) | collective-permute-done | bytes 131104 | tf_op jit(solution)/shard_map/ppermute | solution.py:392
  35.3 9.3 %shard_map.174 = (f32[512,512]{1,0:T(8,128)S(1)}, bf16[512,512]{1,0:T(8,128)(2,1)S(1)}, bf16[1024,512]{1,0:T(8,128)(2,1)S(1)}, bf16[512,128]{1,0:T(8,128)(2,1)S(...) custom-call(bf16[512,128]{1,0:T(8,128)(2,1)S(1)} %get-tuple-element.94.refs_0_, ...), custom_call_target="tpu_custom_call" | custom-call | flops 1 | bytes 1 | tf_op jit(solution)/shard_map/pallas_call | solution.py:42
  50.5 5.1 %collective-permute-done.22.refs_1_ = bf16[512,128]{1,0:T(8,128)(2,1)S(1)} collective-permute-done((bf16[512,128]{1,0:T(8,128)(2,1)S(1)}, bf16[512,128]{1,0:T(8,128)(2,1)S(1)}, u32[]{:S(2)}, u32[]{:S(2)}) %collective-permute-start.22) | collective-permute-done | bytes 131104 | tf_op jit(solution)/shard_map/ppermute | solution.py:392
  59.4 1.9 %collective-permute-done.25.refs_1_ = bf16[832,512]{1,0:T(8,128)(2,1)S(1)} collective-permute-done((bf16[832,512]{1,0:T(8,128)(2,1)S(1)}, bf16[832,512]{1,0:T(8,128)(2,1)S(1)}, u32[]{:S(2)}, u32[]{:S(2)}) %collective-permute-start.25) | collective-permute-done | bytes 852000 | tf_op jit(solution)/shard_map/ppermute | solution.py:396
  61.7 3.3 %collective-permute-start.31 = (bf16[832,128]{1,0:T(8,128)(2,1)S(1)}, bf16[832,128]{1,0:T(8,128)(2,1)S(1)}, u32[]{:S(2)}, u32[]{:S(2)}) collective-permute-start(bf16[832,128]{1,0:T(8,128)(2,1)S(1)} %get-tuple-element.135), channel_id=1, source_target_pairs={{0,4},{1,5},{2,6},{3,7},{4,0},{5,1},{6,2},{7,3},{8,12},{9,13},{10,... | collective-permute-start | bytes 638984 | tf_op jit(solution)/shard_map/ppermute | solution.py:392
  65.3 4.0 %collective-permute-done.30.refs_1_ = bf16[832,128]{1,0:T(8,128)(2,1)S(1)} collective-permute-done((bf16[832,128]{1,0:T(8,128)(2,1)S(1)}, bf16[832,128]{1,0:T(8,128)(2,1)S(1)}, u32[]{:S(2)}, u32[]{:S(2)}) %collective-permute-start.30) | collective-permute-done | bytes 213024 | tf_op jit(solution)/shard_map/ppermute | solution.py:392
  69.3 5.2 %collective-permute-done.31.refs_2_ = bf16[832,128]{1,0:T(8,128)(2,1)S(1)} collective-permute-done((bf16[832,128]{1,0:T(8,128)(2,1)S(1)}, bf16[832,128]{1,0:T(8,128)(2,1)S(1)}, u32[]{:S(2)}, u32[]{:S(2)}) %collective-permute-start.31) | collective-permute-done | bytes 213024 | tf_op jit(solution)/shard_map/ppermute | solution.py:392
  76.9 3.4 %collective-permute-start.34 = (bf16[400,128]{1,0:T(8,128)(2,1)S(1)}, bf16[400,128]{1,0:T(8,128)(2,1)S(1)}, u32[]{:S(2)}, u32[]{:S(2)}) collective-permute-start(bf16[400,128]{1,0:T(8,128)(2,1)S(1)} %get-tuple-element.146), channel_id=1, source_target_pairs={{0,64},{1,17},{2,66},{3,19},{4,68},{5,21},{6,70},{7,23},{8,72},{9,... | collective-permute-start | bytes 307208 | tf_op jit(solution)/shard_map/ppermute | solution.py:409
  81.8 2.0 %collective-permute-done.34.c = bf16[400,128]{1,0:T(8,128)(2,1)S(1)} collective-permute-done((bf16[400,128]{1,0:T(8,128)(2,1)S(1)}, bf16[400,128]{1,0:T(8,128)(2,1)S(1)}, u32[]{:S(2)}, u32[]{:S(2)}) %collective-permute-start.34) | collective-permute-done | bytes 102432 | tf_op jit(solution)/shard_map/ppermute | solution.py:409
  84.2 2.8 %collective-permute-start.38 = (bf16[400,128]{1,0:T(8,128)(2,1)S(1)}, bf16[400,128]{1,0:T(8,128)(2,1)S(1)}, u32[]{:S(2)}, u32[]{:S(2)}) collective-permute-start(bf16[400,128]{1,0:T(8,128)(2,1)S(1)} %shard_map.182.a), channel_id=1, source_target_pairs={{0,24},{1,97},{2,26},{3,99},{4,28},{5,101},{6,30},{7,103},{8,0},{9... | collective-permute-start | bytes 307208 | tf_op jit(solution)/shard_map/ppermute | solution.py:409
  90.7 1.8 %collective-permute-done.28.r2 = bf16[64,512]{1,0:T(8,128)(2,1)S(1)} collective-permute-done((bf16[64,512]{1,0:T(8,128)(2,1)S(1)}, bf16[64,512]{1,0:T(8,128)(2,1)S(1)}, u32[]{:S(2)}, u32[]{:S(2)}) %collective-permute-start.28) | collective-permute-done | bytes 65568 | tf_op jit(solution)/shard_map/ppermute | solution.py:392
  93.7 2.5 %collective-permute-start.41 = (bf16[400,128]{1,0:T(8,128)(2,1)S(1)}, bf16[400,128]{1,0:T(8,128)(2,1)S(1)}, u32[]{:S(2)}, u32[]{:S(2)}) collective-permute-start(bf16[400,128]{1,0:T(8,128)(2,1)S(1)} %shard_map.184.refs_0_), channel_id=1, source_target_pairs={{0,96},{1,7},{2,98},{3,1},{4,100},{5,3},{6,102},{7,5},{8,104},{9,1... | collective-permute-start | bytes 307208 | tf_op jit(solution)/shard_map/ppermute | solution.py:409
  98.9 2.4 %collective-permute-done.40.refs_2_ = bf16[400,128]{1,0:T(8,128)(2,1)S(1)} collective-permute-done((bf16[400,128]{1,0:T(8,128)(2,1)S(1)}, bf16[400,128]{1,0:T(8,128)(2,1)S(1)}, u32[]{:S(2)}, u32[]{:S(2)}) %collective-permute-start.40) | collective-permute-done | bytes 102432 | tf_op jit(solution)/shard_map/ppermute | solution.py:409
  102.3 2.2 %collective-permute-start.44 = (bf16[1600,128]{1,0:T(8,128)(2,1)S(1)}, bf16[1600,128]{1,0:T(8,128)(2,1)S(1)}, u32[]{:S(2)}, u32[]{:S(2)}) collective-permute-start(bf16[1600,128]{1,0:T(8,128)(2,1)S(1)} %shard_map.185.refs_0_), channel_id=1, source_target_pairs={{0,6},{1,25},{2,0},{3,27},{4,2},{5,29},{6,4},{7,31},{8,14},{9,1},{... | collective-permute-start | bytes 1228808 | tf_op jit(solution)/shard_map/ppermute | solution.py:409
  105.2 6.0 %collective-permute-start.45 = (bf16[1600,128]{1,0:T(8,128)(2,1)S(1)}, bf16[1600,128]{1,0:T(8,128)(2,1)S(1)}, u32[]{:S(2)}, u32[]{:S(2)}) collective-permute-start(bf16[1600,128]{1,0:T(8,128)(2,1)S(1)} %shard_map.185.refs_0_), channel_id=1, source_target_pairs={{0,1},{1,0},{2,3},{3,2},{4,5},{5,4},{6,7},{7,6},{8,9},{9,8},{10,11... | collective-permute-start | bytes 1228808 | tf_op jit(solution)/shard_map/ppermute | solution.py:396
  111.2 2.6 %collective-permute-done.44.refs_3_ = bf16[1600,128]{1,0:T(8,128)(2,1)S(1)} collective-permute-done((bf16[1600,128]{1,0:T(8,128)(2,1)S(1)}, bf16[1600,128]{1,0:T(8,128)(2,1)S(1)}, u32[]{:S(2)}, u32[]{:S(2)}) %collective-permute-start.44) | collective-permute-done | bytes 409632 | tf_op jit(solution)/shard_map/ppermute | solution.py:409
  113.8 6.2 %collective-permute-start.48 = (bf16[1600,128]{1,0:T(8,128)(2,1)S(1)}, bf16[1600,128]{1,0:T(8,128)(2,1)S(1)}, u32[]{:S(2)}, u32[]{:S(2)}) collective-permute-start(bf16[1600,128]{1,0:T(8,128)(2,1)S(1)} %collective-permute-done.44.refs_3_), channel_id=1, source_target_pairs={{0,1},{1,0},{2,3},{3,2},{4,5},{5,4},{6,7},{7,6},{8,9},{9,8},{10,11... | collective-permute-start | bytes 1228808 | tf_op jit(solution)/shard_map/ppermute | solution.py:396
  120.1 3.9 %collective-permute-start.46 = (bf16[1600,128]{1,0:T(8,128)(2,1)S(1)}, bf16[1600,128]{1,0:T(8,128)(2,1)S(1)}, u32[]{:S(2)}, u32[]{:S(2)}) collective-permute-start(bf16[1600,128]{1,0:T(8,128)(2,1)S(1)} %collective-permute-done.42.refs_1_), channel_id=1, source_target_pairs={{0,1},{1,0},{2,3},{3,2},{4,5},{5,4},{6,7},{7,6},{8,9},{9,8},{10,11... | collective-permute-start | bytes 1228808 | tf_op jit(solution)/shard_map/ppermute | solution.py:396
  125.4 3.5 %shard_map.186 = (f32[64,512]{1,0:T(8,128)}, f32[64,512]{1,0:T(8,128)}, f32[2048,512]{1,0:T(8,128)}, f32[8,64,1024]{2,1,0:T(8,128)}) custom-call(bf16[1600,128]{1,0:T(8,128)(2,1)S(1)} %shard_map.185.refs_0_, bf16[1600,128]{1,0:T(8,128)(2,1)S(1)} %collective-permute-done.42.refs_1_, bf16[1600,128]{1,0:T(8,128)(2,1)S(1)} %collective-permute-done.43.refs_2_, ...), custom_call_target="tpu_custom_call" | custom-call | flops 1 | bytes 1 | tf_op jit(solution)/shard_map/pallas_call | solution.py:42
  (99 shorter events, 38.9 us)
Async XLA Ops:
  0.7 12.0 %collective-permute-start.2 = (bf16[64,1024]{1,0:T(8,128)(2,1)}, bf16[64,1024]{1,0:T(8,128)(2,1)S(1)}, u32[]{:S(2)}, u32[]{:S(2)}) collective-permute-start(bf16[64,1024]{1,0:T(8,128)(2,1)} %bitcast.11), channel_id=1, source_target_pairs={{0,6},{1,7},{2,0},{3,1},{4,2},{5,3},{6,4},{7,5},{8,14},{9,15},{10,... | collective-permute-start | bytes 393224 | tf_op jit(solution)/shard_map/ppermute | solution.py:392
  4.0 8.7 %collective-permute-start.1 = (bf16[64,1024]{1,0:T(8,128)(2,1)}, bf16[64,1024]{1,0:T(8,128)(2,1)S(1)}, u32[]{:S(2)}, u32[]{:S(2)}) collective-permute-start(bf16[64,1024]{1,0:T(8,128)(2,1)} %bitcast.12), channel_id=1, source_target_pairs={{0,4},{1,5},{2,6},{3,7},{4,0},{5,1},{6,2},{7,3},{8,12},{9,13},{10,... | collective-permute-start | bytes 393224 | tf_op jit(solution)/shard_map/ppermute | solution.py:392
  4.6 9.2 %collective-permute-start = (bf16[64,1024]{1,0:T(8,128)(2,1)}, bf16[64,1024]{1,0:T(8,128)(2,1)S(1)}, u32[]{:S(2)}, u32[]{:S(2)}) collective-permute-start(bf16[64,1024]{1,0:T(8,128)(2,1)} %bitcast.13), channel_id=1, source_target_pairs={{0,2},{1,3},{2,4},{3,5},{4,6},{5,7},{6,0},{7,1},{8,10},{9,11},{10,... | collective-permute-start | bytes 393224 | tf_op jit(solution)/shard_map/ppermute | solution.py:392
  5.2 10.3 %collective-permute-start.3 = (bf16[64,1024]{1,0:T(8,128)(2,1)}, bf16[64,1024]{1,0:T(8,128)(2,1)S(1)}, u32[]{:S(2)}, u32[]{:S(2)}) collective-permute-start(bf16[64,1024]{1,0:T(8,128)(2,1)} %bitcast.14), channel_id=1, source_target_pairs={{0,1},{1,0},{2,3},{3,2},{4,5},{5,4},{6,7},{7,6},{8,9},{9,8},{10,11... | collective-permute-start | bytes 393224 | tf_op jit(solution)/shard_map/ppermute | solution.py:396
  15.0 8.4 %collective-permute-start.12 = (bf16[64,1024]{1,0:T(8,128)(2,1)S(1)}, bf16[64,1024]{1,0:T(8,128)(2,1)S(1)}, u32[]{:S(2)}, u32[]{:S(2)}) collective-permute-start(bf16[64,1024]{1,0:T(8,128)(2,1)S(1)} %bitcast.19), channel_id=1, source_target_pairs={{0,6},{1,7},{2,0},{3,1},{4,2},{5,3},{6,4},{7,5},{8,14},{9,15},{10,... | collective-permute-start | bytes 393224 | tf_op jit(solution)/shard_map/ppermute | solution.py:392
  15.5 8.7 %collective-permute-start.11 = (bf16[64,1024]{1,0:T(8,128)(2,1)S(1)}, bf16[64,1024]{1,0:T(8,128)(2,1)S(1)}, u32[]{:S(2)}, u32[]{:S(2)}) collective-permute-start(bf16[64,1024]{1,0:T(8,128)(2,1)S(1)} %bitcast.20), channel_id=1, source_target_pairs={{0,4},{1,5},{2,6},{3,7},{4,0},{5,1},{6,2},{7,3},{8,12},{9,13},{10,... | collective-permute-start | bytes 393224 | tf_op jit(solution)/shard_map/ppermute | solution.py:392
  16.7 9.2 %collective-permute-start.10 = (bf16[64,1024]{1,0:T(8,128)(2,1)S(1)}, bf16[64,1024]{1,0:T(8,128)(2,1)S(1)}, u32[]{:S(2)}, u32[]{:S(2)}) collective-permute-start(bf16[64,1024]{1,0:T(8,128)(2,1)S(1)} %bitcast.21), channel_id=1, source_target_pairs={{0,2},{1,3},{2,4},{3,5},{4,6},{5,7},{6,0},{7,1},{8,10},{9,11},{10,... | collective-permute-start | bytes 393224 | tf_op jit(solution)/shard_map/ppermute | solution.py:392
  23.4 8.1 %collective-permute-start.7 = (bf16[512,128]{1,0:T(8,128)(2,1)S(1)}, bf16[512,128]{1,0:T(8,128)(2,1)S(1)}, u32[]{:S(2)}, u32[]{:S(2)}) collective-permute-start(bf16[512,128]{1,0:T(8,128)(2,1)S(1)} %get-tuple-element.94.refs_0_), channel_id=1, source_target_pairs={{0,2},{1,3},{2,4},{3,5},{4,6},{5,7},{6,0},{7,1},{8,10},{9,11},{10,... | collective-permute-start | bytes 393224 | tf_op jit(solution)/shard_map/ppermute | solution.py:392
  24.2 9.2 %collective-permute-start.17 = (bf16[64,1024]{1,0:T(8,128)(2,1)S(1)}, bf16[64,1024]{1,0:T(8,128)(2,1)S(1)}, u32[]{:S(2)}, u32[]{:S(2)}) collective-permute-start(bf16[64,1024]{1,0:T(8,128)(2,1)S(1)} %bitcast.22), channel_id=1, source_target_pairs={{0,1},{1,0},{2,3},{3,2},{4,5},{5,4},{6,7},{7,6},{8,9},{9,8},{10,11... | collective-permute-start | bytes 393224 | tf_op jit(solution)/shard_map/ppermute | solution.py:396
  25.9 7.6 %collective-permute-start.13 = (bf16[512,128]{1,0:T(8,128)(2,1)S(1)}, bf16[512,128]{1,0:T(8,128)(2,1)S(1)}, u32[]{:S(2)}, u32[]{:S(2)}) collective-permute-start(bf16[512,128]{1,0:T(8,128)(2,1)S(1)} %get-tuple-element.94.refs_0_), channel_id=1, source_target_pairs={{0,1},{1,0},{2,3},{3,2},{4,5},{5,4},{6,7},{7,6},{8,9},{9,8},{10,11... | collective-permute-start | bytes 393224 | tf_op jit(solution)/shard_map/ppermute | solution.py:396
  46.8 8.9 %collective-permute-start.22 = (bf16[512,128]{1,0:T(8,128)(2,1)S(1)}, bf16[512,128]{1,0:T(8,128)(2,1)S(1)}, u32[]{:S(2)}, u32[]{:S(2)}) collective-permute-start(bf16[512,128]{1,0:T(8,128)(2,1)S(1)} %get-tuple-element.117), channel_id=1, source_target_pairs={{0,2},{1,3},{2,4},{3,5},{4,6},{5,7},{6,0},{7,1},{8,10},{9,11},{10,... | collective-permute-start | bytes 393224 | tf_op jit(solution)/shard_map/ppermute | solution.py:392
  46.9 8.8 %collective-permute-start.23 = (bf16[512,128]{1,0:T(8,128)(2,1)S(1)}, bf16[512,128]{1,0:T(8,128)(2,1)S(1)}, u32[]{:S(2)}, u32[]{:S(2)}) collective-permute-start(bf16[512,128]{1,0:T(8,128)(2,1)S(1)} %get-tuple-element.118), channel_id=1, source_target_pairs={{0,4},{1,5},{2,6},{3,7},{4,0},{5,1},{6,2},{7,3},{8,12},{9,13},{10,... | collective-permute-start | bytes 393224 | tf_op jit(solution)/shard_map/ppermute | solution.py:392
  48.4 7.6 %collective-permute-start.24 = (bf16[512,128]{1,0:T(8,128)(2,1)S(1)}, bf16[512,128]{1,0:T(8,128)(2,1)S(1)}, u32[]{:S(2)}, u32[]{:S(2)}) collective-permute-start(bf16[512,128]{1,0:T(8,128)(2,1)S(1)} %get-tuple-element.119), channel_id=1, source_target_pairs={{0,6},{1,7},{2,0},{3,1},{4,2},{5,3},{6,4},{7,5},{8,14},{9,15},{10,... | collective-permute-start | bytes 393224 | tf_op jit(solution)/shard_map/ppermute | solution.py:392
  61.6 7.7 %collective-permute-start.30 = (bf16[832,128]{1,0:T(8,128)(2,1)S(1)}, bf16[832,128]{1,0:T(8,128)(2,1)S(1)}, u32[]{:S(2)}, u32[]{:S(2)}) collective-permute-start(bf16[832,128]{1,0:T(8,128)(2,1)S(1)} %get-tuple-element.134), channel_id=1, source_target_pairs={{0,2},{1,3},{2,4},{3,5},{4,6},{5,7},{6,0},{7,1},{8,10},{9,11},{10,... | collective-permute-start | bytes 638984 | tf_op jit(solution)/shard_map/ppermute | solution.py:392
  61.7 12.8 %collective-permute-start.31 = (bf16[832,128]{1,0:T(8,128)(2,1)S(1)}, bf16[832,128]{1,0:T(8,128)(2,1)S(1)}, u32[]{:S(2)}, u32[]{:S(2)}) collective-permute-start(bf16[832,128]{1,0:T(8,128)(2,1)S(1)} %get-tuple-element.135), channel_id=1, source_target_pairs={{0,4},{1,5},{2,6},{3,7},{4,0},{5,1},{6,2},{7,3},{8,12},{9,13},{10,... | collective-permute-start | bytes 638984 | tf_op jit(solution)/shard_map/ppermute | solution.py:392
  65.0 9.6 %collective-permute-start.32 = (bf16[832,128]{1,0:T(8,128)(2,1)S(1)}, bf16[832,128]{1,0:T(8,128)(2,1)S(1)}, u32[]{:S(2)}, u32[]{:S(2)}) collective-permute-start(bf16[832,128]{1,0:T(8,128)(2,1)S(1)} %get-tuple-element.136), channel_id=1, source_target_pairs={{0,6},{1,7},{2,0},{3,1},{4,2},{5,3},{6,4},{7,5},{8,14},{9,15},{10,... | collective-permute-start | bytes 638984 | tf_op jit(solution)/shard_map/ppermute | solution.py:392
  76.9 6.8 %collective-permute-start.34 = (bf16[400,128]{1,0:T(8,128)(2,1)S(1)}, bf16[400,128]{1,0:T(8,128)(2,1)S(1)}, u32[]{:S(2)}, u32[]{:S(2)}) collective-permute-start(bf16[400,128]{1,0:T(8,128)(2,1)S(1)} %get-tuple-element.146), channel_id=1, source_target_pairs={{0,64},{1,17},{2,66},{3,19},{4,68},{5,21},{6,70},{7,23},{8,72},{9,... | collective-permute-start | bytes 307208 | tf_op jit(solution)/shard_map/ppermute | solution.py:409
  81.0 8.2 %collective-permute-start.27 = (bf16[64,512]{1,0:T(8,128)(2,1)S(1)}, bf16[64,512]{1,0:T(8,128)(2,1)S(1)}, u32[]{:S(2)}, u32[]{:S(2)}) collective-permute-start(bf16[64,512]{1,0:T(8,128)(2,1)S(1)} %get-tuple-element.129), channel_id=1, source_target_pairs={{0,2},{1,3},{2,4},{3,5},{4,6},{5,7},{6,0},{7,1},{8,10},{9,11},{10,... | collective-permute-start | bytes 196616 | tf_op jit(solution)/shard_map/ppermute | solution.py:392
  84.2 9.4 %collective-permute-start.38 = (bf16[400,128]{1,0:T(8,128)(2,1)S(1)}, bf16[400,128]{1,0:T(8,128)(2,1)S(1)}, u32[]{:S(2)}, u32[]{:S(2)}) collective-permute-start(bf16[400,128]{1,0:T(8,128)(2,1)S(1)} %shard_map.182.a), channel_id=1, source_target_pairs={{0,24},{1,97},{2,26},{3,99},{4,28},{5,101},{6,30},{7,103},{8,0},{9... | collective-permute-start | bytes 307208 | tf_op jit(solution)/shard_map/ppermute | solution.py:409
  102.3 11.5 %collective-permute-start.44 = (bf16[1600,128]{1,0:T(8,128)(2,1)S(1)}, bf16[1600,128]{1,0:T(8,128)(2,1)S(1)}, u32[]{:S(2)}, u32[]{:S(2)}) collective-permute-start(bf16[1600,128]{1,0:T(8,128)(2,1)S(1)} %shard_map.185.refs_0_), channel_id=1, source_target_pairs={{0,6},{1,25},{2,0},{3,27},{4,2},{5,29},{6,4},{7,31},{8,14},{9,1},{... | collective-permute-start | bytes 1228808 | tf_op jit(solution)/shard_map/ppermute | solution.py:409
  104.5 15.5 %collective-permute-start.43 = (bf16[1600,128]{1,0:T(8,128)(2,1)S(1)}, bf16[1600,128]{1,0:T(8,128)(2,1)S(1)}, u32[]{:S(2)}, u32[]{:S(2)}) collective-permute-start(bf16[1600,128]{1,0:T(8,128)(2,1)S(1)} %shard_map.185.refs_0_), channel_id=1, source_target_pairs={{0,4},{1,17},{2,6},{3,19},{4,0},{5,21},{6,2},{7,23},{8,12},{9,25},... | collective-permute-start | bytes 1228808 | tf_op jit(solution)/shard_map/ppermute | solution.py:409
  104.8 15.3 %collective-permute-start.42 = (bf16[1600,128]{1,0:T(8,128)(2,1)S(1)}, bf16[1600,128]{1,0:T(8,128)(2,1)S(1)}, u32[]{:S(2)}, u32[]{:S(2)}) collective-permute-start(bf16[1600,128]{1,0:T(8,128)(2,1)S(1)} %shard_map.185.refs_0_), channel_id=1, source_target_pairs={{0,2},{1,9},{2,4},{3,11},{4,6},{5,13},{6,0},{7,15},{8,10},{9,17},{... | collective-permute-start | bytes 1228808 | tf_op jit(solution)/shard_map/ppermute | solution.py:409
  105.2 18.8 %collective-permute-start.45 = (bf16[1600,128]{1,0:T(8,128)(2,1)S(1)}, bf16[1600,128]{1,0:T(8,128)(2,1)S(1)}, u32[]{:S(2)}, u32[]{:S(2)}) collective-permute-start(bf16[1600,128]{1,0:T(8,128)(2,1)S(1)} %shard_map.185.refs_0_), channel_id=1, source_target_pairs={{0,1},{1,0},{2,3},{3,2},{4,5},{5,4},{6,7},{7,6},{8,9},{9,8},{10,11... | collective-permute-start | bytes 1228808 | tf_op jit(solution)/shard_map/ppermute | solution.py:396
  113.8 10.2 %collective-permute-start.48 = (bf16[1600,128]{1,0:T(8,128)(2,1)S(1)}, bf16[1600,128]{1,0:T(8,128)(2,1)S(1)}, u32[]{:S(2)}, u32[]{:S(2)}) collective-permute-start(bf16[1600,128]{1,0:T(8,128)(2,1)S(1)} %collective-permute-done.44.refs_3_), channel_id=1, source_target_pairs={{0,1},{1,0},{2,3},{3,2},{4,5},{5,4},{6,7},{7,6},{8,9},{9,8},{10,11... | collective-permute-start | bytes 1228808 | tf_op jit(solution)/shard_map/ppermute | solution.py:396
  (30 other events, 180.9 us)

commit v4 on v3

--- a/solution.py
+++ b/solution.py
@@ -445,7 +445,7 @@
 
     t = [down] + [over_x(down, k) for k in near]
     u = [over_core(down)]
-    t[1], t[2], t[3], p[1], p[2], p[3] = tie(*t[1:], *p[1:])
+    t[2], t[3], p[1], p[2], p[3] = tie(*t[2:], *p[1:])
     q = [over_core(v) for v in p]
     u += [over_core(v) for v in t[1:]]
     keep, send, outer, summed, dzed, d_outer, all_grad = call(

time: 129 us -> 129 us (level)
  waiting for transfers between devices: 39.7 us -> 36.9 us
  starting transfers between devices: 61.2 us -> 63.5 us
    ppermute x18, waiting for transfers between devices: 24.3 us -> 21.1 us  [over_x(): return lax.ppermute(value, 'graph', perm)]
    ppermute x19, starting transfers between devices: 25.3 us -> 27.8 us  [over_core(): return lax.ppermute(value, 'graph', [(i, i ^ 1) for i in range(8)])]
  transfers between devices with their start and end apart: 49 -> 49, of which waited for: 22 -> 20; matrix products, arithmetic and copies ran while one was open for 0% -> 0% of each run, Pallas kernels for 9% -> 9%
where the time goes in v4:
time: 129 us
  starting transfers between devices  63.5 us (49%)
  waiting for transfers between devices  36.9 us (29%)
  Pallas kernels  26.6 us (21%)
  between operations  1.69 us (1%)
    ppermute x19, starting transfers between devices, over_core(): return lax.ppermute(value, 'graph', [(i, i ^ 1) for i in range(8)])  27.8 us
    pallas_call x15, Pallas kernels, call(): pl.pallas_call(placed if here else body, out_shape=[pltpu.HBM(o.shape, o....  26.6 us
    ppermute x18, waiting for transfers between devices, over_x(): return lax.ppermute(value, 'graph', perm)  21.1 us
    ppermute x18, starting transfers between devices, over_x(): return lax.ppermute(value, 'graph', perm)  20.2 us
    ppermute x12, starting transfers between devices, over_dp(): return lax.ppermute(value, ('dp', 'graph'), perm)  15.4 us
    ppermute x12, waiting for transfers between devices, over_dp(): return lax.ppermute(value, ('dp', 'graph'), perm)  9.44 us
    ppermute x19, waiting for transfers between devices, over_core(): return lax.ppermute(value, 'graph', [(i, i ^ 1) for i in range(8)])  6.38 us
  transfers between devices with their start and end apart: 49, of which 20 were waited for; matrix products, arithmetic and copies ran while one was open for 0% of the time, Pallas kernels for 9%

profile of v4, /device:TPU:1, one launch (start us, length us, event | category | flops | bytes accessed | tf_op | source)
XLA Modules:
  0.0 128.7 jit_solution(13661198152373077714)
XLA Ops:
  0.7 3.4 %collective-permute-start.2 = (bf16[64,1024]{1,0:T(8,128)(2,1)}, bf16[64,1024]{1,0:T(8,128)(2,1)S(1)}, u32[]{:S(2)}, u32[]{:S(2)}) collective-permute-start(bf16[64,1024]{1,0:T(8,128)(2,1)} %bitcast.11), channel_id=1, source_target_pairs={{0,6},{1,7},{2,0},{3,1},{4,2},{5,3},{6,4},{7,5},{8,14},{9,15},{10,... | collective-permute-start | bytes 393224 | tf_op jit(solution)/shard_map/ppermute | solution.py:392
  7.3 5.3 %shard_map.172 = (bf16[1024,1024]{1,0:T(8,128)(2,1)S(1)}, bf16[1024,1024]{1,0:T(8,128)(2,1)S(1)}, bf16[2048,1024]{1,0:T(8,128)(2,1)S(1)}, bf16[1024,2048]{1,0:T(...) custom-call(s32[1,1]{1,0:T(1,128)S(6)} %copy.19.cnt, ...), custom_call_target="tpu_custom_call" | custom-call | flops 1 | bytes 1 | tf_op jit(solution)/shard_map/pallas_call | solution.py:42
  16.8 3.2 %shard_map.173 = (bf16[512,128]{1,0:T(8,128)(2,1)S(1)}, bf16[1024,512]{1,0:T(8,128)(2,1)S(1)}, bf16[1024,512]{1,0:T(8,128)(2,1)S(1)}, bf16[512,1024]{1,0:T(8,128)(2,1)S(1)}) custom-call(bf16[64,1024]{1,0:T(8,128)(2,1)S(1)} %bitcast.15, bf16[64,1024]{1,0:T(8,128)(2,1)S(1)} %collective-permute-done.refs_1_, ...), custom_call_target="tpu_custom_call" | custom-call | flops 1 | bytes 1 | tf_op jit(solution)/shard_map/pallas_call | solution.py:42
  20.0 2.7 %collective-permute-start.9 = (bf16[512,128]{1,0:T(8,128)(2,1)S(1)}, bf16[512,128]{1,0:T(8,128)(2,1)S(1)}, u32[]{:S(2)}, u32[]{:S(2)}) collective-permute-start(bf16[512,128]{1,0:T(8,128)(2,1)S(1)} %get-tuple-element.93.refs_0_), channel_id=1, source_target_pairs={{0,6},{1,7},{2,0},{3,1},{4,2},{5,3},{6,4},{7,5},{8,14},{9,15},{10,... | collective-permute-start | bytes 393224 | tf_op jit(solution)/shard_map/ppermute | solution.py:392
  25.7 2.3 %collective-permute-done.8.refs_2_ = bf16[512,128]{1,0:T(8,128)(2,1)S(1)} collective-permute-done((bf16[512,128]{1,0:T(8,128)(2,1)S(1)}, bf16[512,128]{1,0:T(8,128)(2,1)S(1)}, u32[]{:S(2)}, u32[]{:S(2)}) %collective-permute-start.8) | collective-permute-done | bytes 131104 | tf_op jit(solution)/shard_map/ppermute | solution.py:392
  28.0 4.1 %collective-permute-start.15 = (bf16[512,128]{1,0:T(8,128)(2,1)S(1)}, bf16[512,128]{1,0:T(8,128)(2,1)S(1)}, u32[]{:S(2)}, u32[]{:S(2)}) collective-permute-start(bf16[512,128]{1,0:T(8,128)(2,1)S(1)} %collective-permute-done.8.refs_2_), channel_id=1, source_target_pairs={{0,1},{1,0},{2,3},{3,2},{4,5},{5,4},{6,7},{7,6},{8,9},{9,8},{10,11... | collective-permute-start | bytes 393224 | tf_op jit(solution)/shard_map/ppermute | solution.py:396
  34.9 9.3 %shard_map.174 = (f32[512,512]{1,0:T(8,128)S(1)}, bf16[512,512]{1,0:T(8,128)(2,1)S(1)}, bf16[1024,512]{1,0:T(8,128)(2,1)S(1)}, bf16[512,128]{1,0:T(8,128)(2,1)S(...) custom-call(bf16[512,128]{1,0:T(8,128)(2,1)S(1)} %get-tuple-element.93.refs_0_, ...), custom_call_target="tpu_custom_call" | custom-call | flops 1 | bytes 1 | tf_op jit(solution)/shard_map/pallas_call | solution.py:42
  50.2 5.2 %collective-permute-done.22.refs_1_ = bf16[512,128]{1,0:T(8,128)(2,1)S(1)} collective-permute-done((bf16[512,128]{1,0:T(8,128)(2,1)S(1)}, bf16[512,128]{1,0:T(8,128)(2,1)S(1)}, u32[]{:S(2)}, u32[]{:S(2)}) %collective-permute-start.22) | collective-permute-done | bytes 131104 | tf_op jit(solution)/shard_map/ppermute | solution.py:392
  59.0 1.9 %collective-permute-done.25.refs_1_ = bf16[832,512]{1,0:T(8,128)(2,1)S(1)} collective-permute-done((bf16[832,512]{1,0:T(8,128)(2,1)S(1)}, bf16[832,512]{1,0:T(8,128)(2,1)S(1)}, u32[]{:S(2)}, u32[]{:S(2)}) %collective-permute-start.25) | collective-permute-done | bytes 852000 | tf_op jit(solution)/shard_map/ppermute | solution.py:396
  61.4 3.3 %collective-permute-start.31 = (bf16[832,128]{1,0:T(8,128)(2,1)S(1)}, bf16[832,128]{1,0:T(8,128)(2,1)S(1)}, u32[]{:S(2)}, u32[]{:S(2)}) collective-permute-start(bf16[832,128]{1,0:T(8,128)(2,1)S(1)} %get-tuple-element.133), channel_id=1, source_target_pairs={{0,4},{1,5},{2,6},{3,7},{4,0},{5,1},{6,2},{7,3},{8,12},{9,13},{10,... | collective-permute-start | bytes 638984 | tf_op jit(solution)/shard_map/ppermute | solution.py:392
  65.0 3.9 %collective-permute-done.30.refs_1_ = bf16[832,128]{1,0:T(8,128)(2,1)S(1)} collective-permute-done((bf16[832,128]{1,0:T(8,128)(2,1)S(1)}, bf16[832,128]{1,0:T(8,128)(2,1)S(1)}, u32[]{:S(2)}, u32[]{:S(2)}) %collective-permute-start.30) | collective-permute-done | bytes 213024 | tf_op jit(solution)/shard_map/ppermute | solution.py:392
  68.9 5.3 %collective-permute-done.31.refs_2_ = bf16[832,128]{1,0:T(8,128)(2,1)S(1)} collective-permute-done((bf16[832,128]{1,0:T(8,128)(2,1)S(1)}, bf16[832,128]{1,0:T(8,128)(2,1)S(1)}, u32[]{:S(2)}, u32[]{:S(2)}) %collective-permute-start.31) | collective-permute-done | bytes 213024 | tf_op jit(solution)/shard_map/ppermute | solution.py:392
  76.5 3.3 %collective-permute-start.34 = (bf16[400,128]{1,0:T(8,128)(2,1)S(1)}, bf16[400,128]{1,0:T(8,128)(2,1)S(1)}, u32[]{:S(2)}, u32[]{:S(2)}) collective-permute-start(bf16[400,128]{1,0:T(8,128)(2,1)S(1)} %get-tuple-element.144), channel_id=1, source_target_pairs={{0,64},{1,17},{2,66},{3,19},{4,68},{5,21},{6,70},{7,23},{8,72},{9,... | collective-permute-start | bytes 307208 | tf_op jit(solution)/shard_map/ppermute | solution.py:409
  81.3 1.9 %collective-permute-done.34.c = bf16[400,128]{1,0:T(8,128)(2,1)S(1)} collective-permute-done((bf16[400,128]{1,0:T(8,128)(2,1)S(1)}, bf16[400,128]{1,0:T(8,128)(2,1)S(1)}, u32[]{:S(2)}, u32[]{:S(2)}) %collective-permute-start.34) | collective-permute-done | bytes 102432 | tf_op jit(solution)/shard_map/ppermute | solution.py:409
  83.7 2.8 %collective-permute-start.38 = (bf16[400,128]{1,0:T(8,128)(2,1)S(1)}, bf16[400,128]{1,0:T(8,128)(2,1)S(1)}, u32[]{:S(2)}, u32[]{:S(2)}) collective-permute-start(bf16[400,128]{1,0:T(8,128)(2,1)S(1)} %shard_map.182.a), channel_id=1, source_target_pairs={{0,24},{1,97},{2,26},{3,99},{4,28},{5,101},{6,30},{7,103},{8,0},{9... | collective-permute-start | bytes 307208 | tf_op jit(solution)/shard_map/ppermute | solution.py:409
  90.3 1.8 %collective-permute-done.28.r2 = bf16[64,512]{1,0:T(8,128)(2,1)S(1)} collective-permute-done((bf16[64,512]{1,0:T(8,128)(2,1)S(1)}, bf16[64,512]{1,0:T(8,128)(2,1)S(1)}, u32[]{:S(2)}, u32[]{:S(2)}) %collective-permute-start.28) | collective-permute-done | bytes 65568 | tf_op jit(solution)/shard_map/ppermute | solution.py:392
  93.3 2.5 %collective-permute-start.41 = (bf16[400,128]{1,0:T(8,128)(2,1)S(1)}, bf16[400,128]{1,0:T(8,128)(2,1)S(1)}, u32[]{:S(2)}, u32[]{:S(2)}) collective-permute-start(bf16[400,128]{1,0:T(8,128)(2,1)S(1)} %shard_map.184.refs_0_), channel_id=1, source_target_pairs={{0,96},{1,7},{2,98},{3,1},{4,100},{5,3},{6,102},{7,5},{8,104},{9,1... | collective-permute-start | bytes 307208 | tf_op jit(solution)/shard_map/ppermute | solution.py:409
  98.5 2.4 %collective-permute-done.40.refs_2_ = bf16[400,128]{1,0:T(8,128)(2,1)S(1)} collective-permute-done((bf16[400,128]{1,0:T(8,128)(2,1)S(1)}, bf16[400,128]{1,0:T(8,128)(2,1)S(1)}, u32[]{:S(2)}, u32[]{:S(2)}) %collective-permute-start.40) | collective-permute-done | bytes 102432 | tf_op jit(solution)/shard_map/ppermute | solution.py:409
  101.9 2.1 %collective-permute-start.44 = (bf16[1600,128]{1,0:T(8,128)(2,1)S(1)}, bf16[1600,128]{1,0:T(8,128)(2,1)S(1)}, u32[]{:S(2)}, u32[]{:S(2)}) collective-permute-start(bf16[1600,128]{1,0:T(8,128)(2,1)S(1)} %shard_map.185.refs_0_), channel_id=1, source_target_pairs={{0,6},{1,25},{2,0},{3,27},{4,2},{5,29},{6,4},{7,31},{8,14},{9,1},{... | collective-permute-start | bytes 1228808 | tf_op jit(solution)/shard_map/ppermute | solution.py:409
  104.8 6.0 %collective-permute-start.45 = (bf16[1600,128]{1,0:T(8,128)(2,1)S(1)}, bf16[1600,128]{1,0:T(8,128)(2,1)S(1)}, u32[]{:S(2)}, u32[]{:S(2)}) collective-permute-start(bf16[1600,128]{1,0:T(8,128)(2,1)S(1)} %shard_map.185.refs_0_), channel_id=1, source_target_pairs={{0,1},{1,0},{2,3},{3,2},{4,5},{5,4},{6,7},{7,6},{8,9},{9,8},{10,11... | collective-permute-start | bytes 1228808 | tf_op jit(solution)/shard_map/ppermute | solution.py:396
  110.7 2.7 %collective-permute-done.44.refs_3_ = bf16[1600,128]{1,0:T(8,128)(2,1)S(1)} collective-permute-done((bf16[1600,128]{1,0:T(8,128)(2,1)S(1)}, bf16[1600,128]{1,0:T(8,128)(2,1)S(1)}, u32[]{:S(2)}, u32[]{:S(2)}) %collective-permute-start.44) | collective-permute-done | bytes 409632 | tf_op jit(solution)/shard_map/ppermute | solution.py:409
  113.4 6.3 %collective-permute-start.48 = (bf16[1600,128]{1,0:T(8,128)(2,1)S(1)}, bf16[1600,128]{1,0:T(8,128)(2,1)S(1)}, u32[]{:S(2)}, u32[]{:S(2)}) collective-permute-start(bf16[1600,128]{1,0:T(8,128)(2,1)S(1)} %collective-permute-done.44.refs_3_), channel_id=1, source_target_pairs={{0,1},{1,0},{2,3},{3,2},{4,5},{5,4},{6,7},{7,6},{8,9},{9,8},{10,11... | collective-permute-start | bytes 1228808 | tf_op jit(solution)/shard_map/ppermute | solution.py:396
  119.7 3.9 %collective-permute-start.46 = (bf16[1600,128]{1,0:T(8,128)(2,1)S(1)}, bf16[1600,128]{1,0:T(8,128)(2,1)S(1)}, u32[]{:S(2)}, u32[]{:S(2)}) collective-permute-start(bf16[1600,128]{1,0:T(8,128)(2,1)S(1)} %collective-permute-done.42.refs_1_), channel_id=1, source_target_pairs={{0,1},{1,0},{2,3},{3,2},{4,5},{5,4},{6,7},{7,6},{8,9},{9,8},{10,11... | collective-permute-start | bytes 1228808 | tf_op jit(solution)/shard_map/ppermute | solution.py:396
  125.0 3.5 %shard_map.186 = (f32[64,512]{1,0:T(8,128)}, f32[64,512]{1,0:T(8,128)}, f32[2048,512]{1,0:T(8,128)}, f32[8,64,1024]{2,1,0:T(8,128)}) custom-call(bf16[1600,128]{1,0:T(8,128)(2,1)S(1)} %shard_map.185.refs_0_, bf16[1600,128]{1,0:T(8,128)(2,1)S(1)} %collective-permute-done.42.refs_1_, bf16[1600,128]{1,0:T(8,128)(2,1)S(1)} %collective-permute-done.43.refs_2_, ...), custom_call_target="tpu_custom_call" | custom-call | flops 1 | bytes 1 | tf_op jit(solution)/shard_map/pallas_call | solution.py:42
  (99 shorter events, 37.8 us)
Async XLA Ops:
  0.7 12.0 %collective-permute-start.2 = (bf16[64,1024]{1,0:T(8,128)(2,1)}, bf16[64,1024]{1,0:T(8,128)(2,1)S(1)}, u32[]{:S(2)}, u32[]{:S(2)}) collective-permute-start(bf16[64,1024]{1,0:T(8,128)(2,1)} %bitcast.11), channel_id=1, source_target_pairs={{0,6},{1,7},{2,0},{3,1},{4,2},{5,3},{6,4},{7,5},{8,14},{9,15},{10,... | collective-permute-start | bytes 393224 | tf_op jit(solution)/shard_map/ppermute | solution.py:392
  4.0 8.7 %collective-permute-start.1 = (bf16[64,1024]{1,0:T(8,128)(2,1)}, bf16[64,1024]{1,0:T(8,128)(2,1)S(1)}, u32[]{:S(2)}, u32[]{:S(2)}) collective-permute-start(bf16[64,1024]{1,0:T(8,128)(2,1)} %bitcast.12), channel_id=1, source_target_pairs={{0,4},{1,5},{2,6},{3,7},{4,0},{5,1},{6,2},{7,3},{8,12},{9,13},{10,... | collective-permute-start | bytes 393224 | tf_op jit(solution)/shard_map/ppermute | solution.py:392
  4.6 9.2 %collective-permute-start = (bf16[64,1024]{1,0:T(8,128)(2,1)}, bf16[64,1024]{1,0:T(8,128)(2,1)S(1)}, u32[]{:S(2)}, u32[]{:S(2)}) collective-permute-start(bf16[64,1024]{1,0:T(8,128)(2,1)} %bitcast.13), channel_id=1, source_target_pairs={{0,2},{1,3},{2,4},{3,5},{4,6},{5,7},{6,0},{7,1},{8,10},{9,11},{10,... | collective-permute-start | bytes 393224 | tf_op jit(solution)/shard_map/ppermute | solution.py:392
  5.2 10.3 %collective-permute-start.3 = (bf16[64,1024]{1,0:T(8,128)(2,1)}, bf16[64,1024]{1,0:T(8,128)(2,1)S(1)}, u32[]{:S(2)}, u32[]{:S(2)}) collective-permute-start(bf16[64,1024]{1,0:T(8,128)(2,1)} %bitcast.14), channel_id=1, source_target_pairs={{0,1},{1,0},{2,3},{3,2},{4,5},{5,4},{6,7},{7,6},{8,9},{9,8},{10,11... | collective-permute-start | bytes 393224 | tf_op jit(solution)/shard_map/ppermute | solution.py:396
  15.0 8.4 %collective-permute-start.12 = (bf16[64,1024]{1,0:T(8,128)(2,1)S(1)}, bf16[64,1024]{1,0:T(8,128)(2,1)S(1)}, u32[]{:S(2)}, u32[]{:S(2)}) collective-permute-start(bf16[64,1024]{1,0:T(8,128)(2,1)S(1)} %bitcast.19), channel_id=1, source_target_pairs={{0,6},{1,7},{2,0},{3,1},{4,2},{5,3},{6,4},{7,5},{8,14},{9,15},{10,... | collective-permute-start | bytes 393224 | tf_op jit(solution)/shard_map/ppermute | solution.py:392
  15.5 9.6 %collective-permute-start.11 = (bf16[64,1024]{1,0:T(8,128)(2,1)S(1)}, bf16[64,1024]{1,0:T(8,128)(2,1)S(1)}, u32[]{:S(2)}, u32[]{:S(2)}) collective-permute-start(bf16[64,1024]{1,0:T(8,128)(2,1)S(1)} %bitcast.20), channel_id=1, source_target_pairs={{0,4},{1,5},{2,6},{3,7},{4,0},{5,1},{6,2},{7,3},{8,12},{9,13},{10,... | collective-permute-start | bytes 393224 | tf_op jit(solution)/shard_map/ppermute | solution.py:392
  16.7 8.4 %collective-permute-start.10 = (bf16[64,1024]{1,0:T(8,128)(2,1)S(1)}, bf16[64,1024]{1,0:T(8,128)(2,1)S(1)}, u32[]{:S(2)}, u32[]{:S(2)}) collective-permute-start(bf16[64,1024]{1,0:T(8,128)(2,1)S(1)} %bitcast.21), channel_id=1, source_target_pairs={{0,2},{1,3},{2,4},{3,5},{4,6},{5,7},{6,0},{7,1},{8,10},{9,11},{10,... | collective-permute-start | bytes 393224 | tf_op jit(solution)/shard_map/ppermute | solution.py:392
  23.4 8.7 %collective-permute-start.17 = (bf16[64,1024]{1,0:T(8,128)(2,1)S(1)}, bf16[64,1024]{1,0:T(8,128)(2,1)S(1)}, u32[]{:S(2)}, u32[]{:S(2)}) collective-permute-start(bf16[64,1024]{1,0:T(8,128)(2,1)S(1)} %bitcast.22), channel_id=1, source_target_pairs={{0,1},{1,0},{2,3},{3,2},{4,5},{5,4},{6,7},{7,6},{8,9},{9,8},{10,11... | collective-permute-start | bytes 393224 | tf_op jit(solution)/shard_map/ppermute | solution.py:396
  25.0 7.6 %collective-permute-start.13 = (bf16[512,128]{1,0:T(8,128)(2,1)S(1)}, bf16[512,128]{1,0:T(8,128)(2,1)S(1)}, u32[]{:S(2)}, u32[]{:S(2)}) collective-permute-start(bf16[512,128]{1,0:T(8,128)(2,1)S(1)} %get-tuple-element.93.refs_0_), channel_id=1, source_target_pairs={{0,1},{1,0},{2,3},{3,2},{4,5},{5,4},{6,7},{7,6},{8,9},{9,8},{10,11... | collective-permute-start | bytes 393224 | tf_op jit(solution)/shard_map/ppermute | solution.py:396
  25.1 7.6 %collective-permute-start.7 = (bf16[512,128]{1,0:T(8,128)(2,1)S(1)}, bf16[512,128]{1,0:T(8,128)(2,1)S(1)}, u32[]{:S(2)}, u32[]{:S(2)}) collective-permute-start(bf16[512,128]{1,0:T(8,128)(2,1)S(1)} %get-tuple-element.93.refs_0_), channel_id=1, source_target_pairs={{0,2},{1,3},{2,4},{3,5},{4,6},{5,7},{6,0},{7,1},{8,10},{9,11},{10,... | collective-permute-start | bytes 393224 | tf_op jit(solution)/shard_map/ppermute | solution.py:392
  46.4 9.0 %collective-permute-start.22 = (bf16[512,128]{1,0:T(8,128)(2,1)S(1)}, bf16[512,128]{1,0:T(8,128)(2,1)S(1)}, u32[]{:S(2)}, u32[]{:S(2)}) collective-permute-start(bf16[512,128]{1,0:T(8,128)(2,1)S(1)} %get-tuple-element.115), channel_id=1, source_target_pairs={{0,2},{1,3},{2,4},{3,5},{4,6},{5,7},{6,0},{7,1},{8,10},{9,11},{10,... | collective-permute-start | bytes 393224 | tf_op jit(solution)/shard_map/ppermute | solution.py:392
  46.5 8.9 %collective-permute-start.23 = (bf16[512,128]{1,0:T(8,128)(2,1)S(1)}, bf16[512,128]{1,0:T(8,128)(2,1)S(1)}, u32[]{:S(2)}, u32[]{:S(2)}) collective-permute-start(bf16[512,128]{1,0:T(8,128)(2,1)S(1)} %get-tuple-element.116), channel_id=1, source_target_pairs={{0,4},{1,5},{2,6},{3,7},{4,0},{5,1},{6,2},{7,3},{8,12},{9,13},{10,... | collective-permute-start | bytes 393224 | tf_op jit(solution)/shard_map/ppermute | solution.py:392
  47.9 7.9 %collective-permute-start.24 = (bf16[512,128]{1,0:T(8,128)(2,1)S(1)}, bf16[512,128]{1,0:T(8,128)(2,1)S(1)}, u32[]{:S(2)}, u32[]{:S(2)}) collective-permute-start(bf16[512,128]{1,0:T(8,128)(2,1)S(1)} %get-tuple-element.117), channel_id=1, source_target_pairs={{0,6},{1,7},{2,0},{3,1},{4,2},{5,3},{6,4},{7,5},{8,14},{9,15},{10,... | collective-permute-start | bytes 393224 | tf_op jit(solution)/shard_map/ppermute | solution.py:392
  61.2 7.7 %collective-permute-start.30 = (bf16[832,128]{1,0:T(8,128)(2,1)S(1)}, bf16[832,128]{1,0:T(8,128)(2,1)S(1)}, u32[]{:S(2)}, u32[]{:S(2)}) collective-permute-start(bf16[832,128]{1,0:T(8,128)(2,1)S(1)} %get-tuple-element.132), channel_id=1, source_target_pairs={{0,2},{1,3},{2,4},{3,5},{4,6},{5,7},{6,0},{7,1},{8,10},{9,11},{10,... | collective-permute-start | bytes 638984 | tf_op jit(solution)/shard_map/ppermute | solution.py:392
  61.4 12.8 %collective-permute-start.31 = (bf16[832,128]{1,0:T(8,128)(2,1)S(1)}, bf16[832,128]{1,0:T(8,128)(2,1)S(1)}, u32[]{:S(2)}, u32[]{:S(2)}) collective-permute-start(bf16[832,128]{1,0:T(8,128)(2,1)S(1)} %get-tuple-element.133), channel_id=1, source_target_pairs={{0,4},{1,5},{2,6},{3,7},{4,0},{5,1},{6,2},{7,3},{8,12},{9,13},{10,... | collective-permute-start | bytes 638984 | tf_op jit(solution)/shard_map/ppermute | solution.py:392
  64.7 9.6 %collective-permute-start.32 = (bf16[832,128]{1,0:T(8,128)(2,1)S(1)}, bf16[832,128]{1,0:T(8,128)(2,1)S(1)}, u32[]{:S(2)}, u32[]{:S(2)}) collective-permute-start(bf16[832,128]{1,0:T(8,128)(2,1)S(1)} %get-tuple-element.134), channel_id=1, source_target_pairs={{0,6},{1,7},{2,0},{3,1},{4,2},{5,3},{6,4},{7,5},{8,14},{9,15},{10,... | collective-permute-start | bytes 638984 | tf_op jit(solution)/shard_map/ppermute | solution.py:392
  76.5 6.7 %collective-permute-start.34 = (bf16[400,128]{1,0:T(8,128)(2,1)S(1)}, bf16[400,128]{1,0:T(8,128)(2,1)S(1)}, u32[]{:S(2)}, u32[]{:S(2)}) collective-permute-start(bf16[400,128]{1,0:T(8,128)(2,1)S(1)} %get-tuple-element.144), channel_id=1, source_target_pairs={{0,64},{1,17},{2,66},{3,19},{4,68},{5,21},{6,70},{7,23},{8,72},{9,... | collective-permute-start | bytes 307208 | tf_op jit(solution)/shard_map/ppermute | solution.py:409
  80.6 8.2 %collective-permute-start.27 = (bf16[64,512]{1,0:T(8,128)(2,1)S(1)}, bf16[64,512]{1,0:T(8,128)(2,1)S(1)}, u32[]{:S(2)}, u32[]{:S(2)}) collective-permute-start(bf16[64,512]{1,0:T(8,128)(2,1)S(1)} %get-tuple-element.127), channel_id=1, source_target_pairs={{0,2},{1,3},{2,4},{3,5},{4,6},{5,7},{6,0},{7,1},{8,10},{9,11},{10,... | collective-permute-start | bytes 196616 | tf_op jit(solution)/shard_map/ppermute | solution.py:392
  83.7 9.5 %collective-permute-start.38 = (bf16[400,128]{1,0:T(8,128)(2,1)S(1)}, bf16[400,128]{1,0:T(8,128)(2,1)S(1)}, u32[]{:S(2)}, u32[]{:S(2)}) collective-permute-start(bf16[400,128]{1,0:T(8,128)(2,1)S(1)} %shard_map.182.a), channel_id=1, source_target_pairs={{0,24},{1,97},{2,26},{3,99},{4,28},{5,101},{6,30},{7,103},{8,0},{9... | collective-permute-start | bytes 307208 | tf_op jit(solution)/shard_map/ppermute | solution.py:409
  101.9 11.4 %collective-permute-start.44 = (bf16[1600,128]{1,0:T(8,128)(2,1)S(1)}, bf16[1600,128]{1,0:T(8,128)(2,1)S(1)}, u32[]{:S(2)}, u32[]{:S(2)}) collective-permute-start(bf16[1600,128]{1,0:T(8,128)(2,1)S(1)} %shard_map.185.refs_0_), channel_id=1, source_target_pairs={{0,6},{1,25},{2,0},{3,27},{4,2},{5,29},{6,4},{7,31},{8,14},{9,1},{... | collective-permute-start | bytes 1228808 | tf_op jit(solution)/shard_map/ppermute | solution.py:409
  104.1 15.6 %collective-permute-start.43 = (bf16[1600,128]{1,0:T(8,128)(2,1)S(1)}, bf16[1600,128]{1,0:T(8,128)(2,1)S(1)}, u32[]{:S(2)}, u32[]{:S(2)}) collective-permute-start(bf16[1600,128]{1,0:T(8,128)(2,1)S(1)} %shard_map.185.refs_0_), channel_id=1, source_target_pairs={{0,4},{1,17},{2,6},{3,19},{4,0},{5,21},{6,2},{7,23},{8,12},{9,25},... | collective-permute-start | bytes 1228808 | tf_op jit(solution)/shard_map/ppermute | solution.py:409
  104.4 15.3 %collective-permute-start.42 = (bf16[1600,128]{1,0:T(8,128)(2,1)S(1)}, bf16[1600,128]{1,0:T(8,128)(2,1)S(1)}, u32[]{:S(2)}, u32[]{:S(2)}) collective-permute-start(bf16[1600,128]{1,0:T(8,128)(2,1)S(1)} %shard_map.185.refs_0_), channel_id=1, source_target_pairs={{0,2},{1,9},{2,4},{3,11},{4,6},{5,13},{6,0},{7,15},{8,10},{9,17},{... | collective-permute-start | bytes 1228808 | tf_op jit(solution)/shard_map/ppermute | solution.py:409
  104.8 18.8 %collective-permute-start.45 = (bf16[1600,128]{1,0:T(8,128)(2,1)S(1)}, bf16[1600,128]{1,0:T(8,128)(2,1)S(1)}, u32[]{:S(2)}, u32[]{:S(2)}) collective-permute-start(bf16[1600,128]{1,0:T(8,128)(2,1)S(1)} %shard_map.185.refs_0_), channel_id=1, source_target_pairs={{0,1},{1,0},{2,3},{3,2},{4,5},{5,4},{6,7},{7,6},{8,9},{9,8},{10,11... | collective-permute-start | bytes 1228808 | tf_op jit(solution)/shard_map/ppermute | solution.py:396
  113.4 10.2 %collective-permute-start.48 = (bf16[1600,128]{1,0:T(8,128)(2,1)S(1)}, bf16[1600,128]{1,0:T(8,128)(2,1)S(1)}, u32[]{:S(2)}, u32[]{:S(2)}) collective-permute-start(bf16[1600,128]{1,0:T(8,128)(2,1)S(1)} %collective-permute-done.44.refs_3_), channel_id=1, source_target_pairs={{0,1},{1,0},{2,3},{3,2},{4,5},{5,4},{6,7},{7,6},{8,9},{9,8},{10,11... | collective-permute-start | bytes 1228808 | tf_op jit(solution)/shard_map/ppermute | solution.py:396
  (30 other events, 183.3 us)

commit v5 on v4

--- a/solution.py
+++ b/solution.py
@@ -271,7 +271,7 @@
 
 
 def k3_body(
-    xc, own, r1, r2, r3, d_outer, dsilu, inner, st, w_down_t, ot, gup, edge_grad, keep, send, d_pre
+    xc, own, r1, r2, r3, d_outer, dsilu, inner, st, w_down_t, ot, gup, send, d_pre, grads, gdown
 ):
     c = xc[1]
     dd = total4(own[...], r1[...], r2[...], r3[...]).astype(BF)
@@ -280,21 +280,30 @@
             rows = slice(256 * i, 256 * i + 256)
             ch = slice(512 * h + 256 * i, 512 * h + 256 * i + 256)
             d_inner = d_outer[ch, :].astype(F32) + dot(dd[rows, :], w)
-            edge_grad[ch, :] = d_inner.astype(BF)
+            grads[ch, :] = d_inner.astype(BF)
             d_pre[ch, :] = (d_inner * dsilu[ch, :].astype(F32)).astype(BF)
     for i in range(2):
         rows = slice(256 * i, 256 * i + 256)
         send[rows, :] = dot(st[at(2 * (1 - c) + i, 256), :], d_pre[...]).astype(BF)
-        keep[rows, :] = dot(st[at(2 * c + i, 256), :], d_pre[...])
     ddt = dd.T
     first, second = swapped(c, ddt[0:64, :], ddt[64:128, :])
-    gdown = dot(first, inner[0:512, :]) + dot(second, inner[512:1024, :])
-    keep[512:576, :] = jnp.where(c == 0, gup[...], gdown)
-    send[512:576, :] = jnp.where(c == 0, gdown, gup[...]).astype(BF)
+    gdown[...] = dot(first, inner[0:512, :]) + dot(second, inner[512:1024, :])
+    send[512:576, :] = jnp.where(c == 0, gdown[...], gup[...]).astype(BF)
+    for i in range(4):
+        rows = slice(576 + 64 * i, 640 + 64 * i)
+        send[rows, :] = ot[at(2 * i + 1 - c, 64), :]
+
+
+def k3_own_body(xc, st, d_pre, grads, gdown, ot, gup, edge_grad, keep):
+    c = xc[1]
+    edge_grad[...] = grads[...]
+    for i in range(2):
+        rows = slice(256 * i, 256 * i + 256)
+        keep[rows, :] = dot(st[at(2 * c + i, 256), :], d_pre[...])
+    keep[512:576, :] = jnp.where(c == 0, gup[...], gdown[...])
     for i in range(4):
         rows = slice(576 + 64 * i, 640 + 64 * i)
         keep[rows, :] = ot[at(2 * i + c, 64), :].astype(F32)
-        send[rows, :] = ot[at(2 * i + 1 - c, 64), :]
 
 
 def kb_body(xc, keep, recv, own, s1, s2, s3):
@@ -468,14 +477,17 @@
         [outer, st, summed, dzed], here="x", vmem=16,
     )
     o_recv = over_core(o_send)
-    edge_grad, keep, send = call(
+    send, d_pre, grads, gdown = call(
         k3_body,
-        [sds((1024, 512)), sds((832, 512), F32), sds((832, 512))],
-        [*dd, d_outer, dsilu, inner, st, w_down.T, ot, gup],
-        here="x", scratch=[pltpu.VMEM((1024, 512), BF)], vmem=16,
-    )
-
+        [sds((832, 512)), sds((1024, 512)), sds((1024, 512)), sds((64, 512), F32)],
+        [*dd, d_outer, dsilu, inner, st, w_down.T, ot, gup], here="x", vmem=16,
+    )
     recv = over_core(send)
+    edge_grad, keep = call(
+        k3_own_body,
+        [sds((1024, 512)), sds((832, 512), F32)],
+        [st, d_pre, grads, gdown, ot, gup], here="x", vmem=16,
+    )
     parts = call(kb_body, [sds((832, 128))] * 4, [keep, recv], here="x", vmem=12)
     recv, o_recv, all_nodes = tie(recv, o_recv, all_nodes)
     o_parts = call(kr_body, [sds((64, 512))] * 4, [o_keep, o_recv], here="x", vmem=8)

time: 129 us -> 128 us (level)
  waiting for transfers between devices: 36.9 us -> 35.3 us
    ppermute x19, waiting for transfers between devices: 6.38 us -> 4.8 us  [over_core(): return lax.ppermute(value, 'graph', [(i, i ^ 1) for i in range(8)])]
    pallas_call x15 -> x16, Pallas kernels: 26.6 us -> 27.6 us  [call(): pl.pallas_call(placed if here else body, out_shape=[pltpu.HBM(o.shape, o....]
  transfers between devices with their start and end apart: 49 -> 49, of which waited for: 20 -> 20; matrix products, arithmetic and copies ran while one was open for 0% -> 0% of each run, Pallas kernels for 9% -> 10%
where the time goes in v5:
time: 128 us
  starting transfers between devices  63.5 us (50%)
  waiting for transfers between devices  35.3 us (28%)
  Pallas kernels  27.6 us (22%)
  between operations  1.69 us (1%)
    ppermute x19, starting transfers between devices, over_core(): return lax.ppermute(value, 'graph', [(i, i ^ 1) for i in range(8)])  27.8 us
    pallas_call x16, Pallas kernels, call(): pl.pallas_call(placed if here else body, out_shape=[pltpu.HBM(o.shape, o....  27.6 us
    ppermute x18, waiting for transfers between devices, over_x(): return lax.ppermute(value, 'graph', perm)  21.1 us
    ppermute x18, starting transfers between devices, over_x(): return lax.ppermute(value, 'graph', perm)  20.2 us
    ppermute x12, starting transfers between devices, over_dp(): return lax.ppermute(value, ('dp', 'graph'), perm)  15.4 us
    ppermute x12, waiting for transfers between devices, over_dp(): return lax.ppermute(value, ('dp', 'graph'), perm)  9.43 us
    ppermute x19, waiting for transfers between devices, over_core(): return lax.ppermute(value, 'graph', [(i, i ^ 1) for i in range(8)])  4.8 us
  transfers between devices with their start and end apart: 49, of which 20 were waited for; matrix products, arithmetic and copies ran while one was open for 0% of the time, Pallas kernels for 10%

profile of v5, /device:TPU:1, one launch (start us, length us, event | category | flops | bytes accessed | tf_op | source)
XLA Modules:
  0.0 128.2 jit_solution(2978079676420644355)
XLA Ops:
  0.7 3.4 %collective-permute-start.2 = (bf16[64,1024]{1,0:T(8,128)(2,1)}, bf16[64,1024]{1,0:T(8,128)(2,1)S(1)}, u32[]{:S(2)}, u32[]{:S(2)}) collective-permute-start(bf16[64,1024]{1,0:T(8,128)(2,1)} %bitcast.11), channel_id=1, source_target_pairs={{0,6},{1,7},{2,0},{3,1},{4,2},{5,3},{6,4},{7,5},{8,14},{9,15},{10,... | collective-permute-start | bytes 393224 | tf_op jit(solution)/shard_map/ppermute | solution.py:401
  7.3 5.3 %shard_map.172 = (bf16[1024,1024]{1,0:T(8,128)(2,1)S(1)}, bf16[1024,1024]{1,0:T(8,128)(2,1)S(1)}, bf16[2048,1024]{1,0:T(8,128)(2,1)S(1)}, bf16[1024,2048]{1,0:T(...) custom-call(s32[1,1]{1,0:T(1,128)S(6)} %copy.19.cnt, ...), custom_call_target="tpu_custom_call" | custom-call | flops 1 | bytes 1 | tf_op jit(solution)/shard_map/pallas_call | solution.py:42
  16.8 3.2 %shard_map.173 = (bf16[512,128]{1,0:T(8,128)(2,1)S(1)}, bf16[1024,512]{1,0:T(8,128)(2,1)S(1)}, bf16[1024,512]{1,0:T(8,128)(2,1)S(1)}, bf16[512,1024]{1,0:T(8,128)(2,1)S(1)}) custom-call(bf16[64,1024]{1,0:T(8,128)(2,1)S(1)} %bitcast.15, bf16[64,1024]{1,0:T(8,128)(2,1)S(1)} %collective-permute-done.refs_1_, ...), custom_call_target="tpu_custom_call" | custom-call | flops 1 | bytes 1 | tf_op jit(solution)/shard_map/pallas_call | solution.py:42
  20.0 2.7 %collective-permute-start.9 = (bf16[512,128]{1,0:T(8,128)(2,1)S(1)}, bf16[512,128]{1,0:T(8,128)(2,1)S(1)}, u32[]{:S(2)}, u32[]{:S(2)}) collective-permute-start(bf16[512,128]{1,0:T(8,128)(2,1)S(1)} %get-tuple-element.96.refs_0_), channel_id=1, source_target_pairs={{0,6},{1,7},{2,0},{3,1},{4,2},{5,3},{6,4},{7,5},{8,14},{9,15},{10,... | collective-permute-start | bytes 393224 | tf_op jit(solution)/shard_map/ppermute | solution.py:401
  25.7 2.3 %collective-permute-done.8.refs_2_ = bf16[512,128]{1,0:T(8,128)(2,1)S(1)} collective-permute-done((bf16[512,128]{1,0:T(8,128)(2,1)S(1)}, bf16[512,128]{1,0:T(8,128)(2,1)S(1)}, u32[]{:S(2)}, u32[]{:S(2)}) %collective-permute-start.8) | collective-permute-done | bytes 131104 | tf_op jit(solution)/shard_map/ppermute | solution.py:401
  28.0 4.1 %collective-permute-start.15 = (bf16[512,128]{1,0:T(8,128)(2,1)S(1)}, bf16[512,128]{1,0:T(8,128)(2,1)S(1)}, u32[]{:S(2)}, u32[]{:S(2)}) collective-permute-start(bf16[512,128]{1,0:T(8,128)(2,1)S(1)} %collective-permute-done.8.refs_2_), channel_id=1, source_target_pairs={{0,1},{1,0},{2,3},{3,2},{4,5},{5,4},{6,7},{7,6},{8,9},{9,8},{10,11... | collective-permute-start | bytes 393224 | tf_op jit(solution)/shard_map/ppermute | solution.py:405
  34.9 9.3 %shard_map.174 = (f32[512,512]{1,0:T(8,128)S(1)}, bf16[512,512]{1,0:T(8,128)(2,1)S(1)}, bf16[1024,512]{1,0:T(8,128)(2,1)S(1)}, bf16[512,128]{1,0:T(8,128)(2,1)S(...) custom-call(bf16[512,128]{1,0:T(8,128)(2,1)S(1)} %get-tuple-element.96.refs_0_, ...), custom_call_target="tpu_custom_call" | custom-call | flops 1 | bytes 1 | tf_op jit(solution)/shard_map/pallas_call | solution.py:42
  44.5 1.7 %collective-permute-done.21.refs_1_ = bf16[512,512]{1,0:T(8,128)(2,1)S(1)} collective-permute-done((bf16[512,512]{1,0:T(8,128)(2,1)S(1)}, bf16[512,512]{1,0:T(8,128)(2,1)S(1)}, u32[]{:S(2)}, u32[]{:S(2)}) %collective-permute-start.21) | collective-permute-done | bytes 524320 | tf_op jit(solution)/shard_map/ppermute | solution.py:405
  50.2 5.2 %collective-permute-done.22.refs_1_ = bf16[512,128]{1,0:T(8,128)(2,1)S(1)} collective-permute-done((bf16[512,128]{1,0:T(8,128)(2,1)S(1)}, bf16[512,128]{1,0:T(8,128)(2,1)S(1)}, u32[]{:S(2)}, u32[]{:S(2)}) %collective-permute-start.22) | collective-permute-done | bytes 131104 | tf_op jit(solution)/shard_map/ppermute | solution.py:401
  60.9 3.3 %collective-permute-start.31 = (bf16[832,128]{1,0:T(8,128)(2,1)S(1)}, bf16[832,128]{1,0:T(8,128)(2,1)S(1)}, u32[]{:S(2)}, u32[]{:S(2)}) collective-permute-start(bf16[832,128]{1,0:T(8,128)(2,1)S(1)} %get-tuple-element.139), channel_id=1, source_target_pairs={{0,4},{1,5},{2,6},{3,7},{4,0},{5,1},{6,2},{7,3},{8,12},{9,13},{10,... | collective-permute-start | bytes 638984 | tf_op jit(solution)/shard_map/ppermute | solution.py:401
  64.5 3.9 %collective-permute-done.30.refs_1_ = bf16[832,128]{1,0:T(8,128)(2,1)S(1)} collective-permute-done((bf16[832,128]{1,0:T(8,128)(2,1)S(1)}, bf16[832,128]{1,0:T(8,128)(2,1)S(1)}, u32[]{:S(2)}, u32[]{:S(2)}) %collective-permute-start.30) | collective-permute-done | bytes 213024 | tf_op jit(solution)/shard_map/ppermute | solution.py:401
  68.4 5.3 %collective-permute-done.31.refs_2_ = bf16[832,128]{1,0:T(8,128)(2,1)S(1)} collective-permute-done((bf16[832,128]{1,0:T(8,128)(2,1)S(1)}, bf16[832,128]{1,0:T(8,128)(2,1)S(1)}, u32[]{:S(2)}, u32[]{:S(2)}) %collective-permute-start.31) | collective-permute-done | bytes 213024 | tf_op jit(solution)/shard_map/ppermute | solution.py:401
  76.0 3.3 %collective-permute-start.34 = (bf16[400,128]{1,0:T(8,128)(2,1)S(1)}, bf16[400,128]{1,0:T(8,128)(2,1)S(1)}, u32[]{:S(2)}, u32[]{:S(2)}) collective-permute-start(bf16[400,128]{1,0:T(8,128)(2,1)S(1)} %get-tuple-element.150), channel_id=1, source_target_pairs={{0,64},{1,17},{2,66},{3,19},{4,68},{5,21},{6,70},{7,23},{8,72},{9,... | collective-permute-start | bytes 307208 | tf_op jit(solution)/shard_map/ppermute | solution.py:418
  80.8 1.9 %collective-permute-done.34.c = bf16[400,128]{1,0:T(8,128)(2,1)S(1)} collective-permute-done((bf16[400,128]{1,0:T(8,128)(2,1)S(1)}, bf16[400,128]{1,0:T(8,128)(2,1)S(1)}, u32[]{:S(2)}, u32[]{:S(2)}) %collective-permute-start.34) | collective-permute-done | bytes 102432 | tf_op jit(solution)/shard_map/ppermute | solution.py:418
  83.2 2.8 %collective-permute-start.38 = (bf16[400,128]{1,0:T(8,128)(2,1)S(1)}, bf16[400,128]{1,0:T(8,128)(2,1)S(1)}, u32[]{:S(2)}, u32[]{:S(2)}) collective-permute-start(bf16[400,128]{1,0:T(8,128)(2,1)S(1)} %shard_map.183.a), channel_id=1, source_target_pairs={{0,24},{1,97},{2,26},{3,99},{4,28},{5,101},{6,30},{7,103},{8,0},{9... | collective-permute-start | bytes 307208 | tf_op jit(solution)/shard_map/ppermute | solution.py:418
  89.8 1.8 %collective-permute-done.28.r2 = bf16[64,512]{1,0:T(8,128)(2,1)S(1)} collective-permute-done((bf16[64,512]{1,0:T(8,128)(2,1)S(1)}, bf16[64,512]{1,0:T(8,128)(2,1)S(1)}, u32[]{:S(2)}, u32[]{:S(2)}) %collective-permute-start.28) | collective-permute-done | bytes 65568 | tf_op jit(solution)/shard_map/ppermute | solution.py:401
  92.8 2.5 %collective-permute-start.41 = (bf16[400,128]{1,0:T(8,128)(2,1)S(1)}, bf16[400,128]{1,0:T(8,128)(2,1)S(1)}, u32[]{:S(2)}, u32[]{:S(2)}) collective-permute-start(bf16[400,128]{1,0:T(8,128)(2,1)S(1)} %shard_map.185.refs_0_), channel_id=1, source_target_pairs={{0,96},{1,7},{2,98},{3,1},{4,100},{5,3},{6,102},{7,5},{8,104},{9,1... | collective-permute-start | bytes 307208 | tf_op jit(solution)/shard_map/ppermute | solution.py:418
  98.0 2.4 %collective-permute-done.40.refs_2_ = bf16[400,128]{1,0:T(8,128)(2,1)S(1)} collective-permute-done((bf16[400,128]{1,0:T(8,128)(2,1)S(1)}, bf16[400,128]{1,0:T(8,128)(2,1)S(1)}, u32[]{:S(2)}, u32[]{:S(2)}) %collective-permute-start.40) | collective-permute-done | bytes 102432 | tf_op jit(solution)/shard_map/ppermute | solution.py:418
  101.4 2.1 %collective-permute-start.44 = (bf16[1600,128]{1,0:T(8,128)(2,1)S(1)}, bf16[1600,128]{1,0:T(8,128)(2,1)S(1)}, u32[]{:S(2)}, u32[]{:S(2)}) collective-permute-start(bf16[1600,128]{1,0:T(8,128)(2,1)S(1)} %shard_map.186.refs_0_), channel_id=1, source_target_pairs={{0,6},{1,25},{2,0},{3,27},{4,2},{5,29},{6,4},{7,31},{8,14},{9,1},{... | collective-permute-start | bytes 1228808 | tf_op jit(solution)/shard_map/ppermute | solution.py:418
  104.2 5.9 %collective-permute-start.45 = (bf16[1600,128]{1,0:T(8,128)(2,1)S(1)}, bf16[1600,128]{1,0:T(8,128)(2,1)S(1)}, u32[]{:S(2)}, u32[]{:S(2)}) collective-permute-start(bf16[1600,128]{1,0:T(8,128)(2,1)S(1)} %shard_map.186.refs_0_), channel_id=1, source_target_pairs={{0,1},{1,0},{2,3},{3,2},{4,5},{5,4},{6,7},{7,6},{8,9},{9,8},{10,11... | collective-permute-start | bytes 1228808 | tf_op jit(solution)/shard_map/ppermute | solution.py:405
  110.2 2.7 %collective-permute-done.44.refs_3_ = bf16[1600,128]{1,0:T(8,128)(2,1)S(1)} collective-permute-done((bf16[1600,128]{1,0:T(8,128)(2,1)S(1)}, bf16[1600,128]{1,0:T(8,128)(2,1)S(1)}, u32[]{:S(2)}, u32[]{:S(2)}) %collective-permute-start.44) | collective-permute-done | bytes 409632 | tf_op jit(solution)/shard_map/ppermute | solution.py:418
  112.9 6.3 %collective-permute-start.48 = (bf16[1600,128]{1,0:T(8,128)(2,1)S(1)}, bf16[1600,128]{1,0:T(8,128)(2,1)S(1)}, u32[]{:S(2)}, u32[]{:S(2)}) collective-permute-start(bf16[1600,128]{1,0:T(8,128)(2,1)S(1)} %collective-permute-done.44.refs_3_), channel_id=1, source_target_pairs={{0,1},{1,0},{2,3},{3,2},{4,5},{5,4},{6,7},{7,6},{8,9},{9,8},{10,11... | collective-permute-start | bytes 1228808 | tf_op jit(solution)/shard_map/ppermute | solution.py:405
  119.1 3.9 %collective-permute-start.46 = (bf16[1600,128]{1,0:T(8,128)(2,1)S(1)}, bf16[1600,128]{1,0:T(8,128)(2,1)S(1)}, u32[]{:S(2)}, u32[]{:S(2)}) collective-permute-start(bf16[1600,128]{1,0:T(8,128)(2,1)S(1)} %collective-permute-done.42.refs_1_), channel_id=1, source_target_pairs={{0,1},{1,0},{2,3},{3,2},{4,5},{5,4},{6,7},{7,6},{8,9},{9,8},{10,11... | collective-permute-start | bytes 1228808 | tf_op jit(solution)/shard_map/ppermute | solution.py:405
  124.4 3.5 %shard_map.187 = (f32[64,512]{1,0:T(8,128)}, f32[64,512]{1,0:T(8,128)}, f32[2048,512]{1,0:T(8,128)}, f32[8,64,1024]{2,1,0:T(8,128)}) custom-call(bf16[1600,128]{1,0:T(8,128)(2,1)S(1)} %shard_map.186.refs_0_, bf16[1600,128]{1,0:T(8,128)(2,1)S(1)} %collective-permute-done.42.refs_1_, bf16[1600,128]{1,0:T(8,128)(2,1)S(1)} %collective-permute-done.43.refs_2_, ...), custom_call_target="tpu_custom_call" | custom-call | flops 1 | bytes 1 | tf_op jit(solution)/shard_map/pallas_call | solution.py:42
  (100 shorter events, 37.5 us)
Async XLA Ops:
  0.7 12.0 %collective-permute-start.2 = (bf16[64,1024]{1,0:T(8,128)(2,1)}, bf16[64,1024]{1,0:T(8,128)(2,1)S(1)}, u32[]{:S(2)}, u32[]{:S(2)}) collective-permute-start(bf16[64,1024]{1,0:T(8,128)(2,1)} %bitcast.11), channel_id=1, source_target_pairs={{0,6},{1,7},{2,0},{3,1},{4,2},{5,3},{6,4},{7,5},{8,14},{9,15},{10,... | collective-permute-start | bytes 393224 | tf_op jit(solution)/shard_map/ppermute | solution.py:401
  4.0 8.7 %collective-permute-start.1 = (bf16[64,1024]{1,0:T(8,128)(2,1)}, bf16[64,1024]{1,0:T(8,128)(2,1)S(1)}, u32[]{:S(2)}, u32[]{:S(2)}) collective-permute-start(bf16[64,1024]{1,0:T(8,128)(2,1)} %bitcast.12), channel_id=1, source_target_pairs={{0,4},{1,5},{2,6},{3,7},{4,0},{5,1},{6,2},{7,3},{8,12},{9,13},{10,... | collective-permute-start | bytes 393224 | tf_op jit(solution)/shard_map/ppermute | solution.py:401
  4.6 9.2 %collective-permute-start = (bf16[64,1024]{1,0:T(8,128)(2,1)}, bf16[64,1024]{1,0:T(8,128)(2,1)S(1)}, u32[]{:S(2)}, u32[]{:S(2)}) collective-permute-start(bf16[64,1024]{1,0:T(8,128)(2,1)} %bitcast.13), channel_id=1, source_target_pairs={{0,2},{1,3},{2,4},{3,5},{4,6},{5,7},{6,0},{7,1},{8,10},{9,11},{10,... | collective-permute-start | bytes 393224 | tf_op jit(solution)/shard_map/ppermute | solution.py:401
  5.2 10.3 %collective-permute-start.3 = (bf16[64,1024]{1,0:T(8,128)(2,1)}, bf16[64,1024]{1,0:T(8,128)(2,1)S(1)}, u32[]{:S(2)}, u32[]{:S(2)}) collective-permute-start(bf16[64,1024]{1,0:T(8,128)(2,1)} %bitcast.14), channel_id=1, source_target_pairs={{0,1},{1,0},{2,3},{3,2},{4,5},{5,4},{6,7},{7,6},{8,9},{9,8},{10,11... | collective-permute-start | bytes 393224 | tf_op jit(solution)/shard_map/ppermute | solution.py:405
  15.0 8.4 %collective-permute-start.12 = (bf16[64,1024]{1,0:T(8,128)(2,1)S(1)}, bf16[64,1024]{1,0:T(8,128)(2,1)S(1)}, u32[]{:S(2)}, u32[]{:S(2)}) collective-permute-start(bf16[64,1024]{1,0:T(8,128)(2,1)S(1)} %bitcast.19), channel_id=1, source_target_pairs={{0,6},{1,7},{2,0},{3,1},{4,2},{5,3},{6,4},{7,5},{8,14},{9,15},{10,... | collective-permute-start | bytes 393224 | tf_op jit(solution)/shard_map/ppermute | solution.py:401
  15.5 9.6 %collective-permute-start.11 = (bf16[64,1024]{1,0:T(8,128)(2,1)S(1)}, bf16[64,1024]{1,0:T(8,128)(2,1)S(1)}, u32[]{:S(2)}, u32[]{:S(2)}) collective-permute-start(bf16[64,1024]{1,0:T(8,128)(2,1)S(1)} %bitcast.20), channel_id=1, source_target_pairs={{0,4},{1,5},{2,6},{3,7},{4,0},{5,1},{6,2},{7,3},{8,12},{9,13},{10,... | collective-permute-start | bytes 393224 | tf_op jit(solution)/shard_map/ppermute | solution.py:401
  16.7 8.4 %collective-permute-start.10 = (bf16[64,1024]{1,0:T(8,128)(2,1)S(1)}, bf16[64,1024]{1,0:T(8,128)(2,1)S(1)}, u32[]{:S(2)}, u32[]{:S(2)}) collective-permute-start(bf16[64,1024]{1,0:T(8,128)(2,1)S(1)} %bitcast.21), channel_id=1, source_target_pairs={{0,2},{1,3},{2,4},{3,5},{4,6},{5,7},{6,0},{7,1},{8,10},{9,11},{10,... | collective-permute-start | bytes 393224 | tf_op jit(solution)/shard_map/ppermute | solution.py:401
  23.4 8.7 %collective-permute-start.17 = (bf16[64,1024]{1,0:T(8,128)(2,1)S(1)}, bf16[64,1024]{1,0:T(8,128)(2,1)S(1)}, u32[]{:S(2)}, u32[]{:S(2)}) collective-permute-start(bf16[64,1024]{1,0:T(8,128)(2,1)S(1)} %bitcast.22), channel_id=1, source_target_pairs={{0,1},{1,0},{2,3},{3,2},{4,5},{5,4},{6,7},{7,6},{8,9},{9,8},{10,11... | collective-permute-start | bytes 393224 | tf_op jit(solution)/shard_map/ppermute | solution.py:405
  25.0 7.6 %collective-permute-start.13 = (bf16[512,128]{1,0:T(8,128)(2,1)S(1)}, bf16[512,128]{1,0:T(8,128)(2,1)S(1)}, u32[]{:S(2)}, u32[]{:S(2)}) collective-permute-start(bf16[512,128]{1,0:T(8,128)(2,1)S(1)} %get-tuple-element.96.refs_0_), channel_id=1, source_target_pairs={{0,1},{1,0},{2,3},{3,2},{4,5},{5,4},{6,7},{7,6},{8,9},{9,8},{10,11... | collective-permute-start | bytes 393224 | tf_op jit(solution)/shard_map/ppermute | solution.py:405
  25.1 7.6 %collective-permute-start.7 = (bf16[512,128]{1,0:T(8,128)(2,1)S(1)}, bf16[512,128]{1,0:T(8,128)(2,1)S(1)}, u32[]{:S(2)}, u32[]{:S(2)}) collective-permute-start(bf16[512,128]{1,0:T(8,128)(2,1)S(1)} %get-tuple-element.96.refs_0_), channel_id=1, source_target_pairs={{0,2},{1,3},{2,4},{3,5},{4,6},{5,7},{6,0},{7,1},{8,10},{9,11},{10,... | collective-permute-start | bytes 393224 | tf_op jit(solution)/shard_map/ppermute | solution.py:401
  46.4 9.0 %collective-permute-start.22 = (bf16[512,128]{1,0:T(8,128)(2,1)S(1)}, bf16[512,128]{1,0:T(8,128)(2,1)S(1)}, u32[]{:S(2)}, u32[]{:S(2)}) collective-permute-start(bf16[512,128]{1,0:T(8,128)(2,1)S(1)} %get-tuple-element.118), channel_id=1, source_target_pairs={{0,2},{1,3},{2,4},{3,5},{4,6},{5,7},{6,0},{7,1},{8,10},{9,11},{10,... | collective-permute-start | bytes 393224 | tf_op jit(solution)/shard_map/ppermute | solution.py:401
  46.5 8.9 %collective-permute-start.23 = (bf16[512,128]{1,0:T(8,128)(2,1)S(1)}, bf16[512,128]{1,0:T(8,128)(2,1)S(1)}, u32[]{:S(2)}, u32[]{:S(2)}) collective-permute-start(bf16[512,128]{1,0:T(8,128)(2,1)S(1)} %get-tuple-element.119), channel_id=1, source_target_pairs={{0,4},{1,5},{2,6},{3,7},{4,0},{5,1},{6,2},{7,3},{8,12},{9,13},{10,... | collective-permute-start | bytes 393224 | tf_op jit(solution)/shard_map/ppermute | solution.py:401
  47.9 7.9 %collective-permute-start.24 = (bf16[512,128]{1,0:T(8,128)(2,1)S(1)}, bf16[512,128]{1,0:T(8,128)(2,1)S(1)}, u32[]{:S(2)}, u32[]{:S(2)}) collective-permute-start(bf16[512,128]{1,0:T(8,128)(2,1)S(1)} %get-tuple-element.120), channel_id=1, source_target_pairs={{0,6},{1,7},{2,0},{3,1},{4,2},{5,3},{6,4},{7,5},{8,14},{9,15},{10,... | collective-permute-start | bytes 393224 | tf_op jit(solution)/shard_map/ppermute | solution.py:401
  60.7 7.7 %collective-permute-start.30 = (bf16[832,128]{1,0:T(8,128)(2,1)S(1)}, bf16[832,128]{1,0:T(8,128)(2,1)S(1)}, u32[]{:S(2)}, u32[]{:S(2)}) collective-permute-start(bf16[832,128]{1,0:T(8,128)(2,1)S(1)} %get-tuple-element.138), channel_id=1, source_target_pairs={{0,2},{1,3},{2,4},{3,5},{4,6},{5,7},{6,0},{7,1},{8,10},{9,11},{10,... | collective-permute-start | bytes 638984 | tf_op jit(solution)/shard_map/ppermute | solution.py:401
  60.9 12.8 %collective-permute-start.31 = (bf16[832,128]{1,0:T(8,128)(2,1)S(1)}, bf16[832,128]{1,0:T(8,128)(2,1)S(1)}, u32[]{:S(2)}, u32[]{:S(2)}) collective-permute-start(bf16[832,128]{1,0:T(8,128)(2,1)S(1)} %get-tuple-element.139), channel_id=1, source_target_pairs={{0,4},{1,5},{2,6},{3,7},{4,0},{5,1},{6,2},{7,3},{8,12},{9,13},{10,... | collective-permute-start | bytes 638984 | tf_op jit(solution)/shard_map/ppermute | solution.py:401
  64.1 9.6 %collective-permute-start.32 = (bf16[832,128]{1,0:T(8,128)(2,1)S(1)}, bf16[832,128]{1,0:T(8,128)(2,1)S(1)}, u32[]{:S(2)}, u32[]{:S(2)}) collective-permute-start(bf16[832,128]{1,0:T(8,128)(2,1)S(1)} %get-tuple-element.140), channel_id=1, source_target_pairs={{0,6},{1,7},{2,0},{3,1},{4,2},{5,3},{6,4},{7,5},{8,14},{9,15},{10,... | collective-permute-start | bytes 638984 | tf_op jit(solution)/shard_map/ppermute | solution.py:401
  76.0 6.7 %collective-permute-start.34 = (bf16[400,128]{1,0:T(8,128)(2,1)S(1)}, bf16[400,128]{1,0:T(8,128)(2,1)S(1)}, u32[]{:S(2)}, u32[]{:S(2)}) collective-permute-start(bf16[400,128]{1,0:T(8,128)(2,1)S(1)} %get-tuple-element.150), channel_id=1, source_target_pairs={{0,64},{1,17},{2,66},{3,19},{4,68},{5,21},{6,70},{7,23},{8,72},{9,... | collective-permute-start | bytes 307208 | tf_op jit(solution)/shard_map/ppermute | solution.py:418
  80.1 8.2 %collective-permute-start.27 = (bf16[64,512]{1,0:T(8,128)(2,1)S(1)}, bf16[64,512]{1,0:T(8,128)(2,1)S(1)}, u32[]{:S(2)}, u32[]{:S(2)}) collective-permute-start(bf16[64,512]{1,0:T(8,128)(2,1)S(1)} %get-tuple-element.130), channel_id=1, source_target_pairs={{0,2},{1,3},{2,4},{3,5},{4,6},{5,7},{6,0},{7,1},{8,10},{9,11},{10,... | collective-permute-start | bytes 196616 | tf_op jit(solution)/shard_map/ppermute | solution.py:401
  83.2 9.5 %collective-permute-start.38 = (bf16[400,128]{1,0:T(8,128)(2,1)S(1)}, bf16[400,128]{1,0:T(8,128)(2,1)S(1)}, u32[]{:S(2)}, u32[]{:S(2)}) collective-permute-start(bf16[400,128]{1,0:T(8,128)(2,1)S(1)} %shard_map.183.a), channel_id=1, source_target_pairs={{0,24},{1,97},{2,26},{3,99},{4,28},{5,101},{6,30},{7,103},{8,0},{9... | collective-permute-start | bytes 307208 | tf_op jit(solution)/shard_map/ppermute | solution.py:418
  101.4 11.4 %collective-permute-start.44 = (bf16[1600,128]{1,0:T(8,128)(2,1)S(1)}, bf16[1600,128]{1,0:T(8,128)(2,1)S(1)}, u32[]{:S(2)}, u32[]{:S(2)}) collective-permute-start(bf16[1600,128]{1,0:T(8,128)(2,1)S(1)} %shard_map.186.refs_0_), channel_id=1, source_target_pairs={{0,6},{1,25},{2,0},{3,27},{4,2},{5,29},{6,4},{7,31},{8,14},{9,1},{... | collective-permute-start | bytes 1228808 | tf_op jit(solution)/shard_map/ppermute | solution.py:418
  103.6 15.5 %collective-permute-start.43 = (bf16[1600,128]{1,0:T(8,128)(2,1)S(1)}, bf16[1600,128]{1,0:T(8,128)(2,1)S(1)}, u32[]{:S(2)}, u32[]{:S(2)}) collective-permute-start(bf16[1600,128]{1,0:T(8,128)(2,1)S(1)} %shard_map.186.refs_0_), channel_id=1, source_target_pairs={{0,4},{1,17},{2,6},{3,19},{4,0},{5,21},{6,2},{7,23},{8,12},{9,25},... | collective-permute-start | bytes 1228808 | tf_op jit(solution)/shard_map/ppermute | solution.py:418
  103.9 15.3 %collective-permute-start.42 = (bf16[1600,128]{1,0:T(8,128)(2,1)S(1)}, bf16[1600,128]{1,0:T(8,128)(2,1)S(1)}, u32[]{:S(2)}, u32[]{:S(2)}) collective-permute-start(bf16[1600,128]{1,0:T(8,128)(2,1)S(1)} %shard_map.186.refs_0_), channel_id=1, source_target_pairs={{0,2},{1,9},{2,4},{3,11},{4,6},{5,13},{6,0},{7,15},{8,10},{9,17},{... | collective-permute-start | bytes 1228808 | tf_op jit(solution)/shard_map/ppermute | solution.py:418
  104.2 18.8 %collective-permute-start.45 = (bf16[1600,128]{1,0:T(8,128)(2,1)S(1)}, bf16[1600,128]{1,0:T(8,128)(2,1)S(1)}, u32[]{:S(2)}, u32[]{:S(2)}) collective-permute-start(bf16[1600,128]{1,0:T(8,128)(2,1)S(1)} %shard_map.186.refs_0_), channel_id=1, source_target_pairs={{0,1},{1,0},{2,3},{3,2},{4,5},{5,4},{6,7},{7,6},{8,9},{9,8},{10,11... | collective-permute-start | bytes 1228808 | tf_op jit(solution)/shard_map/ppermute | solution.py:405
  112.9 10.2 %collective-permute-start.48 = (bf16[1600,128]{1,0:T(8,128)(2,1)S(1)}, bf16[1600,128]{1,0:T(8,128)(2,1)S(1)}, u32[]{:S(2)}, u32[]{:S(2)}) collective-permute-start(bf16[1600,128]{1,0:T(8,128)(2,1)S(1)} %collective-permute-done.44.refs_3_), channel_id=1, source_target_pairs={{0,1},{1,0},{2,3},{3,2},{4,5},{5,4},{6,7},{7,6},{8,9},{9,8},{10,11... | collective-permute-start | bytes 1228808 | tf_op jit(solution)/shard_map/ppermute | solution.py:405
  (30 other events, 183.3 us)
